TPU v7x, 512 devices: a whole 4x8x8 slice. The times are simulated.
512 devices in a mesh: blk: 32 (over x_lo, z, core), group: 16 (over x_hi, y).
Axes of the slice: x: 4 (x_hi: 2, x_lo: 2; x = x_hi * 2 + x_lo), y: 8, z: 8, core: 2. Of those that a mesh axis runs over, the one named last changes fastest.
Arguments:
- pooled_activations: bfloat16 [16, 4096, 1408], P('group', 'blk'), may hold values from -6 to 6
- caption_encodings: bfloat16 [16, 4096, 1152], P('group', 'blk'), may hold values from -6 to 6
- norm_multiplier: float32 [1408], replicated, may hold values from 0.1 to 1.9
- output_projector: bfloat16 [1408, 1152], replicated, may hold values from -0.15625 to 0.15625
- inverse_softness: float32 [1], replicated, may hold values from 30 to 120
- offset_shift: float32 [1], replicated, may hold values from -7 to -4
Outputs:
- loss: float32 [], replicated
- d_features: bfloat16 [16, 4096, 1408], P('group', 'blk')
- d_gain: float32 [1408], replicated
- head_weight_gradient: float32 [1408, 1152], P('blk')
All inputs are finite; a program needn't handle non-finite values.
Results may differ from a plain program's by a relative error of at most 0.029.
Values may be sent and summed in bfloat16 or wider, within the bound.
No kernel may reach another device: no remote copies, remote signals or barrier semaphores. Data moves between devices by JAX's collectives and lax.ppermute only.
A program may use at most 64 MiB of HBM per device.

v0:
```python
import math

import jax
import jax.numpy as jnp
from jax import lax
from jax.sharding import PartitionSpec as P

EPSILON = 1e-06


def per_device(
    pooled_activations,
    caption_encodings,
    norm_multiplier,
    output_projector,
    inverse_softness,
    offset_shift,
):
    pair_rows = pooled_activations.shape[1]
    emb_width = output_projector.shape[1]
    similarity_multiplier = inverse_softness[0]
    bias_value = offset_shift[0]
    values = pooled_activations[0].astype(jnp.float32)
    row_mean = jnp.mean(values, axis=1, keepdims=True)
    centred = values - row_mean
    scale_inv = lax.rsqrt(jnp.mean(centred * centred, axis=1, keepdims=True) + EPSILON)
    x_hat = centred * scale_inv
    normed = (x_hat * norm_multiplier).astype(jnp.bfloat16)
    proj = jnp.dot(normed, output_projector, preferred_element_type=jnp.float32)
    pnorm = lax.rsqrt(jnp.sum(proj * proj, axis=1, keepdims=True) + EPSILON)
    unit_img = proj * pnorm
    image_vectors = unit_img.astype(jnp.bfloat16)
    text_vals = caption_encodings[0].astype(jnp.float32)
    text_unit = (
        text_vals * lax.rsqrt(jnp.sum(text_vals * text_vals, axis=1, keepdims=True) + EPSILON)
    ).astype(jnp.bfloat16)
    image_index = lax.axis_index("blk") * pair_rows + lax.broadcasted_iota(
        jnp.int32, (pair_rows, 1), 0
    )

    def block_terms(carry, piece, start):
        loss_acc, grad_acc = carry
        sims = lax.dot_general(
            image_vectors, piece, (((1,), (1,)), ((), ())), preferred_element_type=jnp.float32
        )
        pair_logits = similarity_multiplier * sims + bias_value
        text_index = start + lax.broadcasted_iota(jnp.int32, (1, piece.shape[0]), 1)
        sign = jnp.where(image_index == text_index, 1.0, -1.0).astype(jnp.float32)
        loss_acc = loss_acc - jnp.sum(jax.nn.log_sigmoid(sign * pair_logits))
        slope = (-sign * jax.nn.sigmoid(-sign * pair_logits)).astype(jnp.bfloat16)
        grad_acc = grad_acc + jnp.dot(slope, piece, preferred_element_type=jnp.float32)
        return (loss_acc, grad_acc)

    initial = (jnp.zeros((), jnp.float32), jnp.zeros((pair_rows, emb_width), jnp.float32))
    whole = lax.all_gather(text_unit, "blk", axis=0, tiled=True)
    column_span = math.gcd(whole.shape[0], 512)
    block_count = whole.shape[0] // column_span
    blocks = whole.reshape(block_count, column_span, emb_width)
    block_starts = lax.iota(jnp.int32, block_count) * column_span

    def scan_step(carry, operands):
        return (block_terms(carry, operands[1], operands[0]), None)

    folded_result, _ = lax.scan(scan_step, initial, (block_starts, blocks))
    loss_part, grad_sum = folded_result
    image_grad = similarity_multiplier * grad_sum
    inner = jnp.sum(unit_img * image_grad, axis=1, keepdims=True)
    d_proj = ((image_grad - unit_img * inner) * pnorm).astype(jnp.bfloat16)
    d_normed = lax.dot_general(
        d_proj, output_projector, (((1,), (1,)), ((), ())), preferred_element_type=jnp.float32
    )
    gain_part = jnp.sum(x_hat * d_normed, axis=0)
    d_hat = d_normed * norm_multiplier
    d_feat = scale_inv * (
        d_hat
        - jnp.mean(d_hat, axis=1, keepdims=True)
        - x_hat * jnp.mean(d_hat * x_hat, axis=1, keepdims=True)
    )
    d_features = d_feat.astype(jnp.bfloat16)[None]
    partial_value = lax.dot_general(
        normed, d_proj, (((0,), (0,)), ((), ())), preferred_element_type=jnp.float32
    )
    head_share = lax.psum_scatter(
        lax.optimization_barrier(partial_value.astype(jnp.bfloat16))
        .astype(jnp.float32)
        .astype(jnp.bfloat16),
        "blk",
        scatter_dimension=0,
        tiled=True,
    )
    head_weight_gradient = lax.psum(head_share, "group").astype(jnp.float32)
    loss_total, d_gain = lax.psum((loss_part, gain_part), ("blk", "group"))
    loss = loss_total / (pair_rows * lax.axis_size("blk") * lax.axis_size("group"))
    return (loss, d_features, d_gain, head_weight_gradient)


def solution(mesh):
    in_specs = (P("group", "blk", None), P("group", "blk", None), P(), P(), P(), P())
    out_specs = (P(), P("group", "blk", None), P(), P("blk", None))
    return jax.shard_map(
        per_device, mesh=mesh, in_specs=in_specs, out_specs=out_specs, check_vma=False
    )
```

profile of v0, /device:TPU:64, one launch (start us, length us, event | category | flops | bytes accessed | tf_op | source)
XLA Modules:
  0.0 420.7 jit_solution(13463977440582670433)
XLA Ops:
  7.2 1.3 fusion.49
  8.5 1.8 fusion.50
  11.0 1.3 dynamic-slice.4
  13.1 1.1 convert_reduce_fusion
  14.2 1.2 fusion.48
  15.4 1.8 multiply_reduce_fusion.2
  17.3 0.8 copy-done.1
  18.1 0.8 multiply_convert_fusion.1
  18.9 71.7 %all-gather.2.cloned.1.call-done = bf16[4096,1152]{1,0:T(8,128)(2,1)} async-done(((bf16[128,1152]{1,0:T(8,128)(2,1)}), bf16[4096,1152]{1,0:T(8,128)(2,1)}) %all-gather.2.cloned.1.call-update) | async-done | bytes 9437200 | tf_op jit(solution)/shard_map/all_gather | solution.py:55
  90.6 67.7 %while.13 = (s32[]{:T(128)}, f32[]{:T(128)}, f32[128,1152]{1,0:T(8,128)}, s32[8]{0:T(128)S(1)}, f32[]{:T(128)}, /*index=5*/bf16[8,512,1152]{2,1,0:T(8,128)(2,1)}...) while((s32[]{:T(128)}, f32[]{:T(128)}, ...), condition=%wide.region_6.7_spmd.clone, body=%wide.region_4.6_spmd.clone.sunk | while | flops 303727232 | bytes 4367027 | solution.py:64
  91.2 0.6 iota_add_fusion.2
  91.8 3.8 fusion.67
  96.3 2.6 convolution_add_fusion.2
  99.5 0.6 iota_add_fusion.2
  100.1 3.8 fusion.67
  104.6 2.7 convolution_add_fusion.2
  108.0 0.6 iota_add_fusion.2
  108.6 3.8 fusion.67
  113.1 2.7 convolution_add_fusion.2
  116.4 0.6 iota_add_fusion.2
  117.1 3.8 fusion.67
  121.6 2.7 convolution_add_fusion.2
  124.9 0.6 iota_add_fusion.2
  125.6 3.8 fusion.67
  130.1 2.7 convolution_add_fusion.2
  133.4 0.6 iota_add_fusion.2
  134.0 3.8 fusion.67
  138.5 2.7 convolution_add_fusion.2
  142.5 3.8 fusion.67
  147.0 2.7 convolution_add_fusion.2
  151.0 3.8 fusion.67
  155.5 2.7 convolution_add_fusion.2
  158.2 1.4 multiply_reduce_fusion.1
  159.7 1.5 multiply_convert_fusion
  161.2 2.9 fusion.47
  164.1 2.8 convolution_convert_fusion
  166.9 64.4 %fusion.2 = bf16[48,1152]{1,0:T(8,128)(2,1)S(1)} fusion(bf16[1408,1152]{1,0:T(8,128)(2,1)} %convolution_convert_fusion), kind=kCustom, calls=%all-reduce-scatter | all-reduce-scatter fusion | flops 1769473 | bytes 3356672
  231.4 1.9 collective-permute-start.1
  233.3 1.9 collective-permute-start
  235.2 1.7 collective-permute-start.2
  236.9 1.9 collective-permute-done.2
  238.9 2.5 collective-permute-done.1
  241.4 6.0 %concatenate = bf16[172,1152]{1,0:T(8,128)(2,1)} concatenate(bf16[28,1152]{1,0:T(8,128)(2,1)} %copy-done.4, bf16[48,1152]{1,0:T(8,128)(2,1)S(1)} %collective-permute-done.1, bf16[48,1152]{1,0:T(8,128)(2,1)} %collective-permute-done, bf16[48,1152]{1,0:T(8,128)(2,1)S(1)} %fusion.2), dimensions={0} | concatenate | bytes 792576
  247.4 1.6 constant_dynamic-slice_fusion
  249.0 2.2 fusion.51
  251.3 106.4 %all-reduce.2 = (f32[]{:T(128)}, f32[1408]{0:T(1024)}) all-reduce(f32[]{:T(128)} %get-tuple-element.52, f32[1408]{0:T(1024)S(1)} %get-tuple-element.87), channel_id=1, replica_groups=mesh['blk'=32,'group'=16] {'blk','group'}, use_global_device_ids=true, to_apply=%region_7.8 | all-reduce | flops 1409 | bytes 11272 | tf_op jit(solution)/shard_map/psum | solution.py:92
  358.3 52.8 %all-reduce.5.cloned.1.call-done = bf16[44,1152]{1,0:T(8,128)(2,1)} async-done(((bf16[44,1152]{1,0:T(8,128)(2,1)}), bf16[44,1152]{1,0:T(8,128)(2,1)}) %all-reduce.5.cloned.1.call-update) | async-done | bytes 101392 | tf_op jit(solution)/shard_map/psum | solution.py:91
  411.1 1.6 convert_element_type.48
  (40 shorter events, 6.2 us)
Async XLA Ops:
  7.2 8.3 %copy-start = (bf16[1408,1152]{1,0:T(8,128)(2,1)S(1)}, bf16[1408,1152]{1,0:T(8,128)(2,1)}, u32[]{:S(2)}) copy-start(bf16[1408,1152]{1,0:T(8,128)(2,1)} %param.11) | copy-start | bytes 9732100
  7.2 83.4 %all-gather.2.cloned.1.call-start = ((), (), s32[]{:S(2)}) async-start(), calls=%async_computation | async-start | bytes 9732096 | tf_op jit(solution)/shard_map/all_gather | solution.py:55
  10.3 400.8 %all-reduce.5.cloned.1.call-start = ((), (), s32[]{:S(2)}) async-start(), calls=%async_computation.1 | async-start | bytes 221184 | tf_op jit(solution)/shard_map/psum | solution.py:91
  17.2 0.8 copy-start.1
  90.6 70.6 %copy-start.3 = (f32[1408]{0:T(1024)S(1)}, f32[1408]{0:T(1024)}, u32[]{:S(2)}) copy-start(f32[1408]{0:T(1024)} %param.10) | copy-start | bytes 16900
  159.7 4.4 %copy-start.2 = (bf16[1,128,1408]{2,1,0:T(8,128)(2,1)S(1)}, bf16[1,128,1408]{2,1,0:T(8,128)(2,1)}, u32[]{:S(2)}) copy-start(bf16[1,128,1408]{2,1,0:T(8,128)(2,1)} %param.8) | copy-start | bytes 1081348
  231.4 10.0 %collective-permute-start.1 = (bf16[48,1152]{1,0:T(8,128)(2,1)S(1)}, bf16[48,1152]{1,0:T(8,128)(2,1)S(1)}, u32[]{:S(2)}, u32[]{:S(2)}) collective-permute-start(bf16[48,1152]{1,0:T(8,128)(2,1)S(1)} %fusion.2), channel_id=1, source_target_pairs={{0,32},{16,48},{32,64},{48,80},{64,96},{80,112},{96,128},{112,144}... | collective-permute-start | bytes 331784
  233.3 8.0 %collective-permute-start = (bf16[48,1152]{1,0:T(8,128)(2,1)S(1)}, bf16[48,1152]{1,0:T(8,128)(2,1)}, u32[]{:S(2)}, u32[]{:S(2)}) collective-permute-start(bf16[48,1152]{1,0:T(8,128)(2,1)S(1)} %fusion.2), channel_id=1, source_target_pairs={{0,16},{16,32},{32,48},{48,64},{64,80},{80,96},{96,112},{112,128},... | collective-permute-start | bytes 331784
  235.2 3.6 collective-permute-start.2
  238.9 2.5 copy-start.4
Sparse Core Ops, SparseCore 0:
  10.7 79.7 all-gather.1
  249.1 161.9 all-reduce.4
where the time goes:
time: 422 us; the launch traced here: 421 us
  blocking collectives  171 us (41%)
  waiting for transfers between devices  129 us (31%)
  matrix products  60 us (14%)
  other arithmetic  18.2 us (4%)
  between operations  17.3 us (4%)
  local copies, waits for them, and re-layouts  14.5 us (3%)
  starting transfers between devices  5.58 us (1%)
  loops' own time  5.36 us (1%)
    psum x1, blocking collectives, per_device(): loss_total, d_gain = lax.psum((loss_part, gain_part), ('blk', 'group'))  106 us
    all_gather x1, waiting for transfers between devices, per_device(): whole = lax.all_gather(text_unit, 'blk', axis=0, tiled=True)  71.7 us
    unnamed x1, blocking collectives  64.4 us
    psum x1, waiting for transfers between devices, per_device(): head_weight_gradient = lax.psum(head_share, 'group').astype(jnp.float32)  52.8 us
    dot_general x8, matrix products, block_terms(): lax.dot_general(image_vectors, piece, (((1,), (1,)), ((), ())), preferred...  30.7 us
    dot_general x8, matrix products, block_terms(): jnp.dot(slope, piece, preferred_element_type=jnp.float32)  21.7 us
    unnamed x14, local copies, waits for them, and re-layouts  9.8 us
  transfers between devices with their start and end apart: 5, of which 4 were waited for; matrix products, arithmetic and copies ran while one was open for 2% of the time, Pallas kernels for 0%

commit v1 on v0

v1 whole, which is shorter than its diff:
```python
import functools

import jax
import jax.numpy as jnp
from jax import lax
from jax.experimental import pallas as pl
from jax.experimental.pallas import tpu as pltpu
from jax.sharding import Mesh, PartitionSpec as P

EPSILON = 1e-06
ROWS = 128
W = 1408
E = 1152
SHARE = 44
F32 = jnp.float32
BF16 = jnp.bfloat16

X, Z, C, HX, Y = "x", "z", "c", "hx", "y"
NZ = 8
N_GROUP = 16
PIECE = 512
BLOCK = 128
EXTRA = 16
GAIN_AT = 112

SWAP = [(0, 1), (1, 0)]
HOP = [
    (z * 2 + c, ((z + (1 if c == 0 else -1)) % NZ) * 2 + c) for z in range(NZ) for c in range(2)
]

VMEM = pl.BlockSpec(memory_space=pltpu.VMEM)
SMEM = pl.BlockSpec(memory_space=pltpu.SMEM)


def call(kernel, out_shape, *operands, specs=None, scratch=(), flops=0, name=None):
    leaves = jax.tree.leaves(out_shape)
    moved = sum(o.size * o.dtype.itemsize for o in (*operands, *leaves))
    return pl.pallas_call(
        kernel,
        out_shape=out_shape,
        in_specs=specs or [VMEM] * len(operands),
        out_specs=jax.tree.map(lambda _: VMEM, out_shape),
        scratch_shapes=list(scratch),
        name=name,
        cost_estimate=pl.CostEstimate(flops=flops, bytes_accessed=moved, transcendentals=0),
        compiler_params=pltpu.CompilerParams(vmem_limit_bytes=48 << 20),
    )(*operands)


def out(shape, dtype):
    return jax.ShapeDtypeStruct(shape, dtype)


def text_kernel(cap_ref, unit_ref):
    values = cap_ref[...].astype(F32)
    scale = lax.rsqrt(jnp.sum(values * values, axis=1, keepdims=True) + EPSILON)
    unit_ref[...] = (values * scale).astype(BF16)


def moments(values):
    mean = jnp.mean(values, axis=1, keepdims=True)
    centred = values - mean
    scale = lax.rsqrt(jnp.mean(centred * centred, axis=1, keepdims=True) + EPSILON)
    return centred * scale, scale


def norm_kernel(x_ref, gain_ref, normed_ref):
    x_hat, _ = moments(x_ref[...].astype(F32))
    normed_ref[...] = (x_hat * gain_ref[...]).astype(BF16)


def project_kernel(where_ref, n0, n1, n2, n3, w_ref, img_ref, unit_ref, pnorm_ref, pick_ref):
    for i, n in enumerate((n0, n2, n1, n3)):
        rows = pl.ds(i * ROWS, ROWS)
        proj = jnp.dot(n[...], w_ref[...], preferred_element_type=F32)
        pnorm = lax.rsqrt(jnp.sum(proj * proj, axis=1, keepdims=True) + EPSILON)
        unit = proj * pnorm
        img_ref[rows, :] = unit.astype(BF16)
        if i < 2:
            unit_ref[rows, :] = unit
            pnorm_ref[rows, :] = jnp.broadcast_to(pnorm, (ROWS, 128))
    row = lax.broadcasted_iota(jnp.int32, (NZ * 48, 1), 0)
    block = row // 48
    inside = row - block * 48
    source = jnp.where(inside < SHARE, SHARE * (where_ref[0] + 2 * block) + inside, -1)
    column = lax.broadcasted_iota(jnp.int32, (NZ * 48, W), 1)
    select = (column == source).astype(F32).astype(BF16)
    for i, n in enumerate((n0, n2, n1, n3)):
        picked = lax.dot_general(
            select, n[...], (((1,), (1,)), ((), ())), preferred_element_type=F32
        )
        pick_ref[:, pl.ds(i * ROWS, ROWS)] = picked.astype(BF16)


def fold_product(grown):
    rows = grown.shape[0]
    while rows > 8:
        rows //= 2
        one, two = grown[:rows], grown[rows:]
        grown = one + two + one * two
    return grown


def fold_sum(values):
    rows = values.shape[0]
    while rows > 8:
        rows //= 2
        values = values[:rows] + values[rows:]
    return values


def log1p(value):
    up = 1.0 + value
    gap = up - 1.0
    return jnp.where(gap == 0.0, value, jnp.log(up) * (value / jnp.where(gap == 0.0, 1.0, gap)))


def pairs_kernel(sc_ref, img_ref, *refs):
    texts, (keep_ref, send_ref, loss_ref, text, slope) = refs[:8], refs[8:]
    for i, piece in enumerate(texts):
        text[pl.ds(i * ROWS, ROWS), :] = piece[...]
    scale, bias = sc_ref[0], sc_ref[1]
    total = jnp.zeros((8, 128), F32)
    span = 256
    for j in range(8 * ROWS // span):
        sims = lax.dot_general(
            img_ref[...],
            text[pl.ds(j * span, span), :],
            (((1,), (1,)), ((), ())),
            preferred_element_type=F32,
        )
        for half in range(span // ROWS):
            chunk = j * (span // ROWS) + half
            turned = scale * sims[:, half * ROWS : (half + 1) * ROWS] + bias
            if chunk == 0:
                shape = (4 * ROWS, ROWS)
                match = lax.broadcasted_iota(jnp.int32, shape, 0) == lax.broadcasted_iota(
                    jnp.int32, shape, 1
                )
                turned = jnp.where(match, -turned, turned)
            small = jnp.exp(-jnp.abs(turned))
            below = 1.0 + small
            inverse = pl.reciprocal(below, approx=True)
            inverse = inverse * (2.0 - below * inverse)
            sig = jnp.where(turned >= 0.0, 1.0, small) * inverse
            if chunk == 0:
                sig = jnp.where(match, -sig, sig)
            slope[:, chunk * ROWS : (chunk + 1) * ROWS] = sig.astype(BF16)
            total = total + fold_sum(jnp.maximum(turned, 0.0)) + log1p(fold_product(small))
    loss = jnp.broadcast_to(jnp.sum(total, keepdims=True), (1, 128))
    loss_ref[...] = loss
    send_ref[2 * ROWS :, :] = loss_rows(loss)
    grad = jnp.dot(slope[...], text[...], preferred_element_type=F32)
    keep_ref[...] = grad[: 2 * ROWS]
    send_ref[: 2 * ROWS, :] = grad[2 * ROWS :].astype(BF16)


def loss_rows(loss):
    high = loss.astype(BF16).astype(F32)
    row = jnp.concatenate([high, loss - high, jnp.zeros((1, E - 256), F32)], axis=1)
    return jnp.broadcast_to(row, (EXTRA, E)).astype(BF16)


def got_loss(got_ref):
    row = got_ref[2 * ROWS :, :256].astype(F32)[:1]
    return row[:, :128] + row[:, 128:]


def add_kernel(keep_ref, loss_ref, got_ref, sum_ref, loss_out, send_ref):
    total = keep_ref[...] + got_ref[: 2 * ROWS, :].astype(F32)
    sum_ref[...] = total
    send_ref[: 2 * ROWS, :] = total.astype(BF16)
    loss = loss_ref[...] + got_loss(got_ref)
    loss_out[...] = loss
    send_ref[2 * ROWS :, :] = loss_rows(loss)


def dproj_kernel(sc_ref, sum_ref, loss_ref, got_ref, unit_ref, pnorm_ref, dproj_ref, loss_out):
    loss_out[...] = loss_ref[...] + got_loss(got_ref)
    for i in range(2):
        rows, other = pl.ds(i * ROWS, ROWS), pl.ds((1 - i) * ROWS, ROWS)
        grad = sc_ref[0] * (sum_ref[rows, :] + got_ref[other, :].astype(F32))
        unit = unit_ref[rows, :]
        inner = jnp.sum(unit * grad, axis=1, keepdims=True)
        dproj_ref[rows, :] = ((grad - unit * inner) * pnorm_ref[rows, 0:1]).astype(BF16)


def back(dproj, w_ref):
    return lax.dot_general(dproj, w_ref[...], (((1,), (1,)), ((), ())), preferred_element_type=F32)


def features_kernel(dproj_ref, x_ref, gain_ref, n0, n2, w_ref, feat_ref, part_ref):
    d_normed = back(dproj_ref[...], w_ref)
    own = d_normed[:ROWS]
    part_ref[...] = jnp.sum(n0[...].astype(F32) * own, axis=0, keepdims=True) + jnp.sum(
        n2[...].astype(F32) * d_normed[ROWS:], axis=0, keepdims=True
    )
    x_hat, scale = moments(x_ref[...].astype(F32))
    d_hat = own * gain_ref[...]
    feat = scale * (
        d_hat
        - jnp.mean(d_hat, axis=1, keepdims=True)
        - x_hat * jnp.mean(d_hat * x_hat, axis=1, keepdims=True)
    )
    feat_ref[...] = feat.astype(BF16)


def head_kernel(own_ref, got_ref, pick_ref, n1, n3, w_ref, gain_ref, part_ref, loss_ref, out_ref):
    head = jnp.dot(pick_ref[:, : 2 * ROWS], own_ref[...], preferred_element_type=F32) + jnp.dot(
        pick_ref[:, 2 * ROWS :], got_ref[...], preferred_element_type=F32
    )
    head = head.astype(BF16)
    d_normed = back(got_ref[...], w_ref)
    gain = part_ref[...] + jnp.sum(n1[...].astype(F32) * d_normed[:ROWS], axis=0, keepdims=True)
    gain = gain + jnp.sum(n3[...].astype(F32) * d_normed[ROWS:], axis=0, keepdims=True)
    gain = gain / gain_ref[...]
    loss = loss_ref[...]
    rows = [gain[:, :512], gain[:, 512:1024], jnp.concatenate([gain[:, 1024:], loss], axis=1)]
    high = [r.astype(BF16).astype(F32) for r in rows]
    low = [r - h for r, h in zip(rows, high)]
    index = lax.broadcasted_iota(jnp.int32, (16, PIECE), 0)
    packed = jnp.zeros((16, PIECE), F32)
    for i, r in enumerate(high + low):
        packed = jnp.where(index == i, r, packed)
    packed = packed.astype(BF16)
    for k in range(NZ):
        block = head[48 * k : 48 * (k + 1)]
        at = BLOCK * k
        out_ref[at : at + 48, :] = block[:, :512]
        out_ref[at + 48 : at + 96, :] = block[:, 512:1024]
        for i in range(3):
            out_ref[at + 96 : at + 112, 128 * i : 128 * (i + 1)] = block[16 * i : 16 * (i + 1), 1024:]
        out_ref[at + 96 : at + 112, 384:] = jnp.zeros((16, 128), BF16)
        out_ref[at + GAIN_AT : at + BLOCK, :] = packed


def reduce_kernel(where_ref, got_ref, out_ref):
    total = got_ref[...].astype(F32).reshape(N_GROUP * NZ, 8, PIECE).sum(axis=0)
    rest = jnp.concatenate([total[3:], total[:3]], axis=0)
    index = lax.broadcasted_iota(jnp.int32, (8, PIECE), 0)
    whole = total + rest
    high = whole.astype(BF16).astype(F32)
    low = whole - high
    moved = jnp.concatenate([low[5:], low[:5]], axis=0)
    split = jnp.where(index < 3, high, jnp.where(index < 6, moved, 0.0))
    piece = jnp.where(where_ref[1] == GAIN_AT // 8, split, total)
    copies = jnp.broadcast_to(piece[None], (N_GROUP, 8, PIECE)).reshape(BLOCK, PIECE)
    out_ref[...] = copies.astype(BF16)


def unpack_kernel(got_ref, head_ref, gain_ref, loss_ref):
    block = got_ref[...].astype(F32)
    head_ref[:, :512] = block[:SHARE]
    head_ref[:, 512:1024] = block[48 : 48 + SHARE]
    tail = block[96:112]
    head_ref[0:16, 1024:] = tail[:, 0:128]
    head_ref[16:32, 1024:] = tail[:, 128:256]
    head_ref[32:SHARE, 1024:] = tail[: SHARE - 32, 256:384]
    rows = block[GAIN_AT : GAIN_AT + 3] + block[GAIN_AT + 3 : GAIN_AT + 6]
    gain_ref[:, :512] = rows[0:1]
    gain_ref[:, 512:1024] = rows[1:2]
    gain_ref[:, 1024:] = rows[2:3, :384]
    loss_ref[...] = rows[2:3, 384:] * (1.0 / (N_GROUP * NZ * 4 * ROWS))


def per_device(pooled, captions, gain, w, scale, bias):
    x = pooled[0]
    gain = gain.reshape(1, W)
    scalars = jnp.concatenate([scale, bias])
    where = jnp.stack(
        [
            lax.axis_index(X) * 16 + lax.axis_index(C),
            lax.axis_index(HX) * 8 + lax.axis_index(Y),
        ]
    ).astype(jnp.int32)

    across = functools.partial(lax.ppermute, axis_name=X, perm=SWAP)
    between = functools.partial(lax.ppermute, axis_name=C, perm=SWAP)
    hop = functools.partial(lax.ppermute, axis_name=(Z, C), perm=HOP)

    text = call(text_kernel, out((ROWS, E), BF16), captions[0], name="text_unit")
    texts = [text]
    one, two = text, between(text)
    for step in range(4):
        one = hop(one)
        texts.append(one)
        if step < 3:
            two = hop(two)
            texts.append(two)

    n0 = call(norm_kernel, out((ROWS, W), BF16), x, gain, name="normed")
    n2 = across(n0)
    n1 = between(n0)
    n3 = between(n2)
    img, unit, pnorm, pick = call(
        project_kernel,
        (
            out((4 * ROWS, E), BF16),
            out((2 * ROWS, E), F32),
            out((2 * ROWS, 128), F32),
            out((NZ * 48, 4 * ROWS), BF16),
        ),
        where,
        n0,
        n1,
        n2,
        n3,
        w,
        specs=[SMEM] + [VMEM] * 5,
        flops=2 * 4 * ROWS * W * (E + NZ * 48),
        name="project",
    )
    keep, send, loss = call(
        pairs_kernel,
        (out((2 * ROWS, E), F32), out((2 * ROWS + EXTRA, E), BF16), out((1, 128), F32)),
        scalars,
        img,
        *texts,
        specs=[SMEM] + [VMEM] * 9,
        scratch=[pltpu.VMEM((8 * ROWS, E), BF16), pltpu.VMEM((4 * ROWS, 8 * ROWS), BF16)],
        flops=4 * 4 * ROWS * 8 * ROWS * E,
        name="pairs",
    )
    total, loss, send = call(
        add_kernel,
        (out((2 * ROWS, E), F32), out((1, 128), F32), out((2 * ROWS + EXTRA, E), BF16)),
        keep,
        loss,
        between(send),
        name="add_cores",
    )
    dproj, loss = call(
        dproj_kernel,
        (out((2 * ROWS, E), BF16), out((1, 128), F32)),
        scalars,
        total,
        loss,
        across(send),
        unit,
        pnorm,
        specs=[SMEM] + [VMEM] * 5,
        name="d_proj",
    )
    dproj_far = between(dproj)
    d_features, gain_part = call(
        features_kernel,
        (out((ROWS, W), BF16), out((1, W), F32)),
        dproj,
        x,
        gain,
        n0,
        n2,
        w,
        flops=4 * ROWS * W * E,
        name="d_features",
    )
    packed = call(
        head_kernel,
        out((NZ * BLOCK, PIECE), BF16),
        dproj,
        dproj_far,
        pick,
        n1,
        n3,
        w,
        gain,
        gain_part,
        loss,
        flops=4 * ROWS * W * E + 8 * ROWS * NZ * 48 * E,
        name="head",
    )
    packed = lax.all_to_all(packed, (Z, HX, Y), 0, 0, tiled=True)
    piece = call(
        reduce_kernel,
        out((BLOCK, PIECE), BF16),
        where,
        packed,
        specs=[SMEM, VMEM],
        name="reduce",
    )
    block = lax.all_to_all(piece, (HX, Y), 0, 0, tiled=True)
    head, d_gain, loss = call(
        unpack_kernel,
        (out((SHARE, E), F32), out((1, W), F32), out((1, 128), F32)),
        block,
        name="unpack",
    )
    return loss[0, 0], d_features[None], d_gain.reshape(W), head


def solution(mesh):
    fine = Mesh(mesh.devices.reshape(2, NZ, 2, 2, 8), (X, Z, C, HX, Y))
    rows = P((HX, Y), (X, Z, C), None)
    return jax.shard_map(
        per_device,
        mesh=fine,
        in_specs=(rows, rows, P(), P(), P(), P()),
        out_specs=(P(), rows, P(), P((X, Z, C), None)),
        check_vma=False,
    )
```

time: 422 us -> 152 us (0.36)
  the two profiles are of different devices: /device:TPU:64 before, /device:TPU:8 now
where the time goes in v1:
time: 152 us; the launch traced here: 151 us
  blocking collectives  60.9 us (40%)
  starting transfers between devices  40 us (26%)
  waiting for transfers between devices  25.6 us (17%)
  Pallas kernels  18.8 us (12%)
  local copies, waits for them, and re-layouts  2.65 us (2%)
  between operations  2.15 us (1%)
    all_to_all x1, blocking collectives, per_device(): packed = lax.all_to_all(packed, (Z, HX, Y), 0, 0, tiled=True)  46 us
    pallas_call x10, Pallas kernels, call(): pl.pallas_call(kernel, out_shape=out_shape, in_specs=specs or [VMEM] * le...  18.8 us
    ppermute x1, waiting for transfers between devices, per_device(): across(send)  15.6 us
    all_to_all x1, blocking collectives, per_device(): block = lax.all_to_all(piece, (HX, Y), 0, 0, tiled=True)  14.9 us
    ppermute x4, starting transfers between devices, per_device(): one = hop(one)  13.4 us
    ppermute x3, starting transfers between devices, per_device(): two = hop(two)  8.74 us
    ppermute x3, waiting for transfers between devices, per_device(): two = hop(two)  4.7 us
    ppermute x1, starting transfers between devices, per_device(): n1 = between(n0)  4.17 us
  transfers between devices with their start and end apart: 14, of which 6 were waited for; matrix products, arithmetic and copies ran while one was open for 1% of the time, Pallas kernels for 5%

profile of v1, /device:TPU:8, one launch (start us, length us, event | category | flops | bytes accessed | tf_op | source)
XLA Modules:
  0.0 150.8 jit_solution(7277292876928636608)
XLA Ops:
  0.6 0.0 copy-start.3
  0.6 1.0 copy-done.3
  1.6 0.1 text_unit.1.refs_0_
  1.7 1.9 %collective-permute-start.4 = (bf16[128,1152]{1,0:T(8,128)(2,1)S(1)}, bf16[128,1152]{1,0:T(8,128)(2,1)S(1)}, u32[]{:S(2)}, u32[]{:S(2)}) collective-permute-start(bf16[128,1152]{1,0:T(8,128)(2,1)S(1)} %text_unit.1.refs_0_), channel_id=1, source_target_pairs={{0,16},{16,0},{1,17},{17,1},{2,18},{18,2},{3,19},{19,3},{4,20},{20... | collective-permute-start | bytes 884744 | tf_op jit(solution)/shard_map/ppermute | solution.py:283
  3.7 4.3 %collective-permute-start.3 = (bf16[128,1152]{1,0:T(8,128)(2,1)S(1)}, bf16[128,1152]{1,0:T(8,128)(2,1)S(1)}, u32[]{:S(2)}, u32[]{:S(2)}) collective-permute-start(bf16[128,1152]{1,0:T(8,128)(2,1)S(1)} %text_unit.1.refs_0_), channel_id=1, source_target_pairs={{0,32},{16,240},{32,64},{48,16},{64,96},{80,48},{96,128},{112,80},... | collective-permute-start | bytes 884744 | tf_op jit(solution)/shard_map/ppermute | solution.py:285
  8.0 0.7 reshape.18.gain_ref
  8.7 1.0 copy-done.1
  9.6 0.3 normed.1.n0
  9.9 3.4 %collective-permute-start.1 = (bf16[128,1408]{1,0:T(8,128)(2,1)S(1)}, bf16[128,1408]{1,0:T(8,128)(2,1)S(1)}, u32[]{:S(2)}, u32[]{:S(2)}) collective-permute-start(bf16[128,1408]{1,0:T(8,128)(2,1)S(1)} %normed.1.n0), channel_id=1, source_target_pairs={{0,256},{256,0},{1,257},{257,1},{2,258},{258,2},{3,259},{259,3},{4... | collective-permute-start | bytes 1081352 | tf_op jit(solution)/shard_map/ppermute | solution.py:292
  13.3 0.0 collective-permute-done.4
  13.4 4.3 %collective-permute-start.5 = (bf16[128,1152]{1,0:T(8,128)(2,1)S(1)}, bf16[128,1152]{1,0:T(8,128)(2,1)S(1)}, u32[]{:S(2)}, u32[]{:S(2)}) collective-permute-start(bf16[128,1152]{1,0:T(8,128)(2,1)S(1)} %collective-permute-done.4), channel_id=1, source_target_pairs={{0,32},{16,240},{32,64},{48,16},{64,96},{80,48},{96,128},{112,80},... | collective-permute-start | bytes 884744 | tf_op jit(solution)/shard_map/ppermute | solution.py:288
  17.6 1.7 %collective-permute-done.3.refs_1_ = bf16[128,1152]{1,0:T(8,128)(2,1)S(1)} collective-permute-done((bf16[128,1152]{1,0:T(8,128)(2,1)S(1)}, bf16[128,1152]{1,0:T(8,128)(2,1)S(1)}, u32[]{:S(2)}, u32[]{:S(2)}) %collective-permute-start.3) | collective-permute-done | bytes 294944 | tf_op jit(solution)/shard_map/ppermute | solution.py:285
  19.3 2.6 %collective-permute-start.6 = (bf16[128,1152]{1,0:T(8,128)(2,1)S(1)}, bf16[128,1152]{1,0:T(8,128)(2,1)S(1)}, u32[]{:S(2)}, u32[]{:S(2)}) collective-permute-start(bf16[128,1152]{1,0:T(8,128)(2,1)S(1)} %collective-permute-done.3.refs_1_), channel_id=1, source_target_pairs={{0,32},{16,240},{32,64},{48,16},{64,96},{80,48},{96,128},{112,80},... | collective-permute-start | bytes 884744 | tf_op jit(solution)/shard_map/ppermute | solution.py:285
  21.9 4.7 %collective-permute-done.5.refs_2_ = bf16[128,1152]{1,0:T(8,128)(2,1)S(1)} collective-permute-done((bf16[128,1152]{1,0:T(8,128)(2,1)S(1)}, bf16[128,1152]{1,0:T(8,128)(2,1)S(1)}, u32[]{:S(2)}, u32[]{:S(2)}) %collective-permute-start.5) | collective-permute-done | bytes 294944 | tf_op jit(solution)/shard_map/ppermute | solution.py:288
  26.6 1.9 %collective-permute-start.7 = (bf16[128,1152]{1,0:T(8,128)(2,1)S(1)}, bf16[128,1152]{1,0:T(8,128)(2,1)S(1)}, u32[]{:S(2)}, u32[]{:S(2)}) collective-permute-start(bf16[128,1152]{1,0:T(8,128)(2,1)S(1)} %collective-permute-done.5.refs_2_), channel_id=1, source_target_pairs={{0,32},{16,240},{32,64},{48,16},{64,96},{80,48},{96,128},{112,80},... | collective-permute-start | bytes 884744 | tf_op jit(solution)/shard_map/ppermute | solution.py:288
  28.6 1.2 collective-permute-done.6.refs_3_
  29.8 1.9 %collective-permute-start.8 = (bf16[128,1152]{1,0:T(8,128)(2,1)S(1)}, bf16[128,1152]{1,0:T(8,128)(2,1)S(1)}, u32[]{:S(2)}, u32[]{:S(2)}) collective-permute-start(bf16[128,1152]{1,0:T(8,128)(2,1)S(1)} %collective-permute-done.6.refs_3_), channel_id=1, source_target_pairs={{0,32},{16,240},{32,64},{48,16},{64,96},{80,48},{96,128},{112,80},... | collective-permute-start | bytes 884744 | tf_op jit(solution)/shard_map/ppermute | solution.py:285
  31.7 4.2 %collective-permute-start = (bf16[128,1408]{1,0:T(8,128)(2,1)S(1)}, bf16[128,1408]{1,0:T(8,128)(2,1)S(1)}, u32[]{:S(2)}, u32[]{:S(2)}) collective-permute-start(bf16[128,1408]{1,0:T(8,128)(2,1)S(1)} %normed.1.n0), channel_id=1, source_target_pairs={{0,16},{16,0},{1,17},{17,1},{2,18},{18,2},{3,19},{19,3},{4,20},{20... | collective-permute-start | bytes 1081352 | tf_op jit(solution)/shard_map/ppermute | solution.py:293
  35.9 0.0 collective-permute-done.1.n2
  35.9 1.9 %collective-permute-start.2 = (bf16[128,1408]{1,0:T(8,128)(2,1)S(1)}, bf16[128,1408]{1,0:T(8,128)(2,1)S(1)}, u32[]{:S(2)}, u32[]{:S(2)}) collective-permute-start(bf16[128,1408]{1,0:T(8,128)(2,1)S(1)} %collective-permute-done.1.n2), channel_id=1, source_target_pairs={{0,16},{16,0},{1,17},{17,1},{2,18},{18,2},{3,19},{19,3},{4,20},{20... | collective-permute-start | bytes 1081352 | tf_op jit(solution)/shard_map/ppermute | solution.py:294
  39.1 0.1 pad_maximum_fusion.sc_ref
  39.2 0.0 collective-permute-done.7.refs_4_
  39.2 2.6 %collective-permute-start.9 = (bf16[128,1152]{1,0:T(8,128)(2,1)S(1)}, bf16[128,1152]{1,0:T(8,128)(2,1)S(1)}, u32[]{:S(2)}, u32[]{:S(2)}) collective-permute-start(bf16[128,1152]{1,0:T(8,128)(2,1)S(1)} %collective-permute-done.7.refs_4_), channel_id=1, source_target_pairs={{0,32},{16,240},{32,64},{48,16},{64,96},{80,48},{96,128},{112,80},... | collective-permute-start | bytes 884744 | tf_op jit(solution)/shard_map/ppermute | solution.py:288
  41.8 0.0 collective-permute-done.8.refs_5_
  41.8 4.6 %collective-permute-start.10 = (bf16[128,1152]{1,0:T(8,128)(2,1)S(1)}, bf16[128,1152]{1,0:T(8,128)(2,1)S(1)}, u32[]{:S(2)}, u32[]{:S(2)}) collective-permute-start(bf16[128,1152]{1,0:T(8,128)(2,1)S(1)} %collective-permute-done.8.refs_5_), channel_id=1, source_target_pairs={{0,32},{16,240},{32,64},{48,16},{64,96},{80,48},{96,128},{112,80},... | collective-permute-start | bytes 884744 | tf_op jit(solution)/shard_map/ppermute | solution.py:285
  46.4 0.1 pad_add_fusion.where_ref
  46.5 0.0 collective-permute-done.n1
  46.5 0.0 collective-permute-done.2.n3
  46.5 5.4 %project.1 = (bf16[512,1152]{1,0:T(8,128)(2,1)S(1)}, f32[256,1152]{1,0:T(8,128)S(1)}, f32[256,128]{1,0:T(8,128)S(1)}, bf16[384,512]{1,0:T(8,128)(2,1)S(1)}) custom-call(s32[2]{0:T(128)S(1)} %pad_add_fusion.where_ref, bf16[128,1408]{1,0:T(8,128)(2,1)S(1)} %normed.1.n0, bf16[128,1408]{1,0:T(8,128)(2,1)S(1)} %collective-permute-done.n1, ...), custom_call_target="tpu_custom_call" | custom-call | flops 2214592512 | bytes 7569416 | tf_op jit(solution)/shard_map/project/pallas_call | solution.py:38
  51.9 0.0 collective-permute-done.9.refs_6_
  51.9 0.3 collective-permute-done.10.refs_7_
  52.2 4.5 %pairs.1 = (f32[256,1152]{1,0:T(8,128)S(1)}, bf16[272,1152]{1,0:T(8,128)(2,1)S(1)}, f32[1,128]{1,0:T(1,128)S(1)}) custom-call(f32[2]{0:T(128)S(1)} %pad_maximum_fusion.sc_ref, bf16[512,1152]{1,0:T(8,128)(2,1)S(1)} %get-tuple-element.21.img_ref, bf16[128,1152]{1,0:T(8,128)(2,1)S(1)} %text_unit.1.refs_0_, ...), custom_call_target="tpu_custom_call" | custom-call | flops 2415919104 | bytes 5345800 | tf_op jit(solution)/shard_map/pairs/pallas_call | solution.py:38
  56.7 1.9 %collective-permute-start.11 = (bf16[272,1152]{1,0:T(8,128)(2,1)S(1)}, bf16[272,1152]{1,0:T(8,128)(2,1)S(1)}, u32[]{:S(2)}, u32[]{:S(2)}) collective-permute-start(bf16[272,1152]{1,0:T(8,128)(2,1)S(1)} %get-tuple-element.24), channel_id=1, source_target_pairs={{0,16},{16,0},{1,17},{17,1},{2,18},{18,2},{3,19},{19,3},{4,20},{20... | collective-permute-start | bytes 1880072 | tf_op jit(solution)/shard_map/ppermute | solution.py:329
  58.7 2.0 %collective-permute-done.11.got_ref = bf16[272,1152]{1,0:T(8,128)(2,1)S(1)} collective-permute-done((bf16[272,1152]{1,0:T(8,128)(2,1)S(1)}, bf16[272,1152]{1,0:T(8,128)(2,1)S(1)}, u32[]{:S(2)}, u32[]{:S(2)}) %collective-permute-start.11) | collective-permute-done | bytes 626720 | tf_op jit(solution)/shard_map/ppermute | solution.py:329
  60.7 0.2 add_cores.1
  60.9 2.6 %collective-permute-start.12 = (bf16[272,1152]{1,0:T(8,128)(2,1)S(1)}, bf16[272,1152]{1,0:T(8,128)(2,1)S(1)}, u32[]{:S(2)}, u32[]{:S(2)}) collective-permute-start(bf16[272,1152]{1,0:T(8,128)(2,1)S(1)} %get-tuple-element.27), channel_id=1, source_target_pairs={{0,256},{256,0},{1,257},{257,1},{2,258},{258,2},{3,259},{259,3},{4... | collective-permute-start | bytes 1880072 | tf_op jit(solution)/shard_map/ppermute | solution.py:338
  63.5 15.6 %collective-permute-done.12.got_ref = bf16[272,1152]{1,0:T(8,128)(2,1)S(1)} collective-permute-done((bf16[272,1152]{1,0:T(8,128)(2,1)S(1)}, bf16[272,1152]{1,0:T(8,128)(2,1)S(1)}, u32[]{:S(2)}, u32[]{:S(2)}) %collective-permute-start.12) | collective-permute-done | bytes 626720 | tf_op jit(solution)/shard_map/ppermute | solution.py:338
  79.1 1.0 d_proj.1
  80.1 1.9 %collective-permute-start.13 = (bf16[256,1152]{1,0:T(8,128)(2,1)S(1)}, bf16[256,1152]{1,0:T(8,128)(2,1)S(1)}, u32[]{:S(2)}, u32[]{:S(2)}) collective-permute-start(bf16[256,1152]{1,0:T(8,128)(2,1)S(1)} %get-tuple-element.30.dproj_ref.own_ref), channel_id=1, source_target_pairs={{0,16},{16,0},{1,17},{17,1},{2,18},{18,2},{3,19},{19,3},{4,20},{20... | collective-permute-start | bytes 1769480 | tf_op jit(solution)/shard_map/ppermute | solution.py:344
  82.0 0.0 copy-done
  82.0 2.2 %d_features.1 = (bf16[128,1408]{1,0:T(8,128)(2,1)}, f32[1,1408]{1,0:T(1,128)S(1)}) custom-call(bf16[256,1152]{1,0:T(8,128)(2,1)S(1)} %get-tuple-element.30.dproj_ref.own_ref, bf16[128,1408]{1,0:T(8,128)(2,1)S(1)} %bitcast.14, f32[1,1408]{1,0:T(1,128)S(1)} %reshape.18.gain_ref, bf16[128,1408]{1,0:T(8,128)(2,1)S(1)} %normed.1.n0, ...), custom_call_target="tpu_custom_call" | custom-call | flops 830472192 | bytes 5286912 | tf_op jit(solution)/shard_map/d_features/pallas_call | solution.py:38
  84.2 0.0 collective-permute-done.13.got_ref
  84.2 3.7 %head.1 = bf16[1024,512]{1,0:T(8,128)(2,1)S(1)} custom-call(bf16[256,1152]{1,0:T(8,128)(2,1)S(1)} %get-tuple-element.30.dproj_ref.own_ref, bf16[256,1152]{1,0:T(8,128)(2,1)S(1)} %collective-permute-done.13.got_ref, bf16[384,512]{1,0:T(8,128)(2,1)S(1)} %get-tuple-element.31.pick_ref, bf16[128,1408]{1,0:T(8,128)(2,1)S(1)} %collective-permute-done.n1, ...), custom_call_target="tpu_custom_call" | custom-call | flops 1283457024 | bytes 6598144 | tf_op jit(solution)/shard_map/head/pallas_call | solution.py:38
  87.9 46.0 %all_to_all.22 = bf16[128,8,512]{2,1,0:T(8,128)(2,1)S(1)} all-to-all(bf16[128,8,512]{2,1,0:T(8,128)(2,1)S(1)} %bitcast.12), channel_id=1, replica_groups=mesh['x'=2,'z'=8,'c'=2,'hx'=2,'y'=8] {'z','hx','y'}, dimensions={0} | all-to-all | bytes 2097152 | tf_op jit(solution)/shard_map/all_to_all | solution.py:372
  133.8 0.7 reduce.2
  134.6 14.9 %all_to_all.23 = bf16[16,8,512]{2,1,0:T(8,128)(2,1)S(1)} all-to-all(bf16[16,8,512]{2,1,0:T(8,128)(2,1)S(1)} %bitcast.15), channel_id=1, replica_groups=mesh['x'=2,'z'=8,'c'=2,'hx'=2,'y'=8] {'hx','y'}, dimensions={0} | all-to-all | bytes 262144 | tf_op jit(solution)/shard_map/all_to_all | solution.py:381
  149.5 0.7 unpack.1
  150.2 0.6 reduce.1
  (4 shorter events, 0.0 us)
Async XLA Ops:
  0.6 1.0 copy-start.3
  1.7 11.6 %collective-permute-start.4 = (bf16[128,1152]{1,0:T(8,128)(2,1)S(1)}, bf16[128,1152]{1,0:T(8,128)(2,1)S(1)}, u32[]{:S(2)}, u32[]{:S(2)}) collective-permute-start(bf16[128,1152]{1,0:T(8,128)(2,1)S(1)} %text_unit.1.refs_0_), channel_id=1, source_target_pairs={{0,16},{16,0},{1,17},{17,1},{2,18},{18,2},{3,19},{19,3},{4,20},{20... | collective-permute-start | bytes 884744 | tf_op jit(solution)/shard_map/ppermute | solution.py:283
  3.7 15.6 %collective-permute-start.3 = (bf16[128,1152]{1,0:T(8,128)(2,1)S(1)}, bf16[128,1152]{1,0:T(8,128)(2,1)S(1)}, u32[]{:S(2)}, u32[]{:S(2)}) collective-permute-start(bf16[128,1152]{1,0:T(8,128)(2,1)S(1)} %text_unit.1.refs_0_), channel_id=1, source_target_pairs={{0,32},{16,240},{32,64},{48,16},{64,96},{80,48},{96,128},{112,80},... | collective-permute-start | bytes 884744 | tf_op jit(solution)/shard_map/ppermute | solution.py:285
  8.7 1.0 copy-start.1
  9.9 26.0 %collective-permute-start.1 = (bf16[128,1408]{1,0:T(8,128)(2,1)S(1)}, bf16[128,1408]{1,0:T(8,128)(2,1)S(1)}, u32[]{:S(2)}, u32[]{:S(2)}) collective-permute-start(bf16[128,1408]{1,0:T(8,128)(2,1)S(1)} %normed.1.n0), channel_id=1, source_target_pairs={{0,256},{256,0},{1,257},{257,1},{2,258},{258,2},{3,259},{259,3},{4... | collective-permute-start | bytes 1081352 | tf_op jit(solution)/shard_map/ppermute | solution.py:292
  13.4 13.3 %collective-permute-start.5 = (bf16[128,1152]{1,0:T(8,128)(2,1)S(1)}, bf16[128,1152]{1,0:T(8,128)(2,1)S(1)}, u32[]{:S(2)}, u32[]{:S(2)}) collective-permute-start(bf16[128,1152]{1,0:T(8,128)(2,1)S(1)} %collective-permute-done.4), channel_id=1, source_target_pairs={{0,32},{16,240},{32,64},{48,16},{64,96},{80,48},{96,128},{112,80},... | collective-permute-start | bytes 884744 | tf_op jit(solution)/shard_map/ppermute | solution.py:288
  19.3 10.5 %collective-permute-start.6 = (bf16[128,1152]{1,0:T(8,128)(2,1)S(1)}, bf16[128,1152]{1,0:T(8,128)(2,1)S(1)}, u32[]{:S(2)}, u32[]{:S(2)}) collective-permute-start(bf16[128,1152]{1,0:T(8,128)(2,1)S(1)} %collective-permute-done.3.refs_1_), channel_id=1, source_target_pairs={{0,32},{16,240},{32,64},{48,16},{64,96},{80,48},{96,128},{112,80},... | collective-permute-start | bytes 884744 | tf_op jit(solution)/shard_map/ppermute | solution.py:285
  26.6 12.6 %collective-permute-start.7 = (bf16[128,1152]{1,0:T(8,128)(2,1)S(1)}, bf16[128,1152]{1,0:T(8,128)(2,1)S(1)}, u32[]{:S(2)}, u32[]{:S(2)}) collective-permute-start(bf16[128,1152]{1,0:T(8,128)(2,1)S(1)} %collective-permute-done.5.refs_2_), channel_id=1, source_target_pairs={{0,32},{16,240},{32,64},{48,16},{64,96},{80,48},{96,128},{112,80},... | collective-permute-start | bytes 884744 | tf_op jit(solution)/shard_map/ppermute | solution.py:288
  29.8 12.0 %collective-permute-start.8 = (bf16[128,1152]{1,0:T(8,128)(2,1)S(1)}, bf16[128,1152]{1,0:T(8,128)(2,1)S(1)}, u32[]{:S(2)}, u32[]{:S(2)}) collective-permute-start(bf16[128,1152]{1,0:T(8,128)(2,1)S(1)} %collective-permute-done.6.refs_3_), channel_id=1, source_target_pairs={{0,32},{16,240},{32,64},{48,16},{64,96},{80,48},{96,128},{112,80},... | collective-permute-start | bytes 884744 | tf_op jit(solution)/shard_map/ppermute | solution.py:285
  31.7 14.8 %collective-permute-start = (bf16[128,1408]{1,0:T(8,128)(2,1)S(1)}, bf16[128,1408]{1,0:T(8,128)(2,1)S(1)}, u32[]{:S(2)}, u32[]{:S(2)}) collective-permute-start(bf16[128,1408]{1,0:T(8,128)(2,1)S(1)} %normed.1.n0), channel_id=1, source_target_pairs={{0,16},{16,0},{1,17},{17,1},{2,18},{18,2},{3,19},{19,3},{4,20},{20... | collective-permute-start | bytes 1081352 | tf_op jit(solution)/shard_map/ppermute | solution.py:293
  35.9 10.6 %collective-permute-start.2 = (bf16[128,1408]{1,0:T(8,128)(2,1)S(1)}, bf16[128,1408]{1,0:T(8,128)(2,1)S(1)}, u32[]{:S(2)}, u32[]{:S(2)}) collective-permute-start(bf16[128,1408]{1,0:T(8,128)(2,1)S(1)} %collective-permute-done.1.n2), channel_id=1, source_target_pairs={{0,16},{16,0},{1,17},{17,1},{2,18},{18,2},{3,19},{19,3},{4,20},{20... | collective-permute-start | bytes 1081352 | tf_op jit(solution)/shard_map/ppermute | solution.py:294
  39.2 12.6 %collective-permute-start.9 = (bf16[128,1152]{1,0:T(8,128)(2,1)S(1)}, bf16[128,1152]{1,0:T(8,128)(2,1)S(1)}, u32[]{:S(2)}, u32[]{:S(2)}) collective-permute-start(bf16[128,1152]{1,0:T(8,128)(2,1)S(1)} %collective-permute-done.7.refs_4_), channel_id=1, source_target_pairs={{0,32},{16,240},{32,64},{48,16},{64,96},{80,48},{96,128},{112,80},... | collective-permute-start | bytes 884744 | tf_op jit(solution)/shard_map/ppermute | solution.py:288
  41.8 10.4 %collective-permute-start.10 = (bf16[128,1152]{1,0:T(8,128)(2,1)S(1)}, bf16[128,1152]{1,0:T(8,128)(2,1)S(1)}, u32[]{:S(2)}, u32[]{:S(2)}) collective-permute-start(bf16[128,1152]{1,0:T(8,128)(2,1)S(1)} %collective-permute-done.8.refs_5_), channel_id=1, source_target_pairs={{0,32},{16,240},{32,64},{48,16},{64,96},{80,48},{96,128},{112,80},... | collective-permute-start | bytes 884744 | tf_op jit(solution)/shard_map/ppermute | solution.py:285
  56.7 4.0 %collective-permute-start.11 = (bf16[272,1152]{1,0:T(8,128)(2,1)S(1)}, bf16[272,1152]{1,0:T(8,128)(2,1)S(1)}, u32[]{:S(2)}, u32[]{:S(2)}) collective-permute-start(bf16[272,1152]{1,0:T(8,128)(2,1)S(1)} %get-tuple-element.24), channel_id=1, source_target_pairs={{0,16},{16,0},{1,17},{17,1},{2,18},{18,2},{3,19},{19,3},{4,20},{20... | collective-permute-start | bytes 1880072 | tf_op jit(solution)/shard_map/ppermute | solution.py:329
  60.7 21.3 %copy-start = (bf16[1408,1152]{1,0:T(8,128)(2,1)S(1)}, bf16[1408,1152]{1,0:T(8,128)(2,1)}, u32[]{:S(2)}) copy-start(bf16[1408,1152]{1,0:T(8,128)(2,1)} %w_ref.5) | copy-start | bytes 9732100
  60.9 18.2 %collective-permute-start.12 = (bf16[272,1152]{1,0:T(8,128)(2,1)S(1)}, bf16[272,1152]{1,0:T(8,128)(2,1)S(1)}, u32[]{:S(2)}, u32[]{:S(2)}) collective-permute-start(bf16[272,1152]{1,0:T(8,128)(2,1)S(1)} %get-tuple-element.27), channel_id=1, source_target_pairs={{0,256},{256,0},{1,257},{257,1},{2,258},{258,2},{3,259},{259,3},{4... | collective-permute-start | bytes 1880072 | tf_op jit(solution)/shard_map/ppermute | solution.py:338
  79.1 2.9 %copy-start.2 = (bf16[1,128,1408]{2,1,0:T(8,128)(2,1)S(1)}, bf16[1,128,1408]{2,1,0:T(8,128)(2,1)}, u32[]{:S(2)}) copy-start(bf16[1,128,1408]{2,1,0:T(8,128)(2,1)} %param.6) | copy-start | bytes 1081348
  80.1 4.1 %collective-permute-start.13 = (bf16[256,1152]{1,0:T(8,128)(2,1)S(1)}, bf16[256,1152]{1,0:T(8,128)(2,1)S(1)}, u32[]{:S(2)}, u32[]{:S(2)}) collective-permute-start(bf16[256,1152]{1,0:T(8,128)(2,1)S(1)} %get-tuple-element.30.dproj_ref.own_ref), channel_id=1, source_target_pairs={{0,16},{16,0},{1,17},{17,1},{2,18},{18,2},{3,19},{19,3},{4,20},{20... | collective-permute-start | bytes 1769480 | tf_op jit(solution)/shard_map/ppermute | solution.py:344

commit v2 on v1

v2 whole, which is shorter than its diff:
```python
import functools

import jax
import jax.numpy as jnp
from jax import lax
from jax.experimental import pallas as pl
from jax.experimental.pallas import tpu as pltpu
from jax.sharding import Mesh, PartitionSpec as P

EPSILON = 1e-06
ROWS = 128
W = 1408
E = 1152
SHARE = 44
F32 = jnp.float32
BF16 = jnp.bfloat16

X, Z, C, HX, Y = "x", "z", "c", "hx", "y"
NZ = 8
N_GROUP = 16
EARLY, LATE = 5, 3
PIECE = 512
BLOCK = 128
EXTRA = 16
GAIN_AT = 112

SWAP = [(0, 1), (1, 0)]
HOP = [
    (z * 2 + c, ((z + (1 if c == 0 else -1)) % NZ) * 2 + c) for z in range(NZ) for c in range(2)
]

VMEM = pl.BlockSpec(memory_space=pltpu.VMEM)
ANY = pl.BlockSpec(memory_space=pl.ANY)
SMEM = pl.BlockSpec(memory_space=pltpu.SMEM)


def call(kernel, out_shape, *operands, specs=None, outs=None, scratch=(), flops=0, name=None):
    leaves = jax.tree.leaves(out_shape)
    moved = sum(o.size * o.dtype.itemsize for o in (*operands, *leaves))
    return pl.pallas_call(
        kernel,
        out_shape=out_shape,
        in_specs=specs or [VMEM] * len(operands),
        out_specs=outs or jax.tree.map(lambda _: VMEM, out_shape),
        scratch_shapes=list(scratch),
        name=name,
        cost_estimate=pl.CostEstimate(flops=flops, bytes_accessed=moved, transcendentals=0),
        compiler_params=pltpu.CompilerParams(vmem_limit_bytes=32 << 20),
    )(*operands)


def out(shape, dtype):
    return jax.ShapeDtypeStruct(shape, dtype)


def text_kernel(cap_ref, unit_ref):
    values = cap_ref[...].astype(F32)
    scale = lax.rsqrt(jnp.sum(values * values, axis=1, keepdims=True) + EPSILON)
    unit_ref[...] = (values * scale).astype(BF16)


def moments(values):
    mean = jnp.mean(values, axis=1, keepdims=True)
    centred = values - mean
    scale = lax.rsqrt(jnp.mean(centred * centred, axis=1, keepdims=True) + EPSILON)
    return centred * scale, scale


def norm_kernel(x_ref, gain_ref, after_ref, normed_ref):
    del after_ref
    x_hat, _ = moments(x_ref[...].astype(F32))
    normed_ref[...] = (x_hat * gain_ref[...]).astype(BF16)


def project_kernel(n_own, n_far, w_ref, img_ref, unit_ref, pnorm_ref, rows_ref):
    rows_ref[: 2 * ROWS, :] = n_own[...]
    rows_ref[2 * ROWS :, :] = n_far[...]
    proj = jnp.dot(rows_ref[...], w_ref[...], preferred_element_type=F32)
    pnorm = lax.rsqrt(jnp.sum(proj * proj, axis=1, keepdims=True) + EPSILON)
    unit = proj * pnorm
    img_ref[...] = unit.astype(BF16)
    unit_ref[...] = unit[: 2 * ROWS]
    pnorm_ref[...] = jnp.broadcast_to(pnorm[: 2 * ROWS], (2 * ROWS, 128))


def pick_kernel(where_ref, after_ref, n_own, n_far, pick_ref):
    del after_ref
    row = lax.broadcasted_iota(jnp.int32, (NZ * 48, 1), 0)
    block = row // 48
    inside = row - block * 48
    source = jnp.where(inside < SHARE, SHARE * (where_ref[0] + 2 * block) + inside, -1)
    column = lax.broadcasted_iota(jnp.int32, (NZ * 48, W), 1)
    select = (column == source).astype(F32).astype(BF16)
    for i, n in enumerate((n_own, n_far)):
        picked = lax.dot_general(
            select, n[...], (((1,), (1,)), ((), ())), preferred_element_type=F32
        )
        pick_ref[:, 2 * ROWS * i : 2 * ROWS * (i + 1)] = picked.astype(BF16)


def fold_product(grown):
    rows = grown.shape[0]
    while rows > 8:
        rows //= 2
        one, two = grown[:rows], grown[rows:]
        grown = one + two + one * two
    return grown


def fold_sum(values):
    rows = values.shape[0]
    while rows > 8:
        rows //= 2
        values = values[:rows] + values[rows:]
    return values


def log1p(value):
    up = 1.0 + value
    gap = up - 1.0
    return jnp.where(gap == 0.0, value, jnp.log(up) * (value / jnp.where(gap == 0.0, 1.0, gap)))


def pair_terms(sc_ref, img_ref, texts, text, slope, own_first):
    for i, piece in enumerate(texts):
        text[pl.ds(i * ROWS, ROWS), :] = piece[...]
    scale, bias = sc_ref[0], sc_ref[1]
    total = jnp.zeros((8, 128), F32)
    count = len(texts)
    for start in range(0, count, 2):
        span = min(2, count - start)
        sims = lax.dot_general(
            img_ref[...],
            text[pl.ds(start * ROWS, span * ROWS), :],
            (((1,), (1,)), ((), ())),
            preferred_element_type=F32,
        )
        for half in range(span):
            chunk = start + half
            turned = scale * sims[:, half * ROWS : (half + 1) * ROWS] + bias
            if own_first and chunk == 0:
                shape = (4 * ROWS, ROWS)
                match = lax.broadcasted_iota(jnp.int32, shape, 0) == lax.broadcasted_iota(
                    jnp.int32, shape, 1
                )
                turned = jnp.where(match, -turned, turned)
            small = jnp.exp(-jnp.abs(turned))
            below = 1.0 + small
            inverse = pl.reciprocal(below, approx=True)
            inverse = inverse * (2.0 - below * inverse)
            sig = jnp.where(turned >= 0.0, 1.0, small) * inverse
            if own_first and chunk == 0:
                sig = jnp.where(match, -sig, sig)
            slope[:, chunk * ROWS : (chunk + 1) * ROWS] = sig.astype(BF16)
            total = total + fold_sum(jnp.maximum(turned, 0.0)) + log1p(fold_product(small))
    return total


def first_pairs_kernel(sc_ref, img_ref, *refs):
    texts, (grad_ref, loss_ref, text, slope) = refs[:EARLY], refs[EARLY:]
    loss_ref[...] = pair_terms(sc_ref, img_ref, texts, text, slope, True)
    grad_ref[...] = jnp.dot(slope[...], text[...], preferred_element_type=F32)


def last_pairs_kernel(sc_ref, img_ref, grad_ref, part_ref, *refs):
    texts, (keep_ref, send_ref, loss_ref, text, slope) = refs[:LATE], refs[LATE:]
    total = part_ref[...] + pair_terms(sc_ref, img_ref, texts, text, slope, False)
    loss = jnp.broadcast_to(jnp.sum(total, keepdims=True), (1, 128))
    loss_ref[...] = loss
    grad = grad_ref[...] + jnp.dot(slope[...], text[...], preferred_element_type=F32)
    keep_ref[...] = grad[: 2 * ROWS]
    send_ref[: 2 * ROWS, :] = grad[2 * ROWS :].astype(BF16)
    send_ref[2 * ROWS :, :] = loss_rows(loss)


def loss_rows(loss):
    high = loss.astype(BF16).astype(F32)
    row = jnp.concatenate([high, loss - high, jnp.zeros((1, E - 256), F32)], axis=1)
    return jnp.broadcast_to(row, (EXTRA, E)).astype(BF16)


def got_loss(got_ref):
    row = got_ref[2 * ROWS :, :256].astype(F32)[:1]
    return row[:, :128] + row[:, 128:]


def add_kernel(keep_ref, loss_ref, got_ref, sum_ref, loss_out, send_ref):
    total = keep_ref[...] + got_ref[: 2 * ROWS, :].astype(F32)
    sum_ref[...] = total
    send_ref[: 2 * ROWS, :] = total.astype(BF16)
    loss = loss_ref[...] + got_loss(got_ref)
    loss_out[...] = loss
    send_ref[2 * ROWS :, :] = loss_rows(loss)


def dproj_kernel(
    sc_ref, sum_ref, loss_ref, got_ref, unit_ref, pnorm_ref, after_ref, dproj_ref, loss_out
):
    del after_ref
    loss_out[...] = loss_ref[...] + got_loss(got_ref)
    for i in range(2):
        rows, other = pl.ds(i * ROWS, ROWS), pl.ds((1 - i) * ROWS, ROWS)
        grad = sc_ref[0] * (sum_ref[rows, :] + got_ref[other, :].astype(F32))
        unit = unit_ref[rows, :]
        inner = jnp.sum(unit * grad, axis=1, keepdims=True)
        dproj_ref[rows, :] = ((grad - unit * inner) * pnorm_ref[rows, 0:1]).astype(BF16)


def back(dproj, w_ref):
    return lax.dot_general(dproj, w_ref[...], (((1,), (1,)), ((), ())), preferred_element_type=F32)


def features_kernel(dproj_ref, x_ref, gain_ref, n_own, w_ref, feat_ref, part_ref):
    d_normed = back(dproj_ref[...], w_ref)
    own = d_normed[:ROWS]
    part_ref[...] = jnp.sum(n_own[...].astype(F32) * d_normed, axis=0, keepdims=True)
    x_hat, scale = moments(x_ref[...].astype(F32))
    d_hat = own * gain_ref[...]
    feat = scale * (
        d_hat
        - jnp.mean(d_hat, axis=1, keepdims=True)
        - x_hat * jnp.mean(d_hat * x_hat, axis=1, keepdims=True)
    )
    feat_ref[...] = feat.astype(BF16)


def head_kernel(own_ref, got_ref, pick_ref, n_far, w_ref, gain_ref, part_ref, loss_ref, out_ref):
    head = jnp.dot(pick_ref[:, : 2 * ROWS], own_ref[...], preferred_element_type=F32) + jnp.dot(
        pick_ref[:, 2 * ROWS :], got_ref[...], preferred_element_type=F32
    )
    d_normed = back(got_ref[...], w_ref)
    gain = part_ref[...] + jnp.sum(n_far[...].astype(F32) * d_normed, axis=0, keepdims=True)
    gain = gain / gain_ref[...]
    rows = [
        gain[:, :E],
        jnp.concatenate([gain[:, E:], loss_ref[...], jnp.zeros((1, 2 * E - W - 128), F32)], axis=1),
    ]
    high = [r.astype(BF16).astype(F32) for r in rows]
    low = [r - h for r, h in zip(rows, high)]
    index = lax.broadcasted_iota(jnp.int32, (16, E), 0)
    extra = jnp.zeros((16, E), F32)
    for i, r in enumerate(high + low):
        extra = jnp.where(index == 12 + i, r, extra)
    for k in range(NZ):
        out_ref[48 * k : 48 * k + 32, :] = head[48 * k : 48 * k + 32].astype(BF16)
        tail = jnp.where(index < 12, head[48 * k + 32 : 48 * k + 48], extra)
        out_ref[48 * k + 32 : 48 * k + 48, :] = tail.astype(BF16)


def sum_z_kernel(got_ref, out_ref):
    total = got_ref[...].astype(F32).reshape(NZ, 48, E).sum(axis=0)
    out_ref[0:48, :] = total[:, :512].astype(BF16)
    out_ref[48:96, :] = total[:, 512:1024].astype(BF16)
    for i in range(3):
        out_ref[96:112, 128 * i : 128 * (i + 1)] = total[16 * i : 16 * (i + 1), 1024:].astype(BF16)
    out_ref[96:112, 384:] = jnp.zeros((16, 128), BF16)
    both = total[44:46] + total[46:48]
    gain = jnp.concatenate([both[0:1], both[1:2]], axis=1)
    out_ref[GAIN_AT:BLOCK, :] = split_rows(gain[:, :W], gain[:, W : W + 128])


def split_rows(gain, loss):
    rows = [gain[:, :512], gain[:, 512:1024], jnp.concatenate([gain[:, 1024:], loss], axis=1)]
    high = [r.astype(BF16).astype(F32) for r in rows]
    low = [r - h for r, h in zip(rows, high)]
    index = lax.broadcasted_iota(jnp.int32, (16, PIECE), 0)
    packed = jnp.zeros((16, PIECE), F32)
    for i, r in enumerate(high + low):
        packed = jnp.where(index == i, r, packed)
    return packed.astype(BF16)


def sum_groups_kernel(where_ref, got_ref, out_ref):
    total = got_ref[...].astype(F32).reshape(N_GROUP, 8, PIECE).sum(axis=0)
    rest = jnp.concatenate([total[3:], total[:3]], axis=0)
    index = lax.broadcasted_iota(jnp.int32, (8, PIECE), 0)
    whole = total + rest
    high = whole.astype(BF16).astype(F32)
    low = whole - high
    moved = jnp.concatenate([low[5:], low[:5]], axis=0)
    split = jnp.where(index < 3, high, jnp.where(index < 6, moved, 0.0))
    piece = jnp.where(where_ref[1] == GAIN_AT // 8, split, total)
    copies = jnp.broadcast_to(piece[None], (N_GROUP, 8, PIECE)).reshape(BLOCK, PIECE)
    out_ref[...] = copies.astype(BF16)


def unpack_kernel(got_ref, head_ref, gain_ref, loss_ref):
    block = got_ref[...].astype(F32)
    head_ref[:, :512] = block[:SHARE]
    head_ref[:, 512:1024] = block[48 : 48 + SHARE]
    tail = block[96:112]
    head_ref[0:16, 1024:] = tail[:, 0:128]
    head_ref[16:32, 1024:] = tail[:, 128:256]
    head_ref[32:SHARE, 1024:] = tail[: SHARE - 32, 256:384]
    rows = block[GAIN_AT : GAIN_AT + 3] + block[GAIN_AT + 3 : GAIN_AT + 6]
    gain_ref[:, :512] = rows[0:1]
    gain_ref[:, 512:1024] = rows[1:2]
    gain_ref[:, 1024:] = rows[2:3, :384]
    loss_ref[0, 0] = jnp.max(rows[2:3, 384:]) * (1.0 / (N_GROUP * NZ * 4 * ROWS))


def per_device(pooled, captions, gain, w, scale, bias):
    x = pooled[0]
    gain = gain.reshape(1, W)
    scalars = jnp.concatenate([scale, bias])
    where = jnp.stack(
        [
            lax.axis_index(X) * 16 + lax.axis_index(C),
            lax.axis_index(HX) * 8 + lax.axis_index(Y),
        ]
    ).astype(jnp.int32)

    across = functools.partial(lax.ppermute, axis_name=X, perm=SWAP)
    between = functools.partial(lax.ppermute, axis_name=C, perm=SWAP)
    hop = functools.partial(lax.ppermute, axis_name=(Z, C), perm=HOP)

    text = call(text_kernel, out((ROWS, E), BF16), captions[0], name="text_unit")
    texts = [text]
    swapped = between(text)
    one, two = text, swapped
    for step in range(4):
        one = hop(one)
        texts.append(one)
        if step < 3:
            two = hop(two)
            texts.append(two)

    n0 = call(norm_kernel, out((ROWS, W), BF16), x, gain, swapped, specs=[VMEM, VMEM, ANY], name="normed")
    n_own = jnp.concatenate([n0, across(n0)], axis=0)
    n_far = between(n_own)
    img, unit, pnorm = call(
        project_kernel,
        (out((4 * ROWS, E), BF16), out((2 * ROWS, E), F32), out((2 * ROWS, 128), F32)),
        n_own,
        n_far,
        w,
        scratch=[pltpu.VMEM((4 * ROWS, W), BF16)],
        flops=2 * 4 * ROWS * W * E,
        name="project",
    )
    grad, loss = call(
        first_pairs_kernel,
        (out((4 * ROWS, E), F32), out((8, 128), F32)),
        scalars,
        img,
        *texts[:EARLY],
        specs=[SMEM] + [VMEM] * (1 + EARLY),
        scratch=[pltpu.VMEM((EARLY * ROWS, E), BF16), pltpu.VMEM((4 * ROWS, EARLY * ROWS), BF16)],
        flops=4 * 4 * ROWS * EARLY * ROWS * E,
        name="first_pairs",
    )
    keep, send, loss = call(
        last_pairs_kernel,
        (out((2 * ROWS, E), F32), out((2 * ROWS + EXTRA, E), BF16), out((1, 128), F32)),
        scalars,
        img,
        grad,
        loss,
        *texts[EARLY:],
        specs=[SMEM] + [VMEM] * (3 + LATE),
        scratch=[pltpu.VMEM((LATE * ROWS, E), BF16), pltpu.VMEM((4 * ROWS, LATE * ROWS), BF16)],
        flops=4 * 4 * ROWS * LATE * ROWS * E,
        name="last_pairs",
    )
    total, loss, send = call(
        add_kernel,
        (out((2 * ROWS, E), F32), out((1, 128), F32), out((2 * ROWS + EXTRA, E), BF16)),
        keep,
        loss,
        between(send),
        name="add_cores",
    )
    pick = call(
        pick_kernel,
        out((NZ * 48, 4 * ROWS), BF16),
        where,
        loss,
        n_own,
        n_far,
        specs=[SMEM, ANY] + [VMEM] * 2,
        flops=2 * 4 * ROWS * W * NZ * 48,
        name="pick",
    )
    dproj, loss = call(
        dproj_kernel,
        (out((2 * ROWS, E), BF16), out((1, 128), F32)),
        scalars,
        total,
        loss,
        across(send),
        unit,
        pnorm,
        pick,
        specs=[SMEM] + [VMEM] * 5 + [ANY],
        name="d_proj",
    )
    dproj_far = between(dproj)
    d_features, gain_part = call(
        features_kernel,
        (out((ROWS, W), BF16), out((1, W), F32)),
        dproj,
        x,
        gain,
        n_own,
        w,
        flops=4 * ROWS * W * E,
        name="d_features",
    )
    packed = call(
        head_kernel,
        out((NZ * 48, E), BF16),
        dproj,
        dproj_far,
        pick,
        n_far,
        w,
        gain,
        gain_part,
        loss,
        flops=4 * ROWS * W * E + 8 * ROWS * NZ * 48 * E,
        name="head",
    )
    packed = lax.all_to_all(packed, Z, 0, 0, tiled=True)
    block = call(sum_z_kernel, out((BLOCK, PIECE), BF16), packed, name="sum_z")
    block = lax.all_to_all(block, (HX, Y), 0, 0, tiled=True)
    piece = call(
        sum_groups_kernel,
        out((BLOCK, PIECE), BF16),
        where,
        block,
        specs=[SMEM, VMEM],
        name="sum_groups",
    )
    block = lax.all_to_all(piece, (HX, Y), 0, 0, tiled=True)
    head, d_gain, loss = call(
        unpack_kernel,
        (out((SHARE, E), F32), out((1, W), F32), out((1, 1), F32)),
        block,
        outs=(VMEM, VMEM, SMEM),
        name="unpack",
    )
    return loss.reshape(()), d_features[None], d_gain.reshape(W), head


def solution(mesh):
    fine = Mesh(mesh.devices.reshape(2, NZ, 2, 2, 8), (X, Z, C, HX, Y))
    rows = P((HX, Y), (X, Z, C), None)
    return jax.shard_map(
        per_device,
        mesh=fine,
        in_specs=(rows, rows, P(), P(), P(), P()),
        out_specs=(P(), rows, P(), P((X, Z, C), None)),
        check_vma=False,
    )
```

time: 152 us -> 159 us (1.046)
  waiting for transfers between devices: 25.6 us -> 33.1 us
  starting transfers between devices: 40 us -> 35.7 us
  local copies, waits for them, and re-layouts: 2.65 us -> 5.68 us
  blocking collectives: 60.9 us -> 62.6 us
    ppermute x3, waiting for transfers between devices: 4.7 us -> 10.4 us  [per_device(): two = hop(two)]
    ppermute x4 -> x3, waiting for transfers between devices: 0.01 us -> 5.5 us  [the longest x1 4.65 us: per_device(): n_own = jnp.concatenate([n0, across(n0)], axis=0)]
    all_to_all x1 -> x2, blocking collectives: 46 us -> 49.5 us  [the longest x1 29.9 us: per_device(): packed = lax.all_to_all(packed, Z, 0, 0, tiled=True)]
    unnamed x8 -> x14, local copies, waits for them, and re-layouts: 1.95 us -> 4.97 us
    ppermute x1, waiting for transfers between devices: 15.6 us -> 12.6 us  [per_device(): across(send)]
    ppermute x4 -> x3, starting transfers between devices: 11.4 us -> 8.83 us  [the longest x1 3.51 us: per_device(): n_far = between(n_own)]
    ppermute x3, starting transfers between devices: 8.74 us -> 6.51 us  [per_device(): two = hop(two)]
    all_to_all x1, blocking collectives: 14.9 us -> 13.1 us  [per_device(): block = lax.all_to_all(piece, (HX, Y), 0, 0, tiled=True)]
  transfers between devices with their start and end apart: 14 -> 13, of which waited for: 6 -> 9; matrix products, arithmetic and copies ran while one was open for 1% -> 1% of each run, Pallas kernels for 5% -> 6%
where the time goes in v2:
time: 159 us; the launch traced here: 158 us
  blocking collectives  62.6 us (39%)
  starting transfers between devices  35.7 us (22%)
  waiting for transfers between devices  33.1 us (21%)
  Pallas kernels  18.3 us (12%)
  local copies, waits for them, and re-layouts  5.68 us (4%)
  between operations  2.19 us (1%)
    all_to_all x1, blocking collectives, per_device(): packed = lax.all_to_all(packed, Z, 0, 0, tiled=True)  29.9 us
    all_to_all x1, blocking collectives, per_device(): block = lax.all_to_all(block, (HX, Y), 0, 0, tiled=True)  19.5 us
    pallas_call x13, Pallas kernels, call(): pl.pallas_call(kernel, out_shape=out_shape, in_specs=specs or [VMEM] * le...  18.3 us
    all_to_all x1, blocking collectives, per_device(): block = lax.all_to_all(piece, (HX, Y), 0, 0, tiled=True)  13.1 us
    ppermute x1, waiting for transfers between devices, per_device(): across(send)  12.6 us
    ppermute x4, starting transfers between devices, per_device(): one = hop(one)  12 us
    ppermute x3, waiting for transfers between devices, per_device(): two = hop(two)  10.4 us
    ppermute x3, starting transfers between devices, per_device(): two = hop(two)  6.51 us
  transfers between devices with their start and end apart: 13, of which 9 were waited for; matrix products, arithmetic and copies ran while one was open for 1% of the time, Pallas kernels for 6%

profile of v2, /device:TPU:8, one launch (start us, length us, event | category | flops | bytes accessed | tf_op | source)
XLA Modules:
  0.0 158.4 jit_solution(10006970703879394610)
XLA Ops:
  0.6 1.0 copy-done.6
  1.6 0.1 text_unit.1.refs_0_
  1.7 1.9 %collective-permute-start = (bf16[128,1152]{1,0:T(8,128)(2,1)S(1)}, bf16[128,1152]{1,0:T(8,128)(2,1)S(1)}, u32[]{:S(2)}, u32[]{:S(2)}) collective-permute-start(bf16[128,1152]{1,0:T(8,128)(2,1)S(1)} %text_unit.1.refs_0_), channel_id=1, source_target_pairs={{0,16},{16,0},{1,17},{17,1},{2,18},{18,2},{3,19},{19,3},{4,20},{20... | collective-permute-start | bytes 884744 | tf_op jit(solution)/shard_map/ppermute | solution.py:319
  3.7 0.7 reshape.23.gain_ref
  4.4 0.8 collective-permute-done.after_ref
  5.2 1.0 copy-done.2
  6.2 0.3 normed.1
  6.5 3.4 %collective-permute-start.1 = (bf16[128,1408]{1,0:T(8,128)(2,1)S(1)}, bf16[128,1408]{1,0:T(8,128)(2,1)S(1)}, u32[]{:S(2)}, u32[]{:S(2)}) collective-permute-start(bf16[128,1408]{1,0:T(8,128)(2,1)S(1)} %normed.1), channel_id=1, source_target_pairs={{0,256},{256,0},{1,257},{257,1},{2,258},{258,2},{3,259},{259,3},{4... | collective-permute-start | bytes 1081352 | tf_op jit(solution)/shard_map/ppermute | solution.py:329
  9.9 4.3 %collective-permute-start.3 = (bf16[128,1152]{1,0:T(8,128)(2,1)S(1)}, bf16[128,1152]{1,0:T(8,128)(2,1)S(1)}, u32[]{:S(2)}, u32[]{:S(2)}) collective-permute-start(bf16[128,1152]{1,0:T(8,128)(2,1)S(1)} %text_unit.1.refs_0_), channel_id=1, source_target_pairs={{0,32},{16,240},{32,64},{48,16},{64,96},{80,48},{96,128},{112,80},... | collective-permute-start | bytes 884744 | tf_op jit(solution)/shard_map/ppermute | solution.py:322
  14.2 4.7 %collective-permute-done.1 = bf16[128,1408]{1,0:T(8,128)(2,1)S(1)} collective-permute-done((bf16[128,1408]{1,0:T(8,128)(2,1)S(1)}, bf16[128,1408]{1,0:T(8,128)(2,1)S(1)}, u32[]{:S(2)}, u32[]{:S(2)}) %collective-permute-start.1) | collective-permute-done | bytes 360480 | tf_op jit(solution)/shard_map/ppermute | solution.py:329
  18.8 0.1 pad_maximum_fusion.n_own
  18.9 3.5 %collective-permute-start.2 = (bf16[256,1408]{1,0:T(8,128)(2,1)S(1)}, bf16[256,1408]{1,0:T(8,128)(2,1)S(1)}, u32[]{:S(2)}, u32[]{:S(2)}) collective-permute-start(bf16[256,1408]{1,0:T(8,128)(2,1)S(1)} %pad_maximum_fusion.n_own), channel_id=1, source_target_pairs={{0,16},{16,0},{1,17},{17,1},{2,18},{18,2},{3,19},{19,3},{4,20},{20... | collective-permute-start | bytes 2162696 | tf_op jit(solution)/shard_map/ppermute | solution.py:330
  22.4 2.7 %collective-permute-start.4 = (bf16[128,1152]{1,0:T(8,128)(2,1)S(1)}, bf16[128,1152]{1,0:T(8,128)(2,1)S(1)}, u32[]{:S(2)}, u32[]{:S(2)}) collective-permute-start(bf16[128,1152]{1,0:T(8,128)(2,1)S(1)} %collective-permute-done.after_ref), channel_id=1, source_target_pairs={{0,32},{16,240},{32,64},{48,16},{64,96},{80,48},{96,128},{112,80},... | collective-permute-start | bytes 884744 | tf_op jit(solution)/shard_map/ppermute | solution.py:325
  25.1 0.4 collective-permute-done.3.refs_1_
  25.5 3.9 %collective-permute-start.5 = (bf16[128,1152]{1,0:T(8,128)(2,1)S(1)}, bf16[128,1152]{1,0:T(8,128)(2,1)S(1)}, u32[]{:S(2)}, u32[]{:S(2)}) collective-permute-start(bf16[128,1152]{1,0:T(8,128)(2,1)S(1)} %collective-permute-done.3.refs_1_), channel_id=1, source_target_pairs={{0,32},{16,240},{32,64},{48,16},{64,96},{80,48},{96,128},{112,80},... | collective-permute-start | bytes 884744 | tf_op jit(solution)/shard_map/ppermute | solution.py:322
  29.4 7.1 %collective-permute-done.4.refs_2_ = bf16[128,1152]{1,0:T(8,128)(2,1)S(1)} collective-permute-done((bf16[128,1152]{1,0:T(8,128)(2,1)S(1)}, bf16[128,1152]{1,0:T(8,128)(2,1)S(1)}, u32[]{:S(2)}, u32[]{:S(2)}) %collective-permute-start.4) | collective-permute-done | bytes 294944 | tf_op jit(solution)/shard_map/ppermute | solution.py:325
  36.5 1.9 %collective-permute-start.6 = (bf16[128,1152]{1,0:T(8,128)(2,1)S(1)}, bf16[128,1152]{1,0:T(8,128)(2,1)S(1)}, u32[]{:S(2)}, u32[]{:S(2)}) collective-permute-start(bf16[128,1152]{1,0:T(8,128)(2,1)S(1)} %collective-permute-done.4.refs_2_), channel_id=1, source_target_pairs={{0,32},{16,240},{32,64},{48,16},{64,96},{80,48},{96,128},{112,80},... | collective-permute-start | bytes 884744 | tf_op jit(solution)/shard_map/ppermute | solution.py:325
  38.4 1.2 collective-permute-done.5.refs_3_
  39.6 1.9 %collective-permute-start.7 = (bf16[128,1152]{1,0:T(8,128)(2,1)S(1)}, bf16[128,1152]{1,0:T(8,128)(2,1)S(1)}, u32[]{:S(2)}, u32[]{:S(2)}) collective-permute-start(bf16[128,1152]{1,0:T(8,128)(2,1)S(1)} %collective-permute-done.5.refs_3_), channel_id=1, source_target_pairs={{0,32},{16,240},{32,64},{48,16},{64,96},{80,48},{96,128},{112,80},... | collective-permute-start | bytes 884744 | tf_op jit(solution)/shard_map/ppermute | solution.py:322
  42.9 0.1 pad_maximum_fusion.1.sc_ref
  42.9 3.4 %collective-permute-done.6.refs_4_ = bf16[128,1152]{1,0:T(8,128)(2,1)S(1)} collective-permute-done((bf16[128,1152]{1,0:T(8,128)(2,1)S(1)}, bf16[128,1152]{1,0:T(8,128)(2,1)S(1)}, u32[]{:S(2)}, u32[]{:S(2)}) %collective-permute-start.6) | collective-permute-done | bytes 294944 | tf_op jit(solution)/shard_map/ppermute | solution.py:325
  46.3 1.9 %collective-permute-start.8 = (bf16[128,1152]{1,0:T(8,128)(2,1)S(1)}, bf16[128,1152]{1,0:T(8,128)(2,1)S(1)}, u32[]{:S(2)}, u32[]{:S(2)}) collective-permute-start(bf16[128,1152]{1,0:T(8,128)(2,1)S(1)} %collective-permute-done.6.refs_4_), channel_id=1, source_target_pairs={{0,32},{16,240},{32,64},{48,16},{64,96},{80,48},{96,128},{112,80},... | collective-permute-start | bytes 884744 | tf_op jit(solution)/shard_map/ppermute | solution.py:325
  48.2 1.2 collective-permute-done.7.refs_0_
  49.5 1.9 %collective-permute-start.9 = (bf16[128,1152]{1,0:T(8,128)(2,1)S(1)}, bf16[128,1152]{1,0:T(8,128)(2,1)S(1)}, u32[]{:S(2)}, u32[]{:S(2)}) collective-permute-start(bf16[128,1152]{1,0:T(8,128)(2,1)S(1)} %collective-permute-done.7.refs_0_), channel_id=1, source_target_pairs={{0,32},{16,240},{32,64},{48,16},{64,96},{80,48},{96,128},{112,80},... | collective-permute-start | bytes 884744 | tf_op jit(solution)/shard_map/ppermute | solution.py:322
  51.4 0.0 copy-start
  51.4 1.9 %copy-done = bf16[1408,1152]{1,0:T(8,128)(2,1)S(1)} copy-done((bf16[1408,1152]{1,0:T(8,128)(2,1)S(1)}, bf16[1408,1152]{1,0:T(8,128)(2,1)}, u32[]{:S(2)}) %copy-start) | copy-done | bytes 3244056
  53.3 2.4 %project.1 = (bf16[512,1152]{1,0:T(8,128)(2,1)S(1)}, f32[256,1152]{1,0:T(8,128)S(1)}, f32[256,128]{1,0:T(8,128)S(1)}) custom-call(bf16[256,1408]{1,0:T(8,128)(2,1)S(1)} %pad_maximum_fusion.n_own, bf16[256,1408]{1,0:T(8,128)(2,1)S(1)} %collective-permute-done.2.n_far, bf16[1408,1152]{1,0:T(8,128)(2,1)S(1)} %copy-done), custom_call_target="tpu_custom_call" | custom-call | flops 1660944384 | bytes 7176192 | tf_op jit(solution)/shard_map/project/pallas_call | solution.py:40
  55.7 3.6 %first_pairs.1 = (f32[512,1152]{1,0:T(8,128)S(1)}, f32[8,128]{1,0:T(8,128)S(1)}) custom-call(f32[2]{0:T(128)S(1)} %pad_maximum_fusion.1.sc_ref, bf16[512,1152]{1,0:T(8,128)(2,1)S(1)} %get-tuple-element.22.img_ref, bf16[128,1152]{1,0:T(8,128)(2,1)S(1)} %text_unit.1.refs_0_, bf16[128,1152]{1,0:T(8,128)(2,1)S(1)} %collective-permute-done.3.refs_1_, ...), custom_call_target="tpu_custom_call" | custom-call | flops 1509949440 | bytes 5017608 | tf_op jit(solution)/shard_map/first_pairs/pallas_call | solution.py:40
  59.3 2.5 %last_pairs.1 = (f32[256,1152]{1,0:T(8,128)S(1)}, bf16[272,1152]{1,0:T(8,128)(2,1)S(1)}, f32[1,128]{1,0:T(1,128)S(1)}) custom-call(f32[2]{0:T(128)S(1)} %pad_maximum_fusion.1.sc_ref, bf16[512,1152]{1,0:T(8,128)(2,1)S(1)} %get-tuple-element.22.img_ref, f32[512,1152]{1,0:T(8,128)S(1)} %get-tuple-element.23.grad_ref, f32[8,128]{1,0:T(8,128)S(1)} %get-tuple-element.24.part_ref, ...), custom_call_target="tpu_custom_call" | custom-call | flops 905969664 | bytes 6234632 | tf_op jit(solution)/shard_map/last_pairs/pallas_call | solution.py:40
  61.8 3.0 %collective-permute-start.10 = (bf16[272,1152]{1,0:T(8,128)(2,1)S(1)}, bf16[272,1152]{1,0:T(8,128)(2,1)S(1)}, u32[]{:S(2)}, u32[]{:S(2)}) collective-permute-start(bf16[272,1152]{1,0:T(8,128)(2,1)S(1)} %get-tuple-element.27), channel_id=1, source_target_pairs={{0,16},{16,0},{1,17},{17,1},{2,18},{18,2},{3,19},{19,3},{4,20},{20... | collective-permute-start | bytes 1880072 | tf_op jit(solution)/shard_map/ppermute | solution.py:370
  64.9 1.7 %collective-permute-done.10.got_ref = bf16[272,1152]{1,0:T(8,128)(2,1)S(1)} collective-permute-done((bf16[272,1152]{1,0:T(8,128)(2,1)S(1)}, bf16[272,1152]{1,0:T(8,128)(2,1)S(1)}, u32[]{:S(2)}, u32[]{:S(2)}) %collective-permute-start.10) | collective-permute-done | bytes 626720 | tf_op jit(solution)/shard_map/ppermute | solution.py:370
  66.5 1.0 add_cores.1
  67.5 3.4 %collective-permute-start.11 = (bf16[272,1152]{1,0:T(8,128)(2,1)}, bf16[272,1152]{1,0:T(8,128)(2,1)}, u32[]{:S(2)}, u32[]{:S(2)}) collective-permute-start(bf16[272,1152]{1,0:T(8,128)(2,1)} %get-tuple-element.30), channel_id=1, source_target_pairs={{0,256},{256,0},{1,257},{257,1},{2,258},{258,2},{3,259},{259,3},{4... | collective-permute-start | bytes 1880072 | tf_op jit(solution)/shard_map/ppermute | solution.py:390
  71.0 0.1 pad_add_fusion.where_ref
  71.0 1.1 copy-done.5
  72.2 1.4 pick.1.after_ref.pick_ref
  73.5 12.6 %collective-permute-done.11.got_ref = bf16[272,1152]{1,0:T(8,128)(2,1)} collective-permute-done((bf16[272,1152]{1,0:T(8,128)(2,1)}, bf16[272,1152]{1,0:T(8,128)(2,1)}, u32[]{:S(2)}, u32[]{:S(2)}) %collective-permute-start.11) | collective-permute-done | bytes 626720 | tf_op jit(solution)/shard_map/ppermute | solution.py:390
  86.1 1.6 %d_proj.1 = (bf16[256,1152]{1,0:T(8,128)(2,1)S(1)}, f32[1,128]{1,0:T(1,128)S(1)}) custom-call(f32[2]{0:T(128)S(1)} %pad_maximum_fusion.1.sc_ref, f32[256,1152]{1,0:T(8,128)S(1)} %get-tuple-element.28.sum_ref, f32[1,128]{1,0:T(1,128)S(1)} %get-tuple-element.29.after_ref.loss_ref, bf16[272,1152]{1,0:T(8,128)(2,1)} %collective-permute-done.11.got_ref, ...), custom_call_target="tpu_custom_call" | custom-call | bytes 4101128 | tf_op jit(solution)/shard_map/d_proj/pallas_call | solution.py:40
  87.8 1.9 %collective-permute-start.12 = (bf16[256,1152]{1,0:T(8,128)(2,1)S(1)}, bf16[256,1152]{1,0:T(8,128)(2,1)S(1)}, u32[]{:S(2)}, u32[]{:S(2)}) collective-permute-start(bf16[256,1152]{1,0:T(8,128)(2,1)S(1)} %get-tuple-element.33.dproj_ref.own_ref), channel_id=1, source_target_pairs={{0,16},{16,0},{1,17},{17,1},{2,18},{18,2},{3,19},{19,3},{4,20},{20... | collective-permute-start | bytes 1769480 | tf_op jit(solution)/shard_map/ppermute | solution.py:397
  89.7 2.2 %d_features.1 = (bf16[128,1408]{1,0:T(8,128)(2,1)}, f32[1,1408]{1,0:T(1,128)S(1)}) custom-call(bf16[256,1152]{1,0:T(8,128)(2,1)S(1)} %get-tuple-element.33.dproj_ref.own_ref, bf16[128,1408]{1,0:T(8,128)(2,1)S(1)} %bitcast.15, f32[1,1408]{1,0:T(1,128)S(1)} %reshape.23.gain_ref, bf16[256,1408]{1,0:T(8,128)(2,1)S(1)} %pad_maximum_fusion.n_own, ...), custom_call_target="tpu_custom_call" | custom-call | flops 830472192 | bytes 5286912 | tf_op jit(solution)/shard_map/d_features/pallas_call | solution.py:40
  91.9 1.8 %head.1 = bf16[384,1152]{1,0:T(8,128)(2,1)S(1)} custom-call(bf16[256,1152]{1,0:T(8,128)(2,1)S(1)} %get-tuple-element.33.dproj_ref.own_ref, bf16[256,1152]{1,0:T(8,128)(2,1)S(1)} %collective-permute-done.12.got_ref, bf16[384,512]{1,0:T(8,128)(2,1)S(1)} %pick.1.after_ref.pick_ref, bf16[256,1408]{1,0:T(8,128)(2,1)S(1)} %copy-done.5, ...), custom_call_target="tpu_custom_call" | custom-call | flops 1283457024 | bytes 6434304 | tf_op jit(solution)/shard_map/head/pallas_call | solution.py:40
  93.7 29.9 %all_to_all.33 = bf16[8,48,1152]{2,1,0:T(8,128)(2,1)S(1)} all-to-all(bf16[8,48,1152]{2,1,0:T(8,128)(2,1)S(1)} %bitcast.13), channel_id=1, replica_groups=mesh['x'=2,'z'=8,'c'=2,'hx'=2,'y'=8] {'z'}, dimensions={0} | all-to-all | bytes 1769472 | tf_op jit(solution)/shard_map/all_to_all | solution.py:423
  123.6 0.1 sum_z.1
  123.8 19.5 %all_to_all.34 = bf16[16,8,512]{2,1,0:T(8,128)(2,1)S(1)} all-to-all(bf16[16,8,512]{2,1,0:T(8,128)(2,1)S(1)} %bitcast.19), channel_id=1, replica_groups=mesh['x'=2,'z'=8,'c'=2,'hx'=2,'y'=8] {'hx','y'}, dimensions={0} | all-to-all | bytes 262144 | tf_op jit(solution)/shard_map/all_to_all | solution.py:425
  143.3 0.6 sum_groups.1
  143.9 13.1 %all_to_all.35 = bf16[16,8,512]{2,1,0:T(8,128)(2,1)S(1)} all-to-all(bf16[16,8,512]{2,1,0:T(8,128)(2,1)S(1)} %bitcast.18), channel_id=1, replica_groups=mesh['x'=2,'z'=8,'c'=2,'hx'=2,'y'=8] {'hx','y'}, dimensions={0} | all-to-all | bytes 262144 | tf_op jit(solution)/shard_map/all_to_all | solution.py:434
  157.0 0.7 unpack.1
  157.7 0.6 reduce
  (13 shorter events, 0.0 us)
Async XLA Ops:
  0.6 1.0 copy-start.6
  1.7 3.5 %collective-permute-start = (bf16[128,1152]{1,0:T(8,128)(2,1)S(1)}, bf16[128,1152]{1,0:T(8,128)(2,1)S(1)}, u32[]{:S(2)}, u32[]{:S(2)}) collective-permute-start(bf16[128,1152]{1,0:T(8,128)(2,1)S(1)} %text_unit.1.refs_0_), channel_id=1, source_target_pairs={{0,16},{16,0},{1,17},{17,1},{2,18},{18,2},{3,19},{19,3},{4,20},{20... | collective-permute-start | bytes 884744 | tf_op jit(solution)/shard_map/ppermute | solution.py:319
  5.2 1.0 copy-start.2
  6.5 12.3 %collective-permute-start.1 = (bf16[128,1408]{1,0:T(8,128)(2,1)S(1)}, bf16[128,1408]{1,0:T(8,128)(2,1)S(1)}, u32[]{:S(2)}, u32[]{:S(2)}) collective-permute-start(bf16[128,1408]{1,0:T(8,128)(2,1)S(1)} %normed.1), channel_id=1, source_target_pairs={{0,256},{256,0},{1,257},{257,1},{2,258},{258,2},{3,259},{259,3},{4... | collective-permute-start | bytes 1081352 | tf_op jit(solution)/shard_map/ppermute | solution.py:329
  9.9 15.6 %collective-permute-start.3 = (bf16[128,1152]{1,0:T(8,128)(2,1)S(1)}, bf16[128,1152]{1,0:T(8,128)(2,1)S(1)}, u32[]{:S(2)}, u32[]{:S(2)}) collective-permute-start(bf16[128,1152]{1,0:T(8,128)(2,1)S(1)} %text_unit.1.refs_0_), channel_id=1, source_target_pairs={{0,32},{16,240},{32,64},{48,16},{64,96},{80,48},{96,128},{112,80},... | collective-permute-start | bytes 884744 | tf_op jit(solution)/shard_map/ppermute | solution.py:322
  18.9 32.5 %collective-permute-start.2 = (bf16[256,1408]{1,0:T(8,128)(2,1)S(1)}, bf16[256,1408]{1,0:T(8,128)(2,1)S(1)}, u32[]{:S(2)}, u32[]{:S(2)}) collective-permute-start(bf16[256,1408]{1,0:T(8,128)(2,1)S(1)} %pad_maximum_fusion.n_own), channel_id=1, source_target_pairs={{0,16},{16,0},{1,17},{17,1},{2,18},{18,2},{3,19},{19,3},{4,20},{20... | collective-permute-start | bytes 2162696 | tf_op jit(solution)/shard_map/ppermute | solution.py:330
  22.4 14.1 %collective-permute-start.4 = (bf16[128,1152]{1,0:T(8,128)(2,1)S(1)}, bf16[128,1152]{1,0:T(8,128)(2,1)S(1)}, u32[]{:S(2)}, u32[]{:S(2)}) collective-permute-start(bf16[128,1152]{1,0:T(8,128)(2,1)S(1)} %collective-permute-done.after_ref), channel_id=1, source_target_pairs={{0,32},{16,240},{32,64},{48,16},{64,96},{80,48},{96,128},{112,80},... | collective-permute-start | bytes 884744 | tf_op jit(solution)/shard_map/ppermute | solution.py:325
  25.5 14.1 %collective-permute-start.5 = (bf16[128,1152]{1,0:T(8,128)(2,1)S(1)}, bf16[128,1152]{1,0:T(8,128)(2,1)S(1)}, u32[]{:S(2)}, u32[]{:S(2)}) collective-permute-start(bf16[128,1152]{1,0:T(8,128)(2,1)S(1)} %collective-permute-done.3.refs_1_), channel_id=1, source_target_pairs={{0,32},{16,240},{32,64},{48,16},{64,96},{80,48},{96,128},{112,80},... | collective-permute-start | bytes 884744 | tf_op jit(solution)/shard_map/ppermute | solution.py:322
  36.5 9.8 %collective-permute-start.6 = (bf16[128,1152]{1,0:T(8,128)(2,1)S(1)}, bf16[128,1152]{1,0:T(8,128)(2,1)S(1)}, u32[]{:S(2)}, u32[]{:S(2)}) collective-permute-start(bf16[128,1152]{1,0:T(8,128)(2,1)S(1)} %collective-permute-done.4.refs_2_), channel_id=1, source_target_pairs={{0,32},{16,240},{32,64},{48,16},{64,96},{80,48},{96,128},{112,80},... | collective-permute-start | bytes 884744 | tf_op jit(solution)/shard_map/ppermute | solution.py:325
  39.6 9.8 %collective-permute-start.7 = (bf16[128,1152]{1,0:T(8,128)(2,1)S(1)}, bf16[128,1152]{1,0:T(8,128)(2,1)S(1)}, u32[]{:S(2)}, u32[]{:S(2)}) collective-permute-start(bf16[128,1152]{1,0:T(8,128)(2,1)S(1)} %collective-permute-done.5.refs_3_), channel_id=1, source_target_pairs={{0,32},{16,240},{32,64},{48,16},{64,96},{80,48},{96,128},{112,80},... | collective-permute-start | bytes 884744 | tf_op jit(solution)/shard_map/ppermute | solution.py:322
  46.3 13.0 %collective-permute-start.8 = (bf16[128,1152]{1,0:T(8,128)(2,1)S(1)}, bf16[128,1152]{1,0:T(8,128)(2,1)S(1)}, u32[]{:S(2)}, u32[]{:S(2)}) collective-permute-start(bf16[128,1152]{1,0:T(8,128)(2,1)S(1)} %collective-permute-done.6.refs_4_), channel_id=1, source_target_pairs={{0,32},{16,240},{32,64},{48,16},{64,96},{80,48},{96,128},{112,80},... | collective-permute-start | bytes 884744 | tf_op jit(solution)/shard_map/ppermute | solution.py:325
  49.5 9.8 %collective-permute-start.9 = (bf16[128,1152]{1,0:T(8,128)(2,1)S(1)}, bf16[128,1152]{1,0:T(8,128)(2,1)S(1)}, u32[]{:S(2)}, u32[]{:S(2)}) collective-permute-start(bf16[128,1152]{1,0:T(8,128)(2,1)S(1)} %collective-permute-done.7.refs_0_), channel_id=1, source_target_pairs={{0,32},{16,240},{32,64},{48,16},{64,96},{80,48},{96,128},{112,80},... | collective-permute-start | bytes 884744 | tf_op jit(solution)/shard_map/ppermute | solution.py:322
  51.4 1.9 %copy-start = (bf16[1408,1152]{1,0:T(8,128)(2,1)S(1)}, bf16[1408,1152]{1,0:T(8,128)(2,1)}, u32[]{:S(2)}) copy-start(bf16[1408,1152]{1,0:T(8,128)(2,1)} %w_ref.5) | copy-start | bytes 9732100
  53.3 2.4 %copy-start.4 = (bf16[256,1408]{1,0:T(8,128)(2,1)}, bf16[256,1408]{1,0:T(8,128)(2,1)S(1)}, u32[]{:S(2)}) copy-start(bf16[256,1408]{1,0:T(8,128)(2,1)S(1)} %collective-permute-done.2.n_far) | copy-start | bytes 2162692
  61.8 4.7 %collective-permute-start.10 = (bf16[272,1152]{1,0:T(8,128)(2,1)S(1)}, bf16[272,1152]{1,0:T(8,128)(2,1)S(1)}, u32[]{:S(2)}, u32[]{:S(2)}) collective-permute-start(bf16[272,1152]{1,0:T(8,128)(2,1)S(1)} %get-tuple-element.27), channel_id=1, source_target_pairs={{0,16},{16,0},{1,17},{17,1},{2,18},{18,2},{3,19},{19,3},{4,20},{20... | collective-permute-start | bytes 1880072 | tf_op jit(solution)/shard_map/ppermute | solution.py:370
  67.5 18.6 %collective-permute-start.11 = (bf16[272,1152]{1,0:T(8,128)(2,1)}, bf16[272,1152]{1,0:T(8,128)(2,1)}, u32[]{:S(2)}, u32[]{:S(2)}) collective-permute-start(bf16[272,1152]{1,0:T(8,128)(2,1)} %get-tuple-element.30), channel_id=1, source_target_pairs={{0,256},{256,0},{1,257},{257,1},{2,258},{258,2},{3,259},{259,3},{4... | collective-permute-start | bytes 1880072 | tf_op jit(solution)/shard_map/ppermute | solution.py:390
  71.0 1.1 copy-start.5
  72.2 17.6 %copy-start.3 = (bf16[1,128,1408]{2,1,0:T(8,128)(2,1)S(1)}, bf16[1,128,1408]{2,1,0:T(8,128)(2,1)}, u32[]{:S(2)}) copy-start(bf16[1,128,1408]{2,1,0:T(8,128)(2,1)} %param.6) | copy-start | bytes 1081348
  86.1 3.6 %copy-start.1 = (bf16[1408,1152]{1,0:T(8,128)(2,1)S(1)}, bf16[1408,1152]{1,0:T(8,128)(2,1)}, u32[]{:S(2)}) copy-start(bf16[1408,1152]{1,0:T(8,128)(2,1)} %w_ref.5) | copy-start | bytes 9732100
  87.8 4.1 %collective-permute-start.12 = (bf16[256,1152]{1,0:T(8,128)(2,1)S(1)}, bf16[256,1152]{1,0:T(8,128)(2,1)S(1)}, u32[]{:S(2)}, u32[]{:S(2)}) collective-permute-start(bf16[256,1152]{1,0:T(8,128)(2,1)S(1)} %get-tuple-element.33.dproj_ref.own_ref), channel_id=1, source_target_pairs={{0,16},{16,0},{1,17},{17,1},{2,18},{18,2},{3,19},{19,3},{4,20},{20... | collective-permute-start | bytes 1769480 | tf_op jit(solution)/shard_map/ppermute | solution.py:397

commit v3 on v1

v3 whole, which is shorter than its diff:
```python
import functools

import jax
import jax.numpy as jnp
from jax import lax
from jax.experimental import pallas as pl
from jax.experimental.pallas import tpu as pltpu
from jax.sharding import Mesh, PartitionSpec as P

EPSILON = 1e-06
ROWS = 128
W = 1408
E = 1152
SHARE = 44
F32 = jnp.float32
BF16 = jnp.bfloat16

X, Z, C, HX, Y = "x", "z", "c", "hx", "y"
NZ = 8
N_GROUP = 16
PIECE = 512
BLOCK = 128
EXTRA = 16
GAIN_AT = 112

SWAP = [(0, 1), (1, 0)]
HOP = [
    (z * 2 + c, ((z + (1 if c == 0 else -1)) % NZ) * 2 + c) for z in range(NZ) for c in range(2)
]

VMEM = pl.BlockSpec(memory_space=pltpu.VMEM)
SMEM = pl.BlockSpec(memory_space=pltpu.SMEM)


def call(kernel, out_shape, *operands, specs=None, outs=None, scratch=(), flops=0, mib=48, name=None):
    leaves = jax.tree.leaves(out_shape)
    moved = sum(o.size * o.dtype.itemsize for o in (*operands, *leaves))
    return pl.pallas_call(
        kernel,
        out_shape=out_shape,
        in_specs=specs or [VMEM] * len(operands),
        out_specs=outs or jax.tree.map(lambda _: VMEM, out_shape),
        scratch_shapes=list(scratch),
        name=name,
        cost_estimate=pl.CostEstimate(flops=flops, bytes_accessed=moved, transcendentals=0),
        compiler_params=pltpu.CompilerParams(vmem_limit_bytes=mib << 20),
    )(*operands)


def out(shape, dtype):
    return jax.ShapeDtypeStruct(shape, dtype)


def moments(values):
    mean = jnp.mean(values, axis=1, keepdims=True)
    centred = values - mean
    scale = lax.rsqrt(jnp.mean(centred * centred, axis=1, keepdims=True) + EPSILON)
    return centred * scale, scale


def prepare_kernel(cap_ref, x_ref, gain_ref, text_ref, both_ref):
    values = cap_ref[...].astype(F32)
    scale = lax.rsqrt(jnp.sum(values * values, axis=1, keepdims=True) + EPSILON)
    text = (values * scale).astype(BF16)
    text_ref[...] = text
    both_ref[:, :E] = text
    x_hat, _ = moments(x_ref[...].astype(F32))
    both_ref[:, E:] = (x_hat * gain_ref[...].reshape(1, W)).astype(BF16)


def unpack_swap_kernel(own_ref, got_ref, text_ref, normed_ref):
    text_ref[...] = got_ref[:, :E]
    normed_ref[:ROWS, :] = own_ref[:, E:]
    normed_ref[ROWS:, :] = got_ref[:, E:]


def collect_kernel(*refs):
    for i, piece in enumerate(refs[:-1]):
        refs[-1][pl.ds(i * ROWS, ROWS), :] = piece[...]


def project_kernel(n_here, n_there, w_ref, after_ref, img_ref, unit_ref, pnorm_ref, rows_ref):
    del after_ref
    for i, part in enumerate((n_here, n_there)):
        rows_ref[i * ROWS : (i + 1) * ROWS, :] = part[:ROWS, :]
        rows_ref[(i + 2) * ROWS : (i + 3) * ROWS, :] = part[ROWS:, :]
    proj = jnp.dot(rows_ref[...], w_ref[...], preferred_element_type=F32)
    pnorm = lax.rsqrt(jnp.sum(proj * proj, axis=1, keepdims=True) + EPSILON)
    unit = proj * pnorm
    img_ref[...] = unit.astype(BF16)
    unit_ref[...] = unit[: 2 * ROWS]
    pnorm_ref[...] = jnp.broadcast_to(pnorm[: 2 * ROWS], (2 * ROWS, 128))


def pick_kernel(after_ref, rows_ref, pick_ref):
    del after_ref
    row = lax.broadcasted_iota(jnp.int32, (NZ * 48, 1), 0)
    block = row // 48
    inside = row - block * 48
    device = lax.axis_index(X) * 16 + lax.axis_index(C)
    source = jnp.where(inside < SHARE, SHARE * (device + 2 * block) + inside, -1)
    column = lax.broadcasted_iota(jnp.int32, (NZ * 48, W), 1)
    select = (column == source).astype(F32).astype(BF16)
    picked = lax.dot_general(
        select, rows_ref[...], (((1,), (1,)), ((), ())), preferred_element_type=F32
    )
    pick_ref[...] = picked.astype(BF16)


def fold_product(grown):
    rows = grown.shape[0]
    while rows > 8:
        rows //= 2
        one, two = grown[:rows], grown[rows:]
        grown = one + two + one * two
    return grown


def fold_sum(values):
    rows = values.shape[0]
    while rows > 8:
        rows //= 2
        values = values[:rows] + values[rows:]
    return values


def log1p(value):
    up = 1.0 + value
    gap = up - 1.0
    return jnp.where(gap == 0.0, value, jnp.log(up) * (value / jnp.where(gap == 0.0, 1.0, gap)))


def pair_terms(scale_ref, bias_ref, img_ref, texts, text, slope):
    text[: 7 * ROWS, :] = texts[0][...]
    text[7 * ROWS :, :] = texts[1][...]
    scale, bias = scale_ref[0], bias_ref[0]
    total = jnp.zeros((8, 128), F32)
    span = 2
    for start in range(0, 8, span):
        sims = lax.dot_general(
            img_ref[...],
            text[pl.ds(start * ROWS, span * ROWS), :],
            (((1,), (1,)), ((), ())),
            preferred_element_type=F32,
        )
        for half in range(span):
            chunk = start + half
            turned = scale * sims[:, half * ROWS : (half + 1) * ROWS] + bias
            if chunk == 0:
                shape = (4 * ROWS, ROWS)
                match = lax.broadcasted_iota(jnp.int32, shape, 0) == lax.broadcasted_iota(
                    jnp.int32, shape, 1
                )
                turned = jnp.where(match, -turned, turned)
            small = jnp.exp(-jnp.abs(turned))
            below = 1.0 + small
            inverse = pltpu.reciprocal(below, approx=True)
            inverse = inverse * (2.0 - below * inverse)
            sig = jnp.where(turned >= 0.0, 1.0, small) * inverse
            if chunk == 0:
                sig = jnp.where(match, -sig, sig)
            slope[:, chunk * ROWS : (chunk + 1) * ROWS] = sig.astype(BF16)
            total = total + fold_sum(jnp.maximum(turned, 0.0)) + log1p(fold_product(small))
    return total


def pairs_kernel(scale_ref, bias_ref, img_ref, *refs):
    texts, (keep_ref, send_ref, loss_ref, text, slope) = refs[:2], refs[2:]
    total = pair_terms(scale_ref, bias_ref, img_ref, texts, text, slope)
    loss = jnp.broadcast_to(jnp.sum(total, keepdims=True), (1, 128))
    loss_ref[...] = loss
    grad = jnp.dot(slope[...], text[...], preferred_element_type=F32)
    keep_ref[...] = grad[: 2 * ROWS]
    send_ref[: 2 * ROWS, :] = grad[2 * ROWS :].astype(BF16)
    send_ref[2 * ROWS :, :] = loss_rows(loss)


def loss_rows(loss):
    high = loss.astype(BF16).astype(F32)
    row = jnp.concatenate([high, loss - high, jnp.zeros((1, E - 256), F32)], axis=1)
    return jnp.broadcast_to(row, (EXTRA, E)).astype(BF16)


def got_loss(got_ref):
    row = got_ref[2 * ROWS :, :256].astype(F32)[:1]
    return row[:, :128] + row[:, 128:]


def add_kernel(keep_ref, loss_ref, got_ref, send_ref):
    total = keep_ref[...] + got_ref[: 2 * ROWS, :].astype(F32)
    send_ref[: 2 * ROWS, :] = total.astype(BF16)
    loss = loss_ref[...] + got_loss(got_ref)
    send_ref[2 * ROWS :, :] = loss_rows(loss)


def dproj_kernel(
    scale_ref, keep_ref, loss_ref, core_ref, got_ref, unit_ref, pnorm_ref, after_ref, dproj_ref, loss_out
):
    del after_ref
    loss_out[...] = loss_ref[...] + got_loss(core_ref) + got_loss(got_ref)
    for i in range(2):
        rows, other = pl.ds(i * ROWS, ROWS), pl.ds((1 - i) * ROWS, ROWS)
        total = keep_ref[rows, :] + core_ref[rows, :].astype(F32)
        grad = scale_ref[0] * (total + got_ref[other, :].astype(F32))
        unit = unit_ref[rows, :]
        inner = jnp.sum(unit * grad, axis=1, keepdims=True)
        dproj_ref[rows, :] = ((grad - unit * inner) * pnorm_ref[rows, 0:1]).astype(BF16)


def back(dproj, w_ref):
    return lax.dot_general(dproj, w_ref[...], (((1,), (1,)), ((), ())), preferred_element_type=F32)


def features_kernel(dproj_ref, x_ref, gain_ref, rows_ref, w_ref, feat_ref, part_ref):
    d_normed = back(dproj_ref[...], w_ref)
    own = d_normed[:ROWS]
    part_ref[...] = jnp.sum(rows_ref[: 2 * ROWS, :].astype(F32) * d_normed, axis=0, keepdims=True)
    x_hat, scale = moments(x_ref[...].astype(F32))
    d_hat = own * gain_ref[...].reshape(1, W)
    feat = scale * (
        d_hat
        - jnp.mean(d_hat, axis=1, keepdims=True)
        - x_hat * jnp.mean(d_hat * x_hat, axis=1, keepdims=True)
    )
    feat_ref[...] = feat.astype(BF16)


def head_kernel(own_ref, got_ref, pick_ref, rows_ref, w_ref, gain_ref, part_ref, loss_ref, out_ref):
    head = jnp.dot(pick_ref[:, : 2 * ROWS], own_ref[...], preferred_element_type=F32) + jnp.dot(
        pick_ref[:, 2 * ROWS :], got_ref[...], preferred_element_type=F32
    )
    head = head.astype(BF16)
    d_normed = back(got_ref[...], w_ref)
    gain = part_ref[...] + jnp.sum(rows_ref[2 * ROWS :, :].astype(F32) * d_normed, axis=0, keepdims=True)
    packed = split_rows(gain / gain_ref[...].reshape(1, W), loss_ref[...])
    for k in range(NZ):
        block = head[48 * k : 48 * (k + 1)]
        at = BLOCK * k
        out_ref[at : at + 48, :] = block[:, :512]
        out_ref[at + 48 : at + 96, :] = block[:, 512:1024]
        for i in range(3):
            out_ref[at + 96 : at + 112, 128 * i : 128 * (i + 1)] = block[16 * i : 16 * (i + 1), 1024:]
        out_ref[at + 96 : at + 112, 384:] = jnp.zeros((16, 128), BF16)
        out_ref[at + GAIN_AT : at + BLOCK, :] = packed


def split_rows(gain, loss):
    rows = [gain[:, :512], gain[:, 512:1024], jnp.concatenate([gain[:, 1024:], loss], axis=1)]
    high = [r.astype(BF16).astype(F32) for r in rows]
    low = [r - h for r, h in zip(rows, high)]
    index = lax.broadcasted_iota(jnp.int32, (16, PIECE), 0)
    packed = jnp.zeros((16, PIECE), F32)
    for i, r in enumerate(high + low):
        packed = jnp.where(index == i, r, packed)
    return packed.astype(BF16)


def reduce_kernel(got_ref, out_ref):
    total = got_ref[...].astype(F32).reshape(N_GROUP * NZ, 8, PIECE).sum(axis=0)
    rest = jnp.concatenate([total[3:], total[:3]], axis=0)
    index = lax.broadcasted_iota(jnp.int32, (8, PIECE), 0)
    whole = total + rest
    high = whole.astype(BF16).astype(F32)
    low = whole - high
    moved = jnp.concatenate([low[5:], low[:5]], axis=0)
    split = jnp.where(index < 3, high, jnp.where(index < 6, moved, 0.0))
    group = lax.axis_index(HX) * 8 + lax.axis_index(Y)
    piece = jnp.where(group == GAIN_AT // 8, split, total)
    copies = jnp.broadcast_to(piece[None], (N_GROUP, 8, PIECE)).reshape(BLOCK, PIECE)
    out_ref[...] = copies.astype(BF16)


def unpack_kernel(got_ref, head_ref, gain_ref, loss_ref):
    block = got_ref[...].astype(F32)
    head_ref[:, :512] = block[:SHARE]
    head_ref[:, 512:1024] = block[48 : 48 + SHARE]
    tail = block[96:112]
    head_ref[0:16, 1024:] = tail[:, 0:128]
    head_ref[16:32, 1024:] = tail[:, 128:256]
    head_ref[32:SHARE, 1024:] = tail[: SHARE - 32, 256:384]
    rows = block[GAIN_AT : GAIN_AT + 3] + block[GAIN_AT + 3 : GAIN_AT + 6]
    gain_ref[...] = jnp.concatenate([rows[0], rows[1], rows[2, :384]])
    loss_ref[0] = jnp.max(rows[2:3, 384:]) * (1.0 / (N_GROUP * NZ * 4 * ROWS))


def per_device(pooled, captions, gain, w, scale, bias):
    x = pooled[0]
    across = functools.partial(lax.ppermute, axis_name=X, perm=SWAP)
    between = functools.partial(lax.ppermute, axis_name=C, perm=SWAP)
    hop = functools.partial(lax.ppermute, axis_name=(Z, C), perm=HOP)

    text, both = call(
        prepare_kernel,
        (out((ROWS, E), BF16), out((ROWS, E + W), BF16)),
        captions[0],
        x,
        gain,
        name="prepare",
    )
    swapped, n_here = call(
        unpack_swap_kernel,
        (out((ROWS, E), BF16), out((2 * ROWS, W), BF16)),
        both,
        between(both),
        name="unpack_swap",
    )
    texts = [text]
    one, two = text, swapped
    for step in range(4):
        one = hop(one)
        if step == 0:
            one, swapped = lax.optimization_barrier((one, swapped))
        texts.append(one)
        if step < 3:
            two = hop(two)
            texts.append(two)

    img, unit, pnorm, rows = call(
        project_kernel,
        (
            out((4 * ROWS, E), BF16),
            out((2 * ROWS, E), F32),
            out((2 * ROWS, 128), F32),
            out((4 * ROWS, W), BF16),
        ),
        n_here,
        across(n_here),
        w,
        texts[5],
        flops=2 * 4 * ROWS * W * E,
        name="project",
    )
    early = call(
        collect_kernel,
        out((7 * ROWS, E), BF16),
        *texts[:7],
        flops=4 * 4 * ROWS * 7 * ROWS * E,
        name="collect",
    )
    keep, send, loss = call(
        pairs_kernel,
        (out((2 * ROWS, E), F32), out((2 * ROWS + EXTRA, E), BF16), out((1, 128), F32)),
        scale,
        bias,
        img,
        early,
        texts[7],
        specs=[SMEM] * 2 + [VMEM] * 3,
        scratch=[pltpu.VMEM((8 * ROWS, E), BF16), pltpu.VMEM((4 * ROWS, 8 * ROWS), BF16)],
        flops=4 * 4 * ROWS * 8 * ROWS * E,
        name="pairs",
    )
    core = between(send)
    send = call(
        add_kernel,
        out((2 * ROWS + EXTRA, E), BF16),
        keep,
        loss,
        core,
        mib=8,
        name="add_cores",
    )
    pick = call(
        pick_kernel,
        out((NZ * 48, 4 * ROWS), BF16),
        send,
        rows,
        flops=2 * 4 * ROWS * W * NZ * 48,
        mib=12,
        name="pick",
    )
    dproj, loss = call(
        dproj_kernel,
        (out((2 * ROWS, E), BF16), out((1, 128), F32)),
        scale,
        keep,
        loss,
        core,
        across(send),
        unit,
        pnorm,
        pick,
        specs=[SMEM] + [VMEM] * 7,
        mib=8,
        name="d_proj",
    )
    dproj_far = between(dproj)
    d_features, gain_part = call(
        features_kernel,
        (out((ROWS, W), BF16), out((1, W), F32)),
        dproj,
        x,
        gain,
        rows,
        w,
        flops=4 * ROWS * W * E,
        mib=16,
        name="d_features",
    )
    packed = call(
        head_kernel,
        out((NZ * BLOCK, PIECE), BF16),
        dproj,
        dproj_far,
        pick,
        rows,
        w,
        gain,
        gain_part,
        loss,
        flops=4 * ROWS * W * E + 8 * ROWS * NZ * 48 * E,
        mib=24,
        name="head",
    )
    packed = lax.all_to_all(packed, (Z, HX, Y), 0, 0, tiled=True)
    piece = call(
        reduce_kernel,
        out((BLOCK, PIECE), BF16),
        packed,
        name="reduce",
    )
    block = lax.all_to_all(piece, (HX, Y), 0, 0, tiled=True)
    head, d_gain, loss = call(
        unpack_kernel,
        (out((SHARE, E), F32), out((W,), F32), out((1,), F32)),
        block,
        outs=(VMEM, VMEM, SMEM),
        name="unpack",
    )
    return loss.reshape(()), d_features[None], d_gain, head


def solution(mesh):
    fine = Mesh(mesh.devices.reshape(2, NZ, 2, 2, 8), (X, Z, C, HX, Y))
    rows = P((HX, Y), (X, Z, C), None)
    return jax.shard_map(
        per_device,
        mesh=fine,
        in_specs=(rows, rows, P(), P(), P(), P()),
        out_specs=(P(), rows, P(), P((X, Z, C), None)),
        check_vma=False,
    )
```

time: 152 us -> 146 us (0.961)
  starting transfers between devices: 40 us -> 32 us
  waiting for transfers between devices: 25.6 us -> 32.3 us
  Pallas kernels: 18.8 us -> 15.2 us
    ppermute x4, waiting for transfers between devices: 3.24 us -> 14 us  [per_device(): one = hop(one)]
    ppermute x5 -> x3, starting transfers between devices: 13.3 us -> 7.24 us  [the longest x1 3.4 us: per_device(): across(n_here)]
    pallas_call x10 -> x12, Pallas kernels: 18.8 us -> 15.2 us  [call(): pl.pallas_call(kernel, out_shape=out_shape, in_specs=specs or [VMEM] * le...]
    ppermute x4, starting transfers between devices: 13.4 us -> 10 us  [per_device(): one = hop(one)]
    ppermute x3, waiting for transfers between devices: 4.7 us -> 2.49 us  [per_device(): two = hop(two)]
    ppermute x1, waiting for transfers between devices: 15.6 us -> 13.8 us  [per_device(): across(send)]
  transfers between devices with their start and end apart: 14 -> 12, of which waited for: 6 -> 8; matrix products, arithmetic and copies ran while one was open for 1% -> 0% of each run, Pallas kernels for 5% -> 5%
where the time goes in v3:
time: 146 us; the launch traced here: 145 us
  blocking collectives  61.2 us (42%)
  waiting for transfers between devices  32.3 us (22%)
  starting transfers between devices  32 us (22%)
  Pallas kernels  15.2 us (10%)
  local copies, waits for them, and re-layouts  2.65 us (2%)
  between operations  2.14 us (1%)
    all_to_all x1, blocking collectives, per_device(): packed = lax.all_to_all(packed, (Z, HX, Y), 0, 0, tiled=True)  46.3 us
    pallas_call x12, Pallas kernels, call(): pl.pallas_call(kernel, out_shape=out_shape, in_specs=specs or [VMEM] * le...  15.2 us
    all_to_all x1, blocking collectives, per_device(): block = lax.all_to_all(piece, (HX, Y), 0, 0, tiled=True)  14.9 us
    ppermute x4, waiting for transfers between devices, per_device(): one = hop(one)  14 us
    ppermute x1, waiting for transfers between devices, per_device(): across(send)  13.8 us
    ppermute x4, starting transfers between devices, per_device(): one = hop(one)  10 us
    ppermute x3, starting transfers between devices, per_device(): two = hop(two)  9.26 us
    ppermute x1, starting transfers between devices, per_device(): across(n_here)  3.4 us
  transfers between devices with their start and end apart: 12, of which 8 were waited for; matrix products, arithmetic and copies ran while one was open for 0% of the time, Pallas kernels for 5%

profile of v3, /device:TPU:8, one launch (start us, length us, event | category | flops | bytes accessed | tf_op | source)
XLA Modules:
  0.0 145.5 jit_solution(7379417807531784599)
XLA Ops:
  0.6 0.0 copy-start.1
  0.6 1.0 copy-done.1
  1.6 0.0 copy-start.3
  1.6 1.0 copy-done.3
  2.6 0.0 copy-start.4
  2.6 0.7 copy-done.4
  3.3 0.3 prepare.1
  3.6 1.9 %collective-permute-start = (bf16[128,2560]{1,0:T(8,128)(2,1)S(1)}, bf16[128,2560]{1,0:T(8,128)(2,1)S(1)}, u32[]{:S(2)}, u32[]{:S(2)}) collective-permute-start(bf16[128,2560]{1,0:T(8,128)(2,1)S(1)} %get-tuple-element.23.own_ref), channel_id=1, source_target_pairs={{0,16},{16,0},{1,17},{17,1},{2,18},{18,2},{3,19},{19,3},{4,20},{20... | collective-permute-start | bytes 1966088 | tf_op jit(solution)/shard_map/ppermute | solution.py:304
  5.5 4.3 %collective-permute-start.2 = (bf16[128,1152]{1,0:T(8,128)(2,1)S(1)}, bf16[128,1152]{1,0:T(8,128)(2,1)S(1)}, u32[]{:S(2)}, u32[]{:S(2)}) collective-permute-start(bf16[128,1152]{1,0:T(8,128)(2,1)S(1)} %get-tuple-element.25.refs_0_), channel_id=1, source_target_pairs={{0,32},{16,240},{32,64},{48,16},{64,96},{80,48},{96,128},{112,80},... | collective-permute-start | bytes 884744 | tf_op jit(solution)/shard_map/ppermute | solution.py:310
  9.8 0.0 collective-permute-done.got_ref
  9.8 0.1 unpack_swap.1
  9.9 4.3 %collective-permute-start.5 = (bf16[128,1152]{1,0:T(8,128)(2,1)S(1)}, bf16[128,1152]{1,0:T(8,128)(2,1)S(1)}, u32[]{:S(2)}, u32[]{:S(2)}) collective-permute-start(bf16[128,1152]{1,0:T(8,128)(2,1)S(1)} %get-tuple-element.26), channel_id=1, source_target_pairs={{0,32},{16,240},{32,64},{48,16},{64,96},{80,48},{96,128},{112,80},... | collective-permute-start | bytes 884744 | tf_op jit(solution)/shard_map/ppermute | solution.py:315
  14.2 3.4 %collective-permute-start.1 = (bf16[256,1408]{1,0:T(8,128)(2,1)S(1)}, bf16[256,1408]{1,0:T(8,128)(2,1)S(1)}, u32[]{:S(2)}, u32[]{:S(2)}) collective-permute-start(bf16[256,1408]{1,0:T(8,128)(2,1)S(1)} %get-tuple-element.24.n_here), channel_id=1, source_target_pairs={{0,256},{256,0},{1,257},{257,1},{2,258},{258,2},{3,259},{259,3},{4... | collective-permute-start | bytes 2162696 | tf_op jit(solution)/shard_map/ppermute | solution.py:327
  17.6 3.6 %collective-permute-done.2.refs_1_ = bf16[128,1152]{1,0:T(8,128)(2,1)S(1)} collective-permute-done((bf16[128,1152]{1,0:T(8,128)(2,1)S(1)}, bf16[128,1152]{1,0:T(8,128)(2,1)S(1)}, u32[]{:S(2)}, u32[]{:S(2)}) %collective-permute-start.2) | collective-permute-done | bytes 294944 | tf_op jit(solution)/shard_map/ppermute | solution.py:310
  21.2 1.9 %collective-permute-start.3 = (bf16[128,1152]{1,0:T(8,128)(2,1)S(1)}, bf16[128,1152]{1,0:T(8,128)(2,1)S(1)}, u32[]{:S(2)}, u32[]{:S(2)}) collective-permute-start(bf16[128,1152]{1,0:T(8,128)(2,1)S(1)} %collective-permute-done.2.refs_1_), channel_id=1, source_target_pairs={{0,32},{16,240},{32,64},{48,16},{64,96},{80,48},{96,128},{112,80},... | collective-permute-start | bytes 884744 | tf_op jit(solution)/shard_map/ppermute | solution.py:310
  23.1 1.2 collective-permute-done.5.refs_2_
  24.3 3.1 %collective-permute-start.6 = (bf16[128,1152]{1,0:T(8,128)(2,1)S(1)}, bf16[128,1152]{1,0:T(8,128)(2,1)S(1)}, u32[]{:S(2)}, u32[]{:S(2)}) collective-permute-start(bf16[128,1152]{1,0:T(8,128)(2,1)S(1)} %collective-permute-done.5.refs_2_), channel_id=1, source_target_pairs={{0,32},{16,240},{32,64},{48,16},{64,96},{80,48},{96,128},{112,80},... | collective-permute-start | bytes 884744 | tf_op jit(solution)/shard_map/ppermute | solution.py:315
  27.4 3.6 %collective-permute-done.3.refs_3_ = bf16[128,1152]{1,0:T(8,128)(2,1)S(1)} collective-permute-done((bf16[128,1152]{1,0:T(8,128)(2,1)S(1)}, bf16[128,1152]{1,0:T(8,128)(2,1)S(1)}, u32[]{:S(2)}, u32[]{:S(2)}) %collective-permute-start.3) | collective-permute-done | bytes 294944 | tf_op jit(solution)/shard_map/ppermute | solution.py:310
  31.0 1.9 %collective-permute-start.4 = (bf16[128,1152]{1,0:T(8,128)(2,1)S(1)}, bf16[128,1152]{1,0:T(8,128)(2,1)S(1)}, u32[]{:S(2)}, u32[]{:S(2)}) collective-permute-start(bf16[128,1152]{1,0:T(8,128)(2,1)S(1)} %collective-permute-done.3.refs_3_), channel_id=1, source_target_pairs={{0,32},{16,240},{32,64},{48,16},{64,96},{80,48},{96,128},{112,80},... | collective-permute-start | bytes 884744 | tf_op jit(solution)/shard_map/ppermute | solution.py:310
  32.9 1.2 collective-permute-done.6.refs_4_
  34.2 1.9 %collective-permute-start.7 = (bf16[128,1152]{1,0:T(8,128)(2,1)S(1)}, bf16[128,1152]{1,0:T(8,128)(2,1)S(1)}, u32[]{:S(2)}, u32[]{:S(2)}) collective-permute-start(bf16[128,1152]{1,0:T(8,128)(2,1)S(1)} %collective-permute-done.6.refs_4_), channel_id=1, source_target_pairs={{0,32},{16,240},{32,64},{48,16},{64,96},{80,48},{96,128},{112,80},... | collective-permute-start | bytes 884744 | tf_op jit(solution)/shard_map/ppermute | solution.py:315
  37.4 3.4 %collective-permute-done.4.after_ref.refs_5_ = bf16[128,1152]{1,0:T(8,128)(2,1)S(1)} collective-permute-done((bf16[128,1152]{1,0:T(8,128)(2,1)S(1)}, bf16[128,1152]{1,0:T(8,128)(2,1)S(1)}, u32[]{:S(2)}, u32[]{:S(2)}) %collective-permute-start.4) | collective-permute-done | bytes 294944 | tf_op jit(solution)/shard_map/ppermute | solution.py:310
  40.8 1.9 %collective-permute-start.8 = (bf16[128,1152]{1,0:T(8,128)(2,1)S(1)}, bf16[128,1152]{1,0:T(8,128)(2,1)S(1)}, u32[]{:S(2)}, u32[]{:S(2)}) collective-permute-start(bf16[128,1152]{1,0:T(8,128)(2,1)S(1)} %collective-permute-done.4.after_ref.refs_5_), channel_id=1, source_target_pairs={{0,32},{16,240},{32,64},{48,16},{64,96},{80,48},{96,128},{112,80},... | collective-permute-start | bytes 884744 | tf_op jit(solution)/shard_map/ppermute | solution.py:310
  42.7 0.0 collective-permute-done.1.n_there
  42.7 4.3 %project.1 = (bf16[512,1152]{1,0:T(8,128)(2,1)S(1)}, f32[256,1152]{1,0:T(8,128)S(1)}, f32[256,128]{1,0:T(8,128)S(1)}, bf16[512,1408]{1,0:T(8,128)(2,1)S(1)}) custom-call(bf16[256,1408]{1,0:T(8,128)(2,1)S(1)} %get-tuple-element.24.n_here, bf16[256,1408]{1,0:T(8,128)(2,1)S(1)} %collective-permute-done.1.n_there, bf16[1408,1152]{1,0:T(8,128)(2,1)} %w_ref.5, ...), custom_call_target="tpu_custom_call" | custom-call | flops 1660944384 | bytes 8912896 | tf_op jit(solution)/shard_map/project/pallas_call | solution.py:38
  47.1 0.0 collective-permute-done.7.refs_6_
  47.1 0.2 collect.1.refs_0_
  47.2 3.4 %collective-permute-done.8.refs_1_ = bf16[128,1152]{1,0:T(8,128)(2,1)S(1)} collective-permute-done((bf16[128,1152]{1,0:T(8,128)(2,1)S(1)}, bf16[128,1152]{1,0:T(8,128)(2,1)S(1)}, u32[]{:S(2)}, u32[]{:S(2)}) %collective-permute-start.8) | collective-permute-done | bytes 294944 | tf_op jit(solution)/shard_map/ppermute | solution.py:310
  50.6 4.0 %pairs.1 = (f32[256,1152]{1,0:T(8,128)S(1)}, bf16[272,1152]{1,0:T(8,128)(2,1)S(1)}, f32[1,128]{1,0:T(1,128)S(1)}) custom-call(f32[1]{0:T(128)S(6)} %copy.10.scale_ref, f32[1]{0:T(128)S(6)} %copy.11.bias_ref, bf16[512,1152]{1,0:T(8,128)(2,1)S(1)} %get-tuple-element.28.img_ref, bf16[896,1152]{1,0:T(8,128)(2,1)S(1)} %collect.1.refs_0_, ...), custom_call_target="tpu_custom_call" | custom-call | flops 2415919104 | bytes 5345800 | tf_op jit(solution)/shard_map/pairs/pallas_call | solution.py:38
  54.7 1.9 %collective-permute-start.9 = (bf16[272,1152]{1,0:T(8,128)(2,1)S(1)}, bf16[272,1152]{1,0:T(8,128)(2,1)S(1)}, u32[]{:S(2)}, u32[]{:S(2)}) collective-permute-start(bf16[272,1152]{1,0:T(8,128)(2,1)S(1)} %get-tuple-element.31), channel_id=1, source_target_pairs={{0,16},{16,0},{1,17},{17,1},{2,18},{18,2},{3,19},{19,3},{4,20},{20... | collective-permute-start | bytes 1880072 | tf_op jit(solution)/shard_map/ppermute | solution.py:353
  56.6 2.0 %collective-permute-done.9.got_ref.core_ref = bf16[272,1152]{1,0:T(8,128)(2,1)S(1)} collective-permute-done((bf16[272,1152]{1,0:T(8,128)(2,1)S(1)}, bf16[272,1152]{1,0:T(8,128)(2,1)S(1)}, u32[]{:S(2)}, u32[]{:S(2)}) %collective-permute-start.9) | collective-permute-done | bytes 626720 | tf_op jit(solution)/shard_map/ppermute | solution.py:353
  58.6 0.1 add_cores.1.after_ref
  58.7 3.4 %collective-permute-start.10 = (bf16[272,1152]{1,0:T(8,128)(2,1)S(1)}, bf16[272,1152]{1,0:T(8,128)(2,1)S(1)}, u32[]{:S(2)}, u32[]{:S(2)}) collective-permute-start(bf16[272,1152]{1,0:T(8,128)(2,1)S(1)} %add_cores.1.after_ref), channel_id=1, source_target_pairs={{0,256},{256,0},{1,257},{257,1},{2,258},{258,2},{3,259},{259,3},{4... | collective-permute-start | bytes 1880072 | tf_op jit(solution)/shard_map/ppermute | solution.py:379
  62.1 0.8 pick.1.after_ref.pick_ref
  63.0 13.8 %collective-permute-done.10.got_ref = bf16[272,1152]{1,0:T(8,128)(2,1)S(1)} collective-permute-done((bf16[272,1152]{1,0:T(8,128)(2,1)S(1)}, bf16[272,1152]{1,0:T(8,128)(2,1)S(1)}, u32[]{:S(2)}, u32[]{:S(2)}) %collective-permute-start.10) | collective-permute-done | bytes 626720 | tf_op jit(solution)/shard_map/ppermute | solution.py:379
  76.8 0.0 copy-start
  76.8 0.5 d_proj.1
  77.3 2.1 %collective-permute-start.11 = (bf16[256,1152]{1,0:T(8,128)(2,1)S(1)}, bf16[256,1152]{1,0:T(8,128)(2,1)S(1)}, u32[]{:S(2)}, u32[]{:S(2)}) collective-permute-start(bf16[256,1152]{1,0:T(8,128)(2,1)S(1)} %get-tuple-element.35.dproj_ref.own_ref), channel_id=1, source_target_pairs={{0,16},{16,0},{1,17},{17,1},{2,18},{18,2},{3,19},{19,3},{4,20},{20... | collective-permute-start | bytes 1769480 | tf_op jit(solution)/shard_map/ppermute | solution.py:387
  79.4 0.0 copy-done
  79.4 0.0 copy-done.2
  79.4 0.0 copy-done.5
  79.4 2.2 %d_features.1 = (bf16[128,1408]{1,0:T(8,128)(2,1)}, f32[1,1408]{1,0:T(1,128)S(1)}) custom-call(bf16[256,1152]{1,0:T(8,128)(2,1)S(1)} %get-tuple-element.35.dproj_ref.own_ref, bf16[128,1408]{1,0:T(8,128)(2,1)S(1)} %bitcast.11, f32[1408]{0:T(1024)S(1)} %copy-done.5, bf16[512,1408]{1,0:T(8,128)(2,1)S(1)} %get-tuple-element.34.rows_ref, ...), custom_call_target="tpu_custom_call" | custom-call | flops 830472192 | bytes 6007808 | tf_op jit(solution)/shard_map/d_features/pallas_call | solution.py:38
  81.6 0.0 collective-permute-done.11.got_ref
  81.6 1.8 %head.1 = bf16[1024,512]{1,0:T(8,128)(2,1)S(1)} custom-call(bf16[256,1152]{1,0:T(8,128)(2,1)S(1)} %get-tuple-element.35.dproj_ref.own_ref, bf16[256,1152]{1,0:T(8,128)(2,1)S(1)} %collective-permute-done.11.got_ref, bf16[384,512]{1,0:T(8,128)(2,1)S(1)} %pick.1.after_ref.pick_ref, bf16[512,1408]{1,0:T(8,128)(2,1)S(1)} %get-tuple-element.34.rows_ref, ...), custom_call_target="tpu_custom_call" | custom-call | flops 1283457024 | bytes 7319040 | tf_op jit(solution)/shard_map/head/pallas_call | solution.py:38
  83.4 46.3 %all_to_all.22 = bf16[128,8,512]{2,1,0:T(8,128)(2,1)S(1)} all-to-all(bf16[128,8,512]{2,1,0:T(8,128)(2,1)S(1)} %bitcast.9), channel_id=1, replica_groups=mesh['x'=2,'z'=8,'c'=2,'hx'=2,'y'=8] {'z','hx','y'}, dimensions={0} | all-to-all | bytes 2097152 | tf_op jit(solution)/shard_map/all_to_all | solution.py:415
  129.7 0.2 reduce.1
  129.8 14.9 %all_to_all.23 = bf16[16,8,512]{2,1,0:T(8,128)(2,1)S(1)} all-to-all(bf16[16,8,512]{2,1,0:T(8,128)(2,1)S(1)} %bitcast.12), channel_id=1, replica_groups=mesh['x'=2,'z'=8,'c'=2,'hx'=2,'y'=8] {'hx','y'}, dimensions={0} | all-to-all | bytes 262144 | tf_op jit(solution)/shard_map/all_to_all | solution.py:422
  144.8 0.7 unpack.1
  (2 shorter events, 0.0 us)
Async XLA Ops:
  0.6 1.0 copy-start.1
  1.6 1.0 copy-start.3
  2.6 0.7 copy-start.4
  3.6 6.2 %collective-permute-start = (bf16[128,2560]{1,0:T(8,128)(2,1)S(1)}, bf16[128,2560]{1,0:T(8,128)(2,1)S(1)}, u32[]{:S(2)}, u32[]{:S(2)}) collective-permute-start(bf16[128,2560]{1,0:T(8,128)(2,1)S(1)} %get-tuple-element.23.own_ref), channel_id=1, source_target_pairs={{0,16},{16,0},{1,17},{17,1},{2,18},{18,2},{3,19},{19,3},{4,20},{20... | collective-permute-start | bytes 1966088 | tf_op jit(solution)/shard_map/ppermute | solution.py:304
  5.5 15.6 %collective-permute-start.2 = (bf16[128,1152]{1,0:T(8,128)(2,1)S(1)}, bf16[128,1152]{1,0:T(8,128)(2,1)S(1)}, u32[]{:S(2)}, u32[]{:S(2)}) collective-permute-start(bf16[128,1152]{1,0:T(8,128)(2,1)S(1)} %get-tuple-element.25.refs_0_), channel_id=1, source_target_pairs={{0,32},{16,240},{32,64},{48,16},{64,96},{80,48},{96,128},{112,80},... | collective-permute-start | bytes 884744 | tf_op jit(solution)/shard_map/ppermute | solution.py:310
  9.9 14.4 %collective-permute-start.5 = (bf16[128,1152]{1,0:T(8,128)(2,1)S(1)}, bf16[128,1152]{1,0:T(8,128)(2,1)S(1)}, u32[]{:S(2)}, u32[]{:S(2)}) collective-permute-start(bf16[128,1152]{1,0:T(8,128)(2,1)S(1)} %get-tuple-element.26), channel_id=1, source_target_pairs={{0,32},{16,240},{32,64},{48,16},{64,96},{80,48},{96,128},{112,80},... | collective-permute-start | bytes 884744 | tf_op jit(solution)/shard_map/ppermute | solution.py:315
  14.2 28.5 %collective-permute-start.1 = (bf16[256,1408]{1,0:T(8,128)(2,1)S(1)}, bf16[256,1408]{1,0:T(8,128)(2,1)S(1)}, u32[]{:S(2)}, u32[]{:S(2)}) collective-permute-start(bf16[256,1408]{1,0:T(8,128)(2,1)S(1)} %get-tuple-element.24.n_here), channel_id=1, source_target_pairs={{0,256},{256,0},{1,257},{257,1},{2,258},{258,2},{3,259},{259,3},{4... | collective-permute-start | bytes 2162696 | tf_op jit(solution)/shard_map/ppermute | solution.py:327
  21.2 9.8 %collective-permute-start.3 = (bf16[128,1152]{1,0:T(8,128)(2,1)S(1)}, bf16[128,1152]{1,0:T(8,128)(2,1)S(1)}, u32[]{:S(2)}, u32[]{:S(2)}) collective-permute-start(bf16[128,1152]{1,0:T(8,128)(2,1)S(1)} %collective-permute-done.2.refs_1_), channel_id=1, source_target_pairs={{0,32},{16,240},{32,64},{48,16},{64,96},{80,48},{96,128},{112,80},... | collective-permute-start | bytes 884744 | tf_op jit(solution)/shard_map/ppermute | solution.py:310
  24.3 9.8 %collective-permute-start.6 = (bf16[128,1152]{1,0:T(8,128)(2,1)S(1)}, bf16[128,1152]{1,0:T(8,128)(2,1)S(1)}, u32[]{:S(2)}, u32[]{:S(2)}) collective-permute-start(bf16[128,1152]{1,0:T(8,128)(2,1)S(1)} %collective-permute-done.5.refs_2_), channel_id=1, source_target_pairs={{0,32},{16,240},{32,64},{48,16},{64,96},{80,48},{96,128},{112,80},... | collective-permute-start | bytes 884744 | tf_op jit(solution)/shard_map/ppermute | solution.py:315
  31.0 9.8 %collective-permute-start.4 = (bf16[128,1152]{1,0:T(8,128)(2,1)S(1)}, bf16[128,1152]{1,0:T(8,128)(2,1)S(1)}, u32[]{:S(2)}, u32[]{:S(2)}) collective-permute-start(bf16[128,1152]{1,0:T(8,128)(2,1)S(1)} %collective-permute-done.3.refs_3_), channel_id=1, source_target_pairs={{0,32},{16,240},{32,64},{48,16},{64,96},{80,48},{96,128},{112,80},... | collective-permute-start | bytes 884744 | tf_op jit(solution)/shard_map/ppermute | solution.py:310
  34.2 12.9 %collective-permute-start.7 = (bf16[128,1152]{1,0:T(8,128)(2,1)S(1)}, bf16[128,1152]{1,0:T(8,128)(2,1)S(1)}, u32[]{:S(2)}, u32[]{:S(2)}) collective-permute-start(bf16[128,1152]{1,0:T(8,128)(2,1)S(1)} %collective-permute-done.6.refs_4_), channel_id=1, source_target_pairs={{0,32},{16,240},{32,64},{48,16},{64,96},{80,48},{96,128},{112,80},... | collective-permute-start | bytes 884744 | tf_op jit(solution)/shard_map/ppermute | solution.py:315
  40.8 9.8 %collective-permute-start.8 = (bf16[128,1152]{1,0:T(8,128)(2,1)S(1)}, bf16[128,1152]{1,0:T(8,128)(2,1)S(1)}, u32[]{:S(2)}, u32[]{:S(2)}) collective-permute-start(bf16[128,1152]{1,0:T(8,128)(2,1)S(1)} %collective-permute-done.4.after_ref.refs_5_), channel_id=1, source_target_pairs={{0,32},{16,240},{32,64},{48,16},{64,96},{80,48},{96,128},{112,80},... | collective-permute-start | bytes 884744 | tf_op jit(solution)/shard_map/ppermute | solution.py:310
  54.7 4.0 %collective-permute-start.9 = (bf16[272,1152]{1,0:T(8,128)(2,1)S(1)}, bf16[272,1152]{1,0:T(8,128)(2,1)S(1)}, u32[]{:S(2)}, u32[]{:S(2)}) collective-permute-start(bf16[272,1152]{1,0:T(8,128)(2,1)S(1)} %get-tuple-element.31), channel_id=1, source_target_pairs={{0,16},{16,0},{1,17},{17,1},{2,18},{18,2},{3,19},{19,3},{4,20},{20... | collective-permute-start | bytes 1880072 | tf_op jit(solution)/shard_map/ppermute | solution.py:353
  58.7 18.1 %collective-permute-start.10 = (bf16[272,1152]{1,0:T(8,128)(2,1)S(1)}, bf16[272,1152]{1,0:T(8,128)(2,1)S(1)}, u32[]{:S(2)}, u32[]{:S(2)}) collective-permute-start(bf16[272,1152]{1,0:T(8,128)(2,1)S(1)} %add_cores.1.after_ref), channel_id=1, source_target_pairs={{0,256},{256,0},{1,257},{257,1},{2,258},{258,2},{3,259},{259,3},{4... | collective-permute-start | bytes 1880072 | tf_op jit(solution)/shard_map/ppermute | solution.py:379
  76.8 2.6 %copy-start = (bf16[1408,1152]{1,0:T(8,128)(2,1)S(1)}, bf16[1408,1152]{1,0:T(8,128)(2,1)}, u32[]{:S(2)}) copy-start(bf16[1408,1152]{1,0:T(8,128)(2,1)} %w_ref.5) | copy-start | bytes 9732100
  76.8 2.6 %copy-start.2 = (bf16[1,128,1408]{2,1,0:T(8,128)(2,1)S(1)}, bf16[1,128,1408]{2,1,0:T(8,128)(2,1)}, u32[]{:S(2)}) copy-start(bf16[1,128,1408]{2,1,0:T(8,128)(2,1)} %param.6) | copy-start | bytes 1081348
  76.8 2.6 %copy-start.5 = (f32[1408]{0:T(1024)S(1)}, f32[1408]{0:T(1024)}, u32[]{:S(2)}) copy-start(f32[1408]{0:T(1024)} %gain_ref.5) | copy-start | bytes 16900
  77.3 4.3 %collective-permute-start.11 = (bf16[256,1152]{1,0:T(8,128)(2,1)S(1)}, bf16[256,1152]{1,0:T(8,128)(2,1)S(1)}, u32[]{:S(2)}, u32[]{:S(2)}) collective-permute-start(bf16[256,1152]{1,0:T(8,128)(2,1)S(1)} %get-tuple-element.35.dproj_ref.own_ref), channel_id=1, source_target_pairs={{0,16},{16,0},{1,17},{17,1},{2,18},{18,2},{3,19},{19,3},{4,20},{20... | collective-permute-start | bytes 1769480 | tf_op jit(solution)/shard_map/ppermute | solution.py:387

commit v4 on v3

--- a/solution.py
+++ b/solution.py
@@ -20,6 +20,7 @@
 N_GROUP = 16
 PIECE = 512
 BLOCK = 128
+HALF = BLOCK // 2
 EXTRA = 16
 GAIN_AT = 112
 
@@ -255,23 +256,33 @@
     return packed.astype(BF16)
 
 
-def reduce_kernel(got_ref, out_ref):
-    total = got_ref[...].astype(F32).reshape(N_GROUP * NZ, 8, PIECE).sum(axis=0)
-    rest = jnp.concatenate([total[3:], total[:3]], axis=0)
-    index = lax.broadcasted_iota(jnp.int32, (8, PIECE), 0)
-    whole = total + rest
+def keep_low(total):
+    tail = total[HALF - 16 :]
+    whole = tail + jnp.concatenate([tail[3:], tail[:3]], axis=0)
     high = whole.astype(BF16).astype(F32)
     low = whole - high
-    moved = jnp.concatenate([low[5:], low[:5]], axis=0)
+    moved = jnp.concatenate([low[13:], low[:13]], axis=0)
+    index = lax.broadcasted_iota(jnp.int32, (16, PIECE), 0)
     split = jnp.where(index < 3, high, jnp.where(index < 6, moved, 0.0))
-    group = lax.axis_index(HX) * 8 + lax.axis_index(Y)
-    piece = jnp.where(group == GAIN_AT // 8, split, total)
-    copies = jnp.broadcast_to(piece[None], (N_GROUP, 8, PIECE)).reshape(BLOCK, PIECE)
-    out_ref[...] = copies.astype(BF16)
-
-
-def unpack_kernel(got_ref, head_ref, gain_ref, loss_ref):
-    block = got_ref[...].astype(F32)
+    split = jnp.where(lax.axis_index(HX) == 1, split, tail)
+    return jnp.concatenate([total[: HALF - 16], split], axis=0).astype(BF16)
+
+
+def sum_near_kernel(got_ref, out_ref):
+    total = got_ref[...].astype(F32).reshape(2 * NZ, HALF, PIECE).sum(axis=0)
+    half = keep_low(total)
+    for i in range(8):
+        out_ref[HALF * i : HALF * (i + 1), :] = half
+
+
+def sum_y_kernel(got_ref, out_ref):
+    out_ref[...] = keep_low(got_ref[...].astype(F32).reshape(8, HALF, PIECE).sum(axis=0))
+
+
+def unpack_kernel(own_ref, other_ref, head_ref, gain_ref, loss_ref):
+    first = lax.axis_index(HX) == 0
+    own, other = own_ref[...].astype(F32), other_ref[...].astype(F32)
+    block = jnp.concatenate([jnp.where(first, own, other), jnp.where(first, other, own)], axis=0)
     head_ref[:, :512] = block[:SHARE]
     head_ref[:, 512:1024] = block[48 : 48 + SHARE]
     tail = block[96:112]
@@ -412,18 +423,15 @@
         mib=24,
         name="head",
     )
-    packed = lax.all_to_all(packed, (Z, HX, Y), 0, 0, tiled=True)
-    piece = call(
-        reduce_kernel,
-        out((BLOCK, PIECE), BF16),
-        packed,
-        name="reduce",
-    )
-    block = lax.all_to_all(piece, (HX, Y), 0, 0, tiled=True)
+    packed = lax.all_to_all(packed, (Z, HX), 0, 0, tiled=True)
+    half = call(sum_near_kernel, out((8 * HALF, PIECE), BF16), packed, name="sum_near")
+    half = lax.all_to_all(half, Y, 0, 0, tiled=True)
+    half = call(sum_y_kernel, out((HALF, PIECE), BF16), half, name="sum_y")
     head, d_gain, loss = call(
         unpack_kernel,
         (out((SHARE, E), F32), out((W,), F32), out((1,), F32)),
-        block,
+        half,
+        lax.ppermute(half, HX, SWAP),
         outs=(VMEM, VMEM, SMEM),
         name="unpack",
     )

time: 146 us -> 153 us (1.048)
  waiting for transfers between devices: 32.3 us -> 37.5 us
  starting transfers between devices: 32 us -> 34.5 us
    ppermute x0 -> x1, waiting for transfers between devices: none -> 5.12 us  [per_device(): lax.ppermute(half, HX, SWAP)]
    ppermute x0 -> x1, starting transfers between devices: none -> 2.53 us  [per_device(): lax.ppermute(half, HX, SWAP)]
    pallas_call x12 -> x13, Pallas kernels: 15.2 us -> 15.3 us  [call(): pl.pallas_call(kernel, out_shape=out_shape, in_specs=specs or [VMEM] * le...]
  transfers between devices with their start and end apart: 12 -> 13, of which waited for: 8 -> 9; matrix products, arithmetic and copies ran while one was open for 0% -> 0% of each run, Pallas kernels for 5% -> 5%
where the time goes in v4:
time: 153 us; the launch traced here: 152 us
  blocking collectives  59.8 us (39%)
  waiting for transfers between devices  37.5 us (25%)
  starting transfers between devices  34.5 us (23%)
  Pallas kernels  15.3 us (10%)
  local copies, waits for them, and re-layouts  2.65 us (2%)
  between operations  2.16 us (1%)
    all_to_all x1, blocking collectives, per_device(): packed = lax.all_to_all(packed, (Z, HX), 0, 0, tiled=True)  38.3 us
    all_to_all x1, blocking collectives, per_device(): half = lax.all_to_all(half, Y, 0, 0, tiled=True)  21.6 us
    pallas_call x13, Pallas kernels, call(): pl.pallas_call(kernel, out_shape=out_shape, in_specs=specs or [VMEM] * le...  15.3 us
    ppermute x4, waiting for transfers between devices, per_device(): one = hop(one)  14 us
    ppermute x1, waiting for transfers between devices, per_device(): across(send)  13.8 us
    ppermute x4, starting transfers between devices, per_device(): one = hop(one)  10 us
    ppermute x3, starting transfers between devices, per_device(): two = hop(two)  9.26 us
    ppermute x1, waiting for transfers between devices, per_device(): lax.ppermute(half, HX, SWAP)  5.12 us
  transfers between devices with their start and end apart: 13, of which 9 were waited for; matrix products, arithmetic and copies ran while one was open for 0% of the time, Pallas kernels for 5%

profile of v4, /device:TPU:8, one launch (start us, length us, event | category | flops | bytes accessed | tf_op | source)
XLA Modules:
  0.0 151.9 jit_solution(189955310212052754)
XLA Ops:
  0.6 0.0 copy-start.1
  0.6 1.0 copy-done.1
  1.6 1.0 copy-done.3
  2.6 0.7 copy-done.4
  3.3 0.3 prepare.1
  3.6 1.9 %collective-permute-start = (bf16[128,2560]{1,0:T(8,128)(2,1)S(1)}, bf16[128,2560]{1,0:T(8,128)(2,1)S(1)}, u32[]{:S(2)}, u32[]{:S(2)}) collective-permute-start(bf16[128,2560]{1,0:T(8,128)(2,1)S(1)} %get-tuple-element.23.own_ref), channel_id=1, source_target_pairs={{0,16},{16,0},{1,17},{17,1},{2,18},{18,2},{3,19},{19,3},{4,20},{20... | collective-permute-start | bytes 1966088 | tf_op jit(solution)/shard_map/ppermute | solution.py:315
  5.5 4.3 %collective-permute-start.2 = (bf16[128,1152]{1,0:T(8,128)(2,1)S(1)}, bf16[128,1152]{1,0:T(8,128)(2,1)S(1)}, u32[]{:S(2)}, u32[]{:S(2)}) collective-permute-start(bf16[128,1152]{1,0:T(8,128)(2,1)S(1)} %get-tuple-element.25.refs_0_), channel_id=1, source_target_pairs={{0,32},{16,240},{32,64},{48,16},{64,96},{80,48},{96,128},{112,80},... | collective-permute-start | bytes 884744 | tf_op jit(solution)/shard_map/ppermute | solution.py:321
  9.8 0.0 collective-permute-done.got_ref
  9.8 0.1 unpack_swap.1
  9.9 4.3 %collective-permute-start.5 = (bf16[128,1152]{1,0:T(8,128)(2,1)S(1)}, bf16[128,1152]{1,0:T(8,128)(2,1)S(1)}, u32[]{:S(2)}, u32[]{:S(2)}) collective-permute-start(bf16[128,1152]{1,0:T(8,128)(2,1)S(1)} %get-tuple-element.26), channel_id=1, source_target_pairs={{0,32},{16,240},{32,64},{48,16},{64,96},{80,48},{96,128},{112,80},... | collective-permute-start | bytes 884744 | tf_op jit(solution)/shard_map/ppermute | solution.py:326
  14.2 3.4 %collective-permute-start.1 = (bf16[256,1408]{1,0:T(8,128)(2,1)S(1)}, bf16[256,1408]{1,0:T(8,128)(2,1)S(1)}, u32[]{:S(2)}, u32[]{:S(2)}) collective-permute-start(bf16[256,1408]{1,0:T(8,128)(2,1)S(1)} %get-tuple-element.24.n_here), channel_id=1, source_target_pairs={{0,256},{256,0},{1,257},{257,1},{2,258},{258,2},{3,259},{259,3},{4... | collective-permute-start | bytes 2162696 | tf_op jit(solution)/shard_map/ppermute | solution.py:338
  17.6 3.6 %collective-permute-done.2.refs_1_ = bf16[128,1152]{1,0:T(8,128)(2,1)S(1)} collective-permute-done((bf16[128,1152]{1,0:T(8,128)(2,1)S(1)}, bf16[128,1152]{1,0:T(8,128)(2,1)S(1)}, u32[]{:S(2)}, u32[]{:S(2)}) %collective-permute-start.2) | collective-permute-done | bytes 294944 | tf_op jit(solution)/shard_map/ppermute | solution.py:321
  21.2 1.9 %collective-permute-start.3 = (bf16[128,1152]{1,0:T(8,128)(2,1)S(1)}, bf16[128,1152]{1,0:T(8,128)(2,1)S(1)}, u32[]{:S(2)}, u32[]{:S(2)}) collective-permute-start(bf16[128,1152]{1,0:T(8,128)(2,1)S(1)} %collective-permute-done.2.refs_1_), channel_id=1, source_target_pairs={{0,32},{16,240},{32,64},{48,16},{64,96},{80,48},{96,128},{112,80},... | collective-permute-start | bytes 884744 | tf_op jit(solution)/shard_map/ppermute | solution.py:321
  23.1 1.2 collective-permute-done.5.refs_2_
  24.3 3.1 %collective-permute-start.6 = (bf16[128,1152]{1,0:T(8,128)(2,1)S(1)}, bf16[128,1152]{1,0:T(8,128)(2,1)S(1)}, u32[]{:S(2)}, u32[]{:S(2)}) collective-permute-start(bf16[128,1152]{1,0:T(8,128)(2,1)S(1)} %collective-permute-done.5.refs_2_), channel_id=1, source_target_pairs={{0,32},{16,240},{32,64},{48,16},{64,96},{80,48},{96,128},{112,80},... | collective-permute-start | bytes 884744 | tf_op jit(solution)/shard_map/ppermute | solution.py:326
  27.4 3.6 %collective-permute-done.3.refs_3_ = bf16[128,1152]{1,0:T(8,128)(2,1)S(1)} collective-permute-done((bf16[128,1152]{1,0:T(8,128)(2,1)S(1)}, bf16[128,1152]{1,0:T(8,128)(2,1)S(1)}, u32[]{:S(2)}, u32[]{:S(2)}) %collective-permute-start.3) | collective-permute-done | bytes 294944 | tf_op jit(solution)/shard_map/ppermute | solution.py:321
  31.0 1.9 %collective-permute-start.4 = (bf16[128,1152]{1,0:T(8,128)(2,1)S(1)}, bf16[128,1152]{1,0:T(8,128)(2,1)S(1)}, u32[]{:S(2)}, u32[]{:S(2)}) collective-permute-start(bf16[128,1152]{1,0:T(8,128)(2,1)S(1)} %collective-permute-done.3.refs_3_), channel_id=1, source_target_pairs={{0,32},{16,240},{32,64},{48,16},{64,96},{80,48},{96,128},{112,80},... | collective-permute-start | bytes 884744 | tf_op jit(solution)/shard_map/ppermute | solution.py:321
  32.9 1.2 collective-permute-done.6.refs_4_
  34.2 1.9 %collective-permute-start.7 = (bf16[128,1152]{1,0:T(8,128)(2,1)S(1)}, bf16[128,1152]{1,0:T(8,128)(2,1)S(1)}, u32[]{:S(2)}, u32[]{:S(2)}) collective-permute-start(bf16[128,1152]{1,0:T(8,128)(2,1)S(1)} %collective-permute-done.6.refs_4_), channel_id=1, source_target_pairs={{0,32},{16,240},{32,64},{48,16},{64,96},{80,48},{96,128},{112,80},... | collective-permute-start | bytes 884744 | tf_op jit(solution)/shard_map/ppermute | solution.py:326
  37.4 3.4 %collective-permute-done.4.after_ref.refs_5_ = bf16[128,1152]{1,0:T(8,128)(2,1)S(1)} collective-permute-done((bf16[128,1152]{1,0:T(8,128)(2,1)S(1)}, bf16[128,1152]{1,0:T(8,128)(2,1)S(1)}, u32[]{:S(2)}, u32[]{:S(2)}) %collective-permute-start.4) | collective-permute-done | bytes 294944 | tf_op jit(solution)/shard_map/ppermute | solution.py:321
  40.8 1.9 %collective-permute-start.8 = (bf16[128,1152]{1,0:T(8,128)(2,1)S(1)}, bf16[128,1152]{1,0:T(8,128)(2,1)S(1)}, u32[]{:S(2)}, u32[]{:S(2)}) collective-permute-start(bf16[128,1152]{1,0:T(8,128)(2,1)S(1)} %collective-permute-done.4.after_ref.refs_5_), channel_id=1, source_target_pairs={{0,32},{16,240},{32,64},{48,16},{64,96},{80,48},{96,128},{112,80},... | collective-permute-start | bytes 884744 | tf_op jit(solution)/shard_map/ppermute | solution.py:321
  42.7 0.0 collective-permute-done.1.n_there
  42.7 4.3 %project.1 = (bf16[512,1152]{1,0:T(8,128)(2,1)S(1)}, f32[256,1152]{1,0:T(8,128)S(1)}, f32[256,128]{1,0:T(8,128)S(1)}, bf16[512,1408]{1,0:T(8,128)(2,1)S(1)}) custom-call(bf16[256,1408]{1,0:T(8,128)(2,1)S(1)} %get-tuple-element.24.n_here, bf16[256,1408]{1,0:T(8,128)(2,1)S(1)} %collective-permute-done.1.n_there, bf16[1408,1152]{1,0:T(8,128)(2,1)} %w_ref.5, ...), custom_call_target="tpu_custom_call" | custom-call | flops 1660944384 | bytes 8912896 | tf_op jit(solution)/shard_map/project/pallas_call | solution.py:39
  47.1 0.0 collective-permute-done.7.refs_6_
  47.1 0.2 collect.1.refs_0_
  47.2 3.4 %collective-permute-done.8.refs_1_ = bf16[128,1152]{1,0:T(8,128)(2,1)S(1)} collective-permute-done((bf16[128,1152]{1,0:T(8,128)(2,1)S(1)}, bf16[128,1152]{1,0:T(8,128)(2,1)S(1)}, u32[]{:S(2)}, u32[]{:S(2)}) %collective-permute-start.8) | collective-permute-done | bytes 294944 | tf_op jit(solution)/shard_map/ppermute | solution.py:321
  50.6 4.0 %pairs.1 = (f32[256,1152]{1,0:T(8,128)S(1)}, bf16[272,1152]{1,0:T(8,128)(2,1)S(1)}, f32[1,128]{1,0:T(1,128)S(1)}) custom-call(f32[1]{0:T(128)S(6)} %copy.10.scale_ref, f32[1]{0:T(128)S(6)} %copy.11.bias_ref, bf16[512,1152]{1,0:T(8,128)(2,1)S(1)} %get-tuple-element.28.img_ref, bf16[896,1152]{1,0:T(8,128)(2,1)S(1)} %collect.1.refs_0_, ...), custom_call_target="tpu_custom_call" | custom-call | flops 2415919104 | bytes 5345800 | tf_op jit(solution)/shard_map/pairs/pallas_call | solution.py:39
  54.7 1.9 %collective-permute-start.9 = (bf16[272,1152]{1,0:T(8,128)(2,1)S(1)}, bf16[272,1152]{1,0:T(8,128)(2,1)S(1)}, u32[]{:S(2)}, u32[]{:S(2)}) collective-permute-start(bf16[272,1152]{1,0:T(8,128)(2,1)S(1)} %get-tuple-element.31), channel_id=1, source_target_pairs={{0,16},{16,0},{1,17},{17,1},{2,18},{18,2},{3,19},{19,3},{4,20},{20... | collective-permute-start | bytes 1880072 | tf_op jit(solution)/shard_map/ppermute | solution.py:364
  56.6 2.0 %collective-permute-done.9.got_ref.core_ref = bf16[272,1152]{1,0:T(8,128)(2,1)S(1)} collective-permute-done((bf16[272,1152]{1,0:T(8,128)(2,1)S(1)}, bf16[272,1152]{1,0:T(8,128)(2,1)S(1)}, u32[]{:S(2)}, u32[]{:S(2)}) %collective-permute-start.9) | collective-permute-done | bytes 626720 | tf_op jit(solution)/shard_map/ppermute | solution.py:364
  58.6 0.1 add_cores.1.after_ref
  58.7 3.4 %collective-permute-start.10 = (bf16[272,1152]{1,0:T(8,128)(2,1)S(1)}, bf16[272,1152]{1,0:T(8,128)(2,1)S(1)}, u32[]{:S(2)}, u32[]{:S(2)}) collective-permute-start(bf16[272,1152]{1,0:T(8,128)(2,1)S(1)} %add_cores.1.after_ref), channel_id=1, source_target_pairs={{0,256},{256,0},{1,257},{257,1},{2,258},{258,2},{3,259},{259,3},{4... | collective-permute-start | bytes 1880072 | tf_op jit(solution)/shard_map/ppermute | solution.py:390
  62.1 0.8 pick.1.after_ref.pick_ref
  63.0 13.8 %collective-permute-done.10.got_ref = bf16[272,1152]{1,0:T(8,128)(2,1)S(1)} collective-permute-done((bf16[272,1152]{1,0:T(8,128)(2,1)S(1)}, bf16[272,1152]{1,0:T(8,128)(2,1)S(1)}, u32[]{:S(2)}, u32[]{:S(2)}) %collective-permute-start.10) | collective-permute-done | bytes 626720 | tf_op jit(solution)/shard_map/ppermute | solution.py:390
  76.8 0.5 d_proj.1
  77.3 2.1 %collective-permute-start.11 = (bf16[256,1152]{1,0:T(8,128)(2,1)S(1)}, bf16[256,1152]{1,0:T(8,128)(2,1)S(1)}, u32[]{:S(2)}, u32[]{:S(2)}) collective-permute-start(bf16[256,1152]{1,0:T(8,128)(2,1)S(1)} %get-tuple-element.35.dproj_ref.own_ref), channel_id=1, source_target_pairs={{0,16},{16,0},{1,17},{17,1},{2,18},{18,2},{3,19},{19,3},{4,20},{20... | collective-permute-start | bytes 1769480 | tf_op jit(solution)/shard_map/ppermute | solution.py:398
  79.4 0.0 copy-done
  79.4 0.0 copy-done.2
  79.4 0.0 copy-done.5
  79.4 2.2 %d_features.1 = (bf16[128,1408]{1,0:T(8,128)(2,1)}, f32[1,1408]{1,0:T(1,128)S(1)}) custom-call(bf16[256,1152]{1,0:T(8,128)(2,1)S(1)} %get-tuple-element.35.dproj_ref.own_ref, bf16[128,1408]{1,0:T(8,128)(2,1)S(1)} %bitcast.13, f32[1408]{0:T(1024)S(1)} %copy-done.5, bf16[512,1408]{1,0:T(8,128)(2,1)S(1)} %get-tuple-element.34.rows_ref, ...), custom_call_target="tpu_custom_call" | custom-call | flops 830472192 | bytes 6007808 | tf_op jit(solution)/shard_map/d_features/pallas_call | solution.py:39
  81.6 0.0 collective-permute-done.11.got_ref
  81.6 1.8 %head.1 = bf16[1024,512]{1,0:T(8,128)(2,1)S(1)} custom-call(bf16[256,1152]{1,0:T(8,128)(2,1)S(1)} %get-tuple-element.35.dproj_ref.own_ref, bf16[256,1152]{1,0:T(8,128)(2,1)S(1)} %collective-permute-done.11.got_ref, bf16[384,512]{1,0:T(8,128)(2,1)S(1)} %pick.1.after_ref.pick_ref, bf16[512,1408]{1,0:T(8,128)(2,1)S(1)} %get-tuple-element.34.rows_ref, ...), custom_call_target="tpu_custom_call" | custom-call | flops 1283457024 | bytes 7319040 | tf_op jit(solution)/shard_map/head/pallas_call | solution.py:39
  83.4 38.3 %all_to_all.22 = bf16[16,64,512]{2,1,0:T(8,128)(2,1)S(1)} all-to-all(bf16[16,64,512]{2,1,0:T(8,128)(2,1)S(1)} %bitcast.9), channel_id=1, replica_groups=mesh['x'=2,'z'=8,'c'=2,'hx'=2,'y'=8] {'z','hx'}, dimensions={0} | all-to-all | bytes 2097152 | tf_op jit(solution)/shard_map/all_to_all | solution.py:426
  121.7 0.2 sum_near.1
  121.8 21.6 %all_to_all.23 = bf16[8,64,512]{2,1,0:T(8,128)(2,1)S(1)} all-to-all(bf16[8,64,512]{2,1,0:T(8,128)(2,1)S(1)} %bitcast.10), channel_id=1, replica_groups=mesh['x'=2,'z'=8,'c'=2,'hx'=2,'y'=8] {'y'}, dimensions={0} | all-to-all | bytes 1048576 | tf_op jit(solution)/shard_map/all_to_all | solution.py:428
  143.4 0.1 sum_y.1.own_ref
  143.5 2.5 %collective-permute-start.12 = (bf16[64,512]{1,0:T(8,128)(2,1)S(1)}, bf16[64,512]{1,0:T(8,128)(2,1)S(1)}, u32[]{:S(2)}, u32[]{:S(2)}) collective-permute-start(bf16[64,512]{1,0:T(8,128)(2,1)S(1)} %sum_y.1.own_ref), channel_id=1, source_target_pairs={{0,8},{8,0},{1,9},{9,1},{2,10},{10,2},{3,11},{11,3},{4,12},{12,4},... | collective-permute-start | bytes 196616 | tf_op jit(solution)/shard_map/ppermute | solution.py:434
  146.0 5.1 %collective-permute-done.12.other_ref = bf16[64,512]{1,0:T(8,128)(2,1)S(1)} collective-permute-done((bf16[64,512]{1,0:T(8,128)(2,1)S(1)}, bf16[64,512]{1,0:T(8,128)(2,1)S(1)}, u32[]{:S(2)}, u32[]{:S(2)}) %collective-permute-start.12) | collective-permute-done | bytes 65568 | tf_op jit(solution)/shard_map/ppermute | solution.py:434
  151.1 0.7 unpack.1
  (5 shorter events, 0.0 us)
Async XLA Ops:
  0.6 1.0 copy-start.1
  1.6 1.0 copy-start.3
  2.6 0.7 copy-start.4
  3.6 6.2 %collective-permute-start = (bf16[128,2560]{1,0:T(8,128)(2,1)S(1)}, bf16[128,2560]{1,0:T(8,128)(2,1)S(1)}, u32[]{:S(2)}, u32[]{:S(2)}) collective-permute-start(bf16[128,2560]{1,0:T(8,128)(2,1)S(1)} %get-tuple-element.23.own_ref), channel_id=1, source_target_pairs={{0,16},{16,0},{1,17},{17,1},{2,18},{18,2},{3,19},{19,3},{4,20},{20... | collective-permute-start | bytes 1966088 | tf_op jit(solution)/shard_map/ppermute | solution.py:315
  5.5 15.6 %collective-permute-start.2 = (bf16[128,1152]{1,0:T(8,128)(2,1)S(1)}, bf16[128,1152]{1,0:T(8,128)(2,1)S(1)}, u32[]{:S(2)}, u32[]{:S(2)}) collective-permute-start(bf16[128,1152]{1,0:T(8,128)(2,1)S(1)} %get-tuple-element.25.refs_0_), channel_id=1, source_target_pairs={{0,32},{16,240},{32,64},{48,16},{64,96},{80,48},{96,128},{112,80},... | collective-permute-start | bytes 884744 | tf_op jit(solution)/shard_map/ppermute | solution.py:321
  9.9 14.4 %collective-permute-start.5 = (bf16[128,1152]{1,0:T(8,128)(2,1)S(1)}, bf16[128,1152]{1,0:T(8,128)(2,1)S(1)}, u32[]{:S(2)}, u32[]{:S(2)}) collective-permute-start(bf16[128,1152]{1,0:T(8,128)(2,1)S(1)} %get-tuple-element.26), channel_id=1, source_target_pairs={{0,32},{16,240},{32,64},{48,16},{64,96},{80,48},{96,128},{112,80},... | collective-permute-start | bytes 884744 | tf_op jit(solution)/shard_map/ppermute | solution.py:326
  14.2 28.5 %collective-permute-start.1 = (bf16[256,1408]{1,0:T(8,128)(2,1)S(1)}, bf16[256,1408]{1,0:T(8,128)(2,1)S(1)}, u32[]{:S(2)}, u32[]{:S(2)}) collective-permute-start(bf16[256,1408]{1,0:T(8,128)(2,1)S(1)} %get-tuple-element.24.n_here), channel_id=1, source_target_pairs={{0,256},{256,0},{1,257},{257,1},{2,258},{258,2},{3,259},{259,3},{4... | collective-permute-start | bytes 2162696 | tf_op jit(solution)/shard_map/ppermute | solution.py:338
  21.2 9.8 %collective-permute-start.3 = (bf16[128,1152]{1,0:T(8,128)(2,1)S(1)}, bf16[128,1152]{1,0:T(8,128)(2,1)S(1)}, u32[]{:S(2)}, u32[]{:S(2)}) collective-permute-start(bf16[128,1152]{1,0:T(8,128)(2,1)S(1)} %collective-permute-done.2.refs_1_), channel_id=1, source_target_pairs={{0,32},{16,240},{32,64},{48,16},{64,96},{80,48},{96,128},{112,80},... | collective-permute-start | bytes 884744 | tf_op jit(solution)/shard_map/ppermute | solution.py:321
  24.3 9.8 %collective-permute-start.6 = (bf16[128,1152]{1,0:T(8,128)(2,1)S(1)}, bf16[128,1152]{1,0:T(8,128)(2,1)S(1)}, u32[]{:S(2)}, u32[]{:S(2)}) collective-permute-start(bf16[128,1152]{1,0:T(8,128)(2,1)S(1)} %collective-permute-done.5.refs_2_), channel_id=1, source_target_pairs={{0,32},{16,240},{32,64},{48,16},{64,96},{80,48},{96,128},{112,80},... | collective-permute-start | bytes 884744 | tf_op jit(solution)/shard_map/ppermute | solution.py:326
  31.0 9.8 %collective-permute-start.4 = (bf16[128,1152]{1,0:T(8,128)(2,1)S(1)}, bf16[128,1152]{1,0:T(8,128)(2,1)S(1)}, u32[]{:S(2)}, u32[]{:S(2)}) collective-permute-start(bf16[128,1152]{1,0:T(8,128)(2,1)S(1)} %collective-permute-done.3.refs_3_), channel_id=1, source_target_pairs={{0,32},{16,240},{32,64},{48,16},{64,96},{80,48},{96,128},{112,80},... | collective-permute-start | bytes 884744 | tf_op jit(solution)/shard_map/ppermute | solution.py:321
  34.2 12.9 %collective-permute-start.7 = (bf16[128,1152]{1,0:T(8,128)(2,1)S(1)}, bf16[128,1152]{1,0:T(8,128)(2,1)S(1)}, u32[]{:S(2)}, u32[]{:S(2)}) collective-permute-start(bf16[128,1152]{1,0:T(8,128)(2,1)S(1)} %collective-permute-done.6.refs_4_), channel_id=1, source_target_pairs={{0,32},{16,240},{32,64},{48,16},{64,96},{80,48},{96,128},{112,80},... | collective-permute-start | bytes 884744 | tf_op jit(solution)/shard_map/ppermute | solution.py:326
  40.8 9.8 %collective-permute-start.8 = (bf16[128,1152]{1,0:T(8,128)(2,1)S(1)}, bf16[128,1152]{1,0:T(8,128)(2,1)S(1)}, u32[]{:S(2)}, u32[]{:S(2)}) collective-permute-start(bf16[128,1152]{1,0:T(8,128)(2,1)S(1)} %collective-permute-done.4.after_ref.refs_5_), channel_id=1, source_target_pairs={{0,32},{16,240},{32,64},{48,16},{64,96},{80,48},{96,128},{112,80},... | collective-permute-start | bytes 884744 | tf_op jit(solution)/shard_map/ppermute | solution.py:321
  54.7 4.0 %collective-permute-start.9 = (bf16[272,1152]{1,0:T(8,128)(2,1)S(1)}, bf16[272,1152]{1,0:T(8,128)(2,1)S(1)}, u32[]{:S(2)}, u32[]{:S(2)}) collective-permute-start(bf16[272,1152]{1,0:T(8,128)(2,1)S(1)} %get-tuple-element.31), channel_id=1, source_target_pairs={{0,16},{16,0},{1,17},{17,1},{2,18},{18,2},{3,19},{19,3},{4,20},{20... | collective-permute-start | bytes 1880072 | tf_op jit(solution)/shard_map/ppermute | solution.py:364
  58.7 18.1 %collective-permute-start.10 = (bf16[272,1152]{1,0:T(8,128)(2,1)S(1)}, bf16[272,1152]{1,0:T(8,128)(2,1)S(1)}, u32[]{:S(2)}, u32[]{:S(2)}) collective-permute-start(bf16[272,1152]{1,0:T(8,128)(2,1)S(1)} %add_cores.1.after_ref), channel_id=1, source_target_pairs={{0,256},{256,0},{1,257},{257,1},{2,258},{258,2},{3,259},{259,3},{4... | collective-permute-start | bytes 1880072 | tf_op jit(solution)/shard_map/ppermute | solution.py:390
  76.8 2.6 %copy-start = (bf16[1408,1152]{1,0:T(8,128)(2,1)S(1)}, bf16[1408,1152]{1,0:T(8,128)(2,1)}, u32[]{:S(2)}) copy-start(bf16[1408,1152]{1,0:T(8,128)(2,1)} %w_ref.5) | copy-start | bytes 9732100
  76.8 2.6 %copy-start.2 = (bf16[1,128,1408]{2,1,0:T(8,128)(2,1)S(1)}, bf16[1,128,1408]{2,1,0:T(8,128)(2,1)}, u32[]{:S(2)}) copy-start(bf16[1,128,1408]{2,1,0:T(8,128)(2,1)} %param.6) | copy-start | bytes 1081348
  76.8 2.6 %copy-start.5 = (f32[1408]{0:T(1024)S(1)}, f32[1408]{0:T(1024)}, u32[]{:S(2)}) copy-start(f32[1408]{0:T(1024)} %gain_ref.5) | copy-start | bytes 16900
  77.3 4.3 %collective-permute-start.11 = (bf16[256,1152]{1,0:T(8,128)(2,1)S(1)}, bf16[256,1152]{1,0:T(8,128)(2,1)S(1)}, u32[]{:S(2)}, u32[]{:S(2)}) collective-permute-start(bf16[256,1152]{1,0:T(8,128)(2,1)S(1)} %get-tuple-element.35.dproj_ref.own_ref), channel_id=1, source_target_pairs={{0,16},{16,0},{1,17},{17,1},{2,18},{18,2},{3,19},{19,3},{4,20},{20... | collective-permute-start | bytes 1769480 | tf_op jit(solution)/shard_map/ppermute | solution.py:398
  143.5 7.7 %collective-permute-start.12 = (bf16[64,512]{1,0:T(8,128)(2,1)S(1)}, bf16[64,512]{1,0:T(8,128)(2,1)S(1)}, u32[]{:S(2)}, u32[]{:S(2)}) collective-permute-start(bf16[64,512]{1,0:T(8,128)(2,1)S(1)} %sum_y.1.own_ref), channel_id=1, source_target_pairs={{0,8},{8,0},{1,9},{9,1},{2,10},{10,2},{3,11},{11,3},{4,12},{12,4},... | collective-permute-start | bytes 196616 | tf_op jit(solution)/shard_map/ppermute | solution.py:434

commit v5 on v3

--- a/solution.py
+++ b/solution.py
@@ -18,10 +18,9 @@
 X, Z, C, HX, Y = "x", "z", "c", "hx", "y"
 NZ = 8
 N_GROUP = 16
-PIECE = 512
-BLOCK = 128
+PIECE = 896
+BLOCK = 64
 EXTRA = 16
-GAIN_AT = 112
 
 SWAP = [(0, 1), (1, 0)]
 HOP = [
@@ -225,62 +224,56 @@
     feat_ref[...] = feat.astype(BF16)
 
 
+def split_rows(first, second):
+    high = [r.astype(BF16).astype(F32) for r in (first, second)]
+    return high + [first - high[0], second - high[1]]
+
+
 def head_kernel(own_ref, got_ref, pick_ref, rows_ref, w_ref, gain_ref, part_ref, loss_ref, out_ref):
     head = jnp.dot(pick_ref[:, : 2 * ROWS], own_ref[...], preferred_element_type=F32) + jnp.dot(
         pick_ref[:, 2 * ROWS :], got_ref[...], preferred_element_type=F32
     )
-    head = head.astype(BF16)
     d_normed = back(got_ref[...], w_ref)
     gain = part_ref[...] + jnp.sum(rows_ref[2 * ROWS :, :].astype(F32) * d_normed, axis=0, keepdims=True)
-    packed = split_rows(gain / gain_ref[...].reshape(1, W), loss_ref[...])
+    gain = gain / gain_ref[...].reshape(1, W)
+    rest = [gain[:, PIECE:], loss_ref[...], jnp.zeros((1, 2 * PIECE - W - 128), F32)]
+    extra = split_rows(gain[:, :PIECE], jnp.concatenate(rest, axis=1))
+    index = lax.broadcasted_iota(jnp.int32, (16, PIECE), 0)
     for k in range(NZ):
         block = head[48 * k : 48 * (k + 1)]
         at = BLOCK * k
-        out_ref[at : at + 48, :] = block[:, :512]
-        out_ref[at + 48 : at + 96, :] = block[:, 512:1024]
+        out_ref[at : at + 32, :] = block[:32, :PIECE].astype(BF16)
+        tail = block[32:, :PIECE]
+        for i, row in enumerate(extra):
+            tail = jnp.where(index == 12 + i, row, tail)
+        out_ref[at + 32 : at + 48, :] = tail.astype(BF16)
         for i in range(3):
-            out_ref[at + 96 : at + 112, 128 * i : 128 * (i + 1)] = block[16 * i : 16 * (i + 1), 1024:]
-        out_ref[at + 96 : at + 112, 384:] = jnp.zeros((16, 128), BF16)
-        out_ref[at + GAIN_AT : at + BLOCK, :] = packed
-
-
-def split_rows(gain, loss):
-    rows = [gain[:, :512], gain[:, 512:1024], jnp.concatenate([gain[:, 1024:], loss], axis=1)]
-    high = [r.astype(BF16).astype(F32) for r in rows]
-    low = [r - h for r, h in zip(rows, high)]
-    index = lax.broadcasted_iota(jnp.int32, (16, PIECE), 0)
-    packed = jnp.zeros((16, PIECE), F32)
-    for i, r in enumerate(high + low):
-        packed = jnp.where(index == i, r, packed)
-    return packed.astype(BF16)
+            side = block[16 * i : 16 * (i + 1), PIECE:].astype(BF16)
+            out_ref[at + 48 : at + 64, 256 * i : 256 * (i + 1)] = side
+        out_ref[at + 48 : at + 64, 768:] = jnp.zeros((16, 128), BF16)
 
 
 def reduce_kernel(got_ref, out_ref):
-    total = got_ref[...].astype(F32).reshape(N_GROUP * NZ, 8, PIECE).sum(axis=0)
-    rest = jnp.concatenate([total[3:], total[:3]], axis=0)
+    total = got_ref[...].astype(F32).reshape(8 * NZ, 8, PIECE).sum(axis=0)
     index = lax.broadcasted_iota(jnp.int32, (8, PIECE), 0)
-    whole = total + rest
-    high = whole.astype(BF16).astype(F32)
-    low = whole - high
-    moved = jnp.concatenate([low[5:], low[:5]], axis=0)
-    split = jnp.where(index < 3, high, jnp.where(index < 6, moved, 0.0))
-    group = lax.axis_index(HX) * 8 + lax.axis_index(Y)
-    piece = jnp.where(group == GAIN_AT // 8, split, total)
-    copies = jnp.broadcast_to(piece[None], (N_GROUP, 8, PIECE)).reshape(BLOCK, PIECE)
+    split = total
+    for i, row in enumerate(split_rows(total[4:5] + total[6:7], total[5:6] + total[7:8])):
+        split = jnp.where(index == 4 + i, row, split)
+    piece = jnp.where(lax.axis_index(Y) == 5, split, total)
+    copies = jnp.broadcast_to(piece[None], (N_GROUP, 8, PIECE)).reshape(8 * N_GROUP, PIECE)
     out_ref[...] = copies.astype(BF16)
 
 
 def unpack_kernel(got_ref, head_ref, gain_ref, loss_ref):
-    block = got_ref[...].astype(F32)
-    head_ref[:, :512] = block[:SHARE]
-    head_ref[:, 512:1024] = block[48 : 48 + SHARE]
-    tail = block[96:112]
-    head_ref[0:16, 1024:] = tail[:, 0:128]
-    head_ref[16:32, 1024:] = tail[:, 128:256]
-    head_ref[32:SHARE, 1024:] = tail[: SHARE - 32, 256:384]
-    rows = block[GAIN_AT : GAIN_AT + 3] + block[GAIN_AT + 3 : GAIN_AT + 6]
-    gain_ref[...] = jnp.concatenate([rows[0], rows[1], rows[2, :384]])
-    loss_ref[0] = jnp.max(rows[2:3, 384:]) * (1.0 / (N_GROUP * NZ * 4 * ROWS))
+    block = got_ref[:BLOCK, :].astype(F32) + got_ref[BLOCK:, :].astype(F32)
+    head_ref[:, :PIECE] = block[:SHARE]
+    head_ref[0:16, PIECE:] = block[48:64, 0:256]
+    head_ref[16:32, PIECE:] = block[48:64, 256:512]
+    head_ref[32:SHARE, PIECE:] = block[48 : 48 + SHARE - 32, 512:768]
+    rows = block[44:46] + block[46:48]
+    gain_ref[...] = jnp.concatenate([rows[0], rows[1, : W - PIECE]])
+    loss = rows[1:2, W - PIECE : W - PIECE + 128]
+    loss_ref[0] = jnp.max(loss) * (1.0 / (N_GROUP * NZ * 4 * ROWS))
 
 
 def per_device(pooled, captions, gain, w, scale, bias):
@@ -412,10 +405,10 @@
         mib=24,
         name="head",
     )
-    packed = lax.all_to_all(packed, (Z, HX, Y), 0, 0, tiled=True)
+    packed = lax.all_to_all(packed, (Z, Y), 0, 0, tiled=True)
     piece = call(
         reduce_kernel,
-        out((BLOCK, PIECE), BF16),
+        out((8 * N_GROUP, PIECE), BF16),
         packed,
         name="reduce",
     )

time: 146 us -> 141 us (0.966)
  blocking collectives: 61.2 us -> 56 us
    all_to_all x1, blocking collectives: 46.3 us -> 38.1 us  [per_device(): packed = lax.all_to_all(packed, (Z, Y), 0, 0, tiled=True)]
    all_to_all x1, blocking collectives: 14.9 us -> 17.9 us  [per_device(): block = lax.all_to_all(piece, (HX, Y), 0, 0, tiled=True)]
where the time goes in v5:
time: 141 us; the launch traced here: 140 us
  blocking collectives  56 us (40%)
  waiting for transfers between devices  32.3 us (23%)
  starting transfers between devices  32 us (23%)
  Pallas kernels  15.2 us (11%)
  local copies, waits for them, and re-layouts  2.65 us (2%)
  between operations  2.14 us (2%)
    all_to_all x1, blocking collectives, per_device(): packed = lax.all_to_all(packed, (Z, Y), 0, 0, tiled=True)  38.1 us
    all_to_all x1, blocking collectives, per_device(): block = lax.all_to_all(piece, (HX, Y), 0, 0, tiled=True)  17.9 us
    pallas_call x12, Pallas kernels, call(): pl.pallas_call(kernel, out_shape=out_shape, in_specs=specs or [VMEM] * le...  15.2 us
    ppermute x4, waiting for transfers between devices, per_device(): one = hop(one)  14 us
    ppermute x1, waiting for transfers between devices, per_device(): across(send)  13.8 us
    ppermute x4, starting transfers between devices, per_device(): one = hop(one)  10 us
    ppermute x3, starting transfers between devices, per_device(): two = hop(two)  9.26 us
    ppermute x1, starting transfers between devices, per_device(): across(n_here)  3.4 us
  transfers between devices with their start and end apart: 12, of which 8 were waited for; matrix products, arithmetic and copies ran while one was open for 0% of the time, Pallas kernels for 5%

profile of v5, /device:TPU:8, one launch (start us, length us, event | category | flops | bytes accessed | tf_op | source)
XLA Modules:
  0.0 140.3 jit_solution(12282949703090316320)
XLA Ops:
  0.6 0.0 copy-start.1
  0.6 1.0 copy-done.1
  1.6 0.0 copy-start.3
  1.6 1.0 copy-done.3
  2.6 0.0 copy-start.4
  2.6 0.7 copy-done.4
  3.3 0.3 prepare.1
  3.6 1.9 %collective-permute-start = (bf16[128,2560]{1,0:T(8,128)(2,1)S(1)}, bf16[128,2560]{1,0:T(8,128)(2,1)S(1)}, u32[]{:S(2)}, u32[]{:S(2)}) collective-permute-start(bf16[128,2560]{1,0:T(8,128)(2,1)S(1)} %get-tuple-element.23.own_ref), channel_id=1, source_target_pairs={{0,16},{16,0},{1,17},{17,1},{2,18},{18,2},{3,19},{19,3},{4,20},{20... | collective-permute-start | bytes 1966088 | tf_op jit(solution)/shard_map/ppermute | solution.py:297
  5.5 4.3 %collective-permute-start.2 = (bf16[128,1152]{1,0:T(8,128)(2,1)S(1)}, bf16[128,1152]{1,0:T(8,128)(2,1)S(1)}, u32[]{:S(2)}, u32[]{:S(2)}) collective-permute-start(bf16[128,1152]{1,0:T(8,128)(2,1)S(1)} %get-tuple-element.25.refs_0_), channel_id=1, source_target_pairs={{0,32},{16,240},{32,64},{48,16},{64,96},{80,48},{96,128},{112,80},... | collective-permute-start | bytes 884744 | tf_op jit(solution)/shard_map/ppermute | solution.py:303
  9.8 0.0 collective-permute-done.got_ref
  9.8 0.1 unpack_swap.1
  9.9 4.3 %collective-permute-start.5 = (bf16[128,1152]{1,0:T(8,128)(2,1)S(1)}, bf16[128,1152]{1,0:T(8,128)(2,1)S(1)}, u32[]{:S(2)}, u32[]{:S(2)}) collective-permute-start(bf16[128,1152]{1,0:T(8,128)(2,1)S(1)} %get-tuple-element.26), channel_id=1, source_target_pairs={{0,32},{16,240},{32,64},{48,16},{64,96},{80,48},{96,128},{112,80},... | collective-permute-start | bytes 884744 | tf_op jit(solution)/shard_map/ppermute | solution.py:308
  14.2 3.4 %collective-permute-start.1 = (bf16[256,1408]{1,0:T(8,128)(2,1)S(1)}, bf16[256,1408]{1,0:T(8,128)(2,1)S(1)}, u32[]{:S(2)}, u32[]{:S(2)}) collective-permute-start(bf16[256,1408]{1,0:T(8,128)(2,1)S(1)} %get-tuple-element.24.n_here), channel_id=1, source_target_pairs={{0,256},{256,0},{1,257},{257,1},{2,258},{258,2},{3,259},{259,3},{4... | collective-permute-start | bytes 2162696 | tf_op jit(solution)/shard_map/ppermute | solution.py:320
  17.6 3.6 %collective-permute-done.2.refs_1_ = bf16[128,1152]{1,0:T(8,128)(2,1)S(1)} collective-permute-done((bf16[128,1152]{1,0:T(8,128)(2,1)S(1)}, bf16[128,1152]{1,0:T(8,128)(2,1)S(1)}, u32[]{:S(2)}, u32[]{:S(2)}) %collective-permute-start.2) | collective-permute-done | bytes 294944 | tf_op jit(solution)/shard_map/ppermute | solution.py:303
  21.2 1.9 %collective-permute-start.3 = (bf16[128,1152]{1,0:T(8,128)(2,1)S(1)}, bf16[128,1152]{1,0:T(8,128)(2,1)S(1)}, u32[]{:S(2)}, u32[]{:S(2)}) collective-permute-start(bf16[128,1152]{1,0:T(8,128)(2,1)S(1)} %collective-permute-done.2.refs_1_), channel_id=1, source_target_pairs={{0,32},{16,240},{32,64},{48,16},{64,96},{80,48},{96,128},{112,80},... | collective-permute-start | bytes 884744 | tf_op jit(solution)/shard_map/ppermute | solution.py:303
  23.1 1.2 collective-permute-done.5.refs_2_
  24.3 3.1 %collective-permute-start.6 = (bf16[128,1152]{1,0:T(8,128)(2,1)S(1)}, bf16[128,1152]{1,0:T(8,128)(2,1)S(1)}, u32[]{:S(2)}, u32[]{:S(2)}) collective-permute-start(bf16[128,1152]{1,0:T(8,128)(2,1)S(1)} %collective-permute-done.5.refs_2_), channel_id=1, source_target_pairs={{0,32},{16,240},{32,64},{48,16},{64,96},{80,48},{96,128},{112,80},... | collective-permute-start | bytes 884744 | tf_op jit(solution)/shard_map/ppermute | solution.py:308
  27.4 3.6 %collective-permute-done.3.refs_3_ = bf16[128,1152]{1,0:T(8,128)(2,1)S(1)} collective-permute-done((bf16[128,1152]{1,0:T(8,128)(2,1)S(1)}, bf16[128,1152]{1,0:T(8,128)(2,1)S(1)}, u32[]{:S(2)}, u32[]{:S(2)}) %collective-permute-start.3) | collective-permute-done | bytes 294944 | tf_op jit(solution)/shard_map/ppermute | solution.py:303
  31.0 1.9 %collective-permute-start.4 = (bf16[128,1152]{1,0:T(8,128)(2,1)S(1)}, bf16[128,1152]{1,0:T(8,128)(2,1)S(1)}, u32[]{:S(2)}, u32[]{:S(2)}) collective-permute-start(bf16[128,1152]{1,0:T(8,128)(2,1)S(1)} %collective-permute-done.3.refs_3_), channel_id=1, source_target_pairs={{0,32},{16,240},{32,64},{48,16},{64,96},{80,48},{96,128},{112,80},... | collective-permute-start | bytes 884744 | tf_op jit(solution)/shard_map/ppermute | solution.py:303
  32.9 1.2 collective-permute-done.6.refs_4_
  34.2 1.9 %collective-permute-start.7 = (bf16[128,1152]{1,0:T(8,128)(2,1)S(1)}, bf16[128,1152]{1,0:T(8,128)(2,1)S(1)}, u32[]{:S(2)}, u32[]{:S(2)}) collective-permute-start(bf16[128,1152]{1,0:T(8,128)(2,1)S(1)} %collective-permute-done.6.refs_4_), channel_id=1, source_target_pairs={{0,32},{16,240},{32,64},{48,16},{64,96},{80,48},{96,128},{112,80},... | collective-permute-start | bytes 884744 | tf_op jit(solution)/shard_map/ppermute | solution.py:308
  37.4 3.4 %collective-permute-done.4.after_ref.refs_5_ = bf16[128,1152]{1,0:T(8,128)(2,1)S(1)} collective-permute-done((bf16[128,1152]{1,0:T(8,128)(2,1)S(1)}, bf16[128,1152]{1,0:T(8,128)(2,1)S(1)}, u32[]{:S(2)}, u32[]{:S(2)}) %collective-permute-start.4) | collective-permute-done | bytes 294944 | tf_op jit(solution)/shard_map/ppermute | solution.py:303
  40.8 1.9 %collective-permute-start.8 = (bf16[128,1152]{1,0:T(8,128)(2,1)S(1)}, bf16[128,1152]{1,0:T(8,128)(2,1)S(1)}, u32[]{:S(2)}, u32[]{:S(2)}) collective-permute-start(bf16[128,1152]{1,0:T(8,128)(2,1)S(1)} %collective-permute-done.4.after_ref.refs_5_), channel_id=1, source_target_pairs={{0,32},{16,240},{32,64},{48,16},{64,96},{80,48},{96,128},{112,80},... | collective-permute-start | bytes 884744 | tf_op jit(solution)/shard_map/ppermute | solution.py:303
  42.7 0.0 collective-permute-done.1.n_there
  42.7 4.3 %project.1 = (bf16[512,1152]{1,0:T(8,128)(2,1)S(1)}, f32[256,1152]{1,0:T(8,128)S(1)}, f32[256,128]{1,0:T(8,128)S(1)}, bf16[512,1408]{1,0:T(8,128)(2,1)S(1)}) custom-call(bf16[256,1408]{1,0:T(8,128)(2,1)S(1)} %get-tuple-element.24.n_here, bf16[256,1408]{1,0:T(8,128)(2,1)S(1)} %collective-permute-done.1.n_there, bf16[1408,1152]{1,0:T(8,128)(2,1)} %w_ref.5, ...), custom_call_target="tpu_custom_call" | custom-call | flops 1660944384 | bytes 8912896 | tf_op jit(solution)/shard_map/project/pallas_call | solution.py:37
  47.1 0.0 collective-permute-done.7.refs_6_
  47.1 0.2 collect.1.refs_0_
  47.2 3.4 %collective-permute-done.8.refs_1_ = bf16[128,1152]{1,0:T(8,128)(2,1)S(1)} collective-permute-done((bf16[128,1152]{1,0:T(8,128)(2,1)S(1)}, bf16[128,1152]{1,0:T(8,128)(2,1)S(1)}, u32[]{:S(2)}, u32[]{:S(2)}) %collective-permute-start.8) | collective-permute-done | bytes 294944 | tf_op jit(solution)/shard_map/ppermute | solution.py:303
  50.6 4.0 %pairs.1 = (f32[256,1152]{1,0:T(8,128)S(1)}, bf16[272,1152]{1,0:T(8,128)(2,1)S(1)}, f32[1,128]{1,0:T(1,128)S(1)}) custom-call(f32[1]{0:T(128)S(6)} %copy.10.scale_ref, f32[1]{0:T(128)S(6)} %copy.11.bias_ref, bf16[512,1152]{1,0:T(8,128)(2,1)S(1)} %get-tuple-element.28.img_ref, bf16[896,1152]{1,0:T(8,128)(2,1)S(1)} %collect.1.refs_0_, ...), custom_call_target="tpu_custom_call" | custom-call | flops 2415919104 | bytes 5345800 | tf_op jit(solution)/shard_map/pairs/pallas_call | solution.py:37
  54.7 1.9 %collective-permute-start.9 = (bf16[272,1152]{1,0:T(8,128)(2,1)S(1)}, bf16[272,1152]{1,0:T(8,128)(2,1)S(1)}, u32[]{:S(2)}, u32[]{:S(2)}) collective-permute-start(bf16[272,1152]{1,0:T(8,128)(2,1)S(1)} %get-tuple-element.31), channel_id=1, source_target_pairs={{0,16},{16,0},{1,17},{17,1},{2,18},{18,2},{3,19},{19,3},{4,20},{20... | collective-permute-start | bytes 1880072 | tf_op jit(solution)/shard_map/ppermute | solution.py:346
  56.6 2.0 %collective-permute-done.9.got_ref.core_ref = bf16[272,1152]{1,0:T(8,128)(2,1)S(1)} collective-permute-done((bf16[272,1152]{1,0:T(8,128)(2,1)S(1)}, bf16[272,1152]{1,0:T(8,128)(2,1)S(1)}, u32[]{:S(2)}, u32[]{:S(2)}) %collective-permute-start.9) | collective-permute-done | bytes 626720 | tf_op jit(solution)/shard_map/ppermute | solution.py:346
  58.6 0.1 add_cores.1.after_ref
  58.7 3.4 %collective-permute-start.10 = (bf16[272,1152]{1,0:T(8,128)(2,1)S(1)}, bf16[272,1152]{1,0:T(8,128)(2,1)S(1)}, u32[]{:S(2)}, u32[]{:S(2)}) collective-permute-start(bf16[272,1152]{1,0:T(8,128)(2,1)S(1)} %add_cores.1.after_ref), channel_id=1, source_target_pairs={{0,256},{256,0},{1,257},{257,1},{2,258},{258,2},{3,259},{259,3},{4... | collective-permute-start | bytes 1880072 | tf_op jit(solution)/shard_map/ppermute | solution.py:372
  62.1 0.8 pick.1.after_ref.pick_ref
  63.0 13.8 %collective-permute-done.10.got_ref = bf16[272,1152]{1,0:T(8,128)(2,1)S(1)} collective-permute-done((bf16[272,1152]{1,0:T(8,128)(2,1)S(1)}, bf16[272,1152]{1,0:T(8,128)(2,1)S(1)}, u32[]{:S(2)}, u32[]{:S(2)}) %collective-permute-start.10) | collective-permute-done | bytes 626720 | tf_op jit(solution)/shard_map/ppermute | solution.py:372
  76.8 0.0 copy-start
  76.8 0.5 d_proj.1
  77.3 2.1 %collective-permute-start.11 = (bf16[256,1152]{1,0:T(8,128)(2,1)S(1)}, bf16[256,1152]{1,0:T(8,128)(2,1)S(1)}, u32[]{:S(2)}, u32[]{:S(2)}) collective-permute-start(bf16[256,1152]{1,0:T(8,128)(2,1)S(1)} %get-tuple-element.35.dproj_ref.own_ref), channel_id=1, source_target_pairs={{0,16},{16,0},{1,17},{17,1},{2,18},{18,2},{3,19},{19,3},{4,20},{20... | collective-permute-start | bytes 1769480 | tf_op jit(solution)/shard_map/ppermute | solution.py:380
  79.4 0.0 copy-done
  79.4 0.0 copy-done.2
  79.4 0.0 copy-done.5
  79.4 2.2 %d_features.1 = (bf16[128,1408]{1,0:T(8,128)(2,1)}, f32[1,1408]{1,0:T(1,128)S(1)}) custom-call(bf16[256,1152]{1,0:T(8,128)(2,1)S(1)} %get-tuple-element.35.dproj_ref.own_ref, bf16[128,1408]{1,0:T(8,128)(2,1)S(1)} %bitcast.11, f32[1408]{0:T(1024)S(1)} %copy-done.5, bf16[512,1408]{1,0:T(8,128)(2,1)S(1)} %get-tuple-element.34.rows_ref, ...), custom_call_target="tpu_custom_call" | custom-call | flops 830472192 | bytes 6007808 | tf_op jit(solution)/shard_map/d_features/pallas_call | solution.py:37
  81.6 0.0 collective-permute-done.11.got_ref
  81.6 1.8 %head.1 = bf16[512,896]{1,0:T(8,128)(2,1)S(1)} custom-call(bf16[256,1152]{1,0:T(8,128)(2,1)S(1)} %get-tuple-element.35.dproj_ref.own_ref, bf16[256,1152]{1,0:T(8,128)(2,1)S(1)} %collective-permute-done.11.got_ref, bf16[384,512]{1,0:T(8,128)(2,1)S(1)} %pick.1.after_ref.pick_ref, bf16[512,1408]{1,0:T(8,128)(2,1)S(1)} %get-tuple-element.34.rows_ref, ...), custom_call_target="tpu_custom_call" | custom-call | flops 1283457024 | bytes 7187968 | tf_op jit(solution)/shard_map/head/pallas_call | solution.py:37
  83.4 38.1 %all_to_all.22 = bf16[64,8,896]{2,1,0:T(8,128)(2,1)S(1)} all-to-all(bf16[64,8,896]{2,1,0:T(8,128)(2,1)S(1)} %bitcast.9), channel_id=1, replica_groups=mesh['x'=2,'z'=8,'c'=2,'hx'=2,'y'=8] {'z','y'}, dimensions={0} | all-to-all | bytes 1835008 | tf_op jit(solution)/shard_map/all_to_all | solution.py:408
  121.5 0.2 reduce.1
  121.7 17.9 %all_to_all.23 = bf16[16,8,896]{2,1,0:T(8,128)(2,1)S(1)} all-to-all(bf16[16,8,896]{2,1,0:T(8,128)(2,1)S(1)} %bitcast.13), channel_id=1, replica_groups=mesh['x'=2,'z'=8,'c'=2,'hx'=2,'y'=8] {'hx','y'}, dimensions={0} | all-to-all | bytes 458752 | tf_op jit(solution)/shard_map/all_to_all | solution.py:415
  139.5 0.7 unpack.1
  (2 shorter events, 0.0 us)
Async XLA Ops:
  0.6 1.0 copy-start.1
  1.6 1.0 copy-start.3
  2.6 0.7 copy-start.4
  3.6 6.2 %collective-permute-start = (bf16[128,2560]{1,0:T(8,128)(2,1)S(1)}, bf16[128,2560]{1,0:T(8,128)(2,1)S(1)}, u32[]{:S(2)}, u32[]{:S(2)}) collective-permute-start(bf16[128,2560]{1,0:T(8,128)(2,1)S(1)} %get-tuple-element.23.own_ref), channel_id=1, source_target_pairs={{0,16},{16,0},{1,17},{17,1},{2,18},{18,2},{3,19},{19,3},{4,20},{20... | collective-permute-start | bytes 1966088 | tf_op jit(solution)/shard_map/ppermute | solution.py:297
  5.5 15.6 %collective-permute-start.2 = (bf16[128,1152]{1,0:T(8,128)(2,1)S(1)}, bf16[128,1152]{1,0:T(8,128)(2,1)S(1)}, u32[]{:S(2)}, u32[]{:S(2)}) collective-permute-start(bf16[128,1152]{1,0:T(8,128)(2,1)S(1)} %get-tuple-element.25.refs_0_), channel_id=1, source_target_pairs={{0,32},{16,240},{32,64},{48,16},{64,96},{80,48},{96,128},{112,80},... | collective-permute-start | bytes 884744 | tf_op jit(solution)/shard_map/ppermute | solution.py:303
  9.9 14.4 %collective-permute-start.5 = (bf16[128,1152]{1,0:T(8,128)(2,1)S(1)}, bf16[128,1152]{1,0:T(8,128)(2,1)S(1)}, u32[]{:S(2)}, u32[]{:S(2)}) collective-permute-start(bf16[128,1152]{1,0:T(8,128)(2,1)S(1)} %get-tuple-element.26), channel_id=1, source_target_pairs={{0,32},{16,240},{32,64},{48,16},{64,96},{80,48},{96,128},{112,80},... | collective-permute-start | bytes 884744 | tf_op jit(solution)/shard_map/ppermute | solution.py:308
  14.2 28.5 %collective-permute-start.1 = (bf16[256,1408]{1,0:T(8,128)(2,1)S(1)}, bf16[256,1408]{1,0:T(8,128)(2,1)S(1)}, u32[]{:S(2)}, u32[]{:S(2)}) collective-permute-start(bf16[256,1408]{1,0:T(8,128)(2,1)S(1)} %get-tuple-element.24.n_here), channel_id=1, source_target_pairs={{0,256},{256,0},{1,257},{257,1},{2,258},{258,2},{3,259},{259,3},{4... | collective-permute-start | bytes 2162696 | tf_op jit(solution)/shard_map/ppermute | solution.py:320
  21.2 9.8 %collective-permute-start.3 = (bf16[128,1152]{1,0:T(8,128)(2,1)S(1)}, bf16[128,1152]{1,0:T(8,128)(2,1)S(1)}, u32[]{:S(2)}, u32[]{:S(2)}) collective-permute-start(bf16[128,1152]{1,0:T(8,128)(2,1)S(1)} %collective-permute-done.2.refs_1_), channel_id=1, source_target_pairs={{0,32},{16,240},{32,64},{48,16},{64,96},{80,48},{96,128},{112,80},... | collective-permute-start | bytes 884744 | tf_op jit(solution)/shard_map/ppermute | solution.py:303
  24.3 9.8 %collective-permute-start.6 = (bf16[128,1152]{1,0:T(8,128)(2,1)S(1)}, bf16[128,1152]{1,0:T(8,128)(2,1)S(1)}, u32[]{:S(2)}, u32[]{:S(2)}) collective-permute-start(bf16[128,1152]{1,0:T(8,128)(2,1)S(1)} %collective-permute-done.5.refs_2_), channel_id=1, source_target_pairs={{0,32},{16,240},{32,64},{48,16},{64,96},{80,48},{96,128},{112,80},... | collective-permute-start | bytes 884744 | tf_op jit(solution)/shard_map/ppermute | solution.py:308
  31.0 9.8 %collective-permute-start.4 = (bf16[128,1152]{1,0:T(8,128)(2,1)S(1)}, bf16[128,1152]{1,0:T(8,128)(2,1)S(1)}, u32[]{:S(2)}, u32[]{:S(2)}) collective-permute-start(bf16[128,1152]{1,0:T(8,128)(2,1)S(1)} %collective-permute-done.3.refs_3_), channel_id=1, source_target_pairs={{0,32},{16,240},{32,64},{48,16},{64,96},{80,48},{96,128},{112,80},... | collective-permute-start | bytes 884744 | tf_op jit(solution)/shard_map/ppermute | solution.py:303
  34.2 12.9 %collective-permute-start.7 = (bf16[128,1152]{1,0:T(8,128)(2,1)S(1)}, bf16[128,1152]{1,0:T(8,128)(2,1)S(1)}, u32[]{:S(2)}, u32[]{:S(2)}) collective-permute-start(bf16[128,1152]{1,0:T(8,128)(2,1)S(1)} %collective-permute-done.6.refs_4_), channel_id=1, source_target_pairs={{0,32},{16,240},{32,64},{48,16},{64,96},{80,48},{96,128},{112,80},... | collective-permute-start | bytes 884744 | tf_op jit(solution)/shard_map/ppermute | solution.py:308
  40.8 9.8 %collective-permute-start.8 = (bf16[128,1152]{1,0:T(8,128)(2,1)S(1)}, bf16[128,1152]{1,0:T(8,128)(2,1)S(1)}, u32[]{:S(2)}, u32[]{:S(2)}) collective-permute-start(bf16[128,1152]{1,0:T(8,128)(2,1)S(1)} %collective-permute-done.4.after_ref.refs_5_), channel_id=1, source_target_pairs={{0,32},{16,240},{32,64},{48,16},{64,96},{80,48},{96,128},{112,80},... | collective-permute-start | bytes 884744 | tf_op jit(solution)/shard_map/ppermute | solution.py:303
  54.7 4.0 %collective-permute-start.9 = (bf16[272,1152]{1,0:T(8,128)(2,1)S(1)}, bf16[272,1152]{1,0:T(8,128)(2,1)S(1)}, u32[]{:S(2)}, u32[]{:S(2)}) collective-permute-start(bf16[272,1152]{1,0:T(8,128)(2,1)S(1)} %get-tuple-element.31), channel_id=1, source_target_pairs={{0,16},{16,0},{1,17},{17,1},{2,18},{18,2},{3,19},{19,3},{4,20},{20... | collective-permute-start | bytes 1880072 | tf_op jit(solution)/shard_map/ppermute | solution.py:346
  58.7 18.1 %collective-permute-start.10 = (bf16[272,1152]{1,0:T(8,128)(2,1)S(1)}, bf16[272,1152]{1,0:T(8,128)(2,1)S(1)}, u32[]{:S(2)}, u32[]{:S(2)}) collective-permute-start(bf16[272,1152]{1,0:T(8,128)(2,1)S(1)} %add_cores.1.after_ref), channel_id=1, source_target_pairs={{0,256},{256,0},{1,257},{257,1},{2,258},{258,2},{3,259},{259,3},{4... | collective-permute-start | bytes 1880072 | tf_op jit(solution)/shard_map/ppermute | solution.py:372
  76.8 2.6 %copy-start = (bf16[1408,1152]{1,0:T(8,128)(2,1)S(1)}, bf16[1408,1152]{1,0:T(8,128)(2,1)}, u32[]{:S(2)}) copy-start(bf16[1408,1152]{1,0:T(8,128)(2,1)} %w_ref.5) | copy-start | bytes 9732100
  76.8 2.6 %copy-start.2 = (bf16[1,128,1408]{2,1,0:T(8,128)(2,1)S(1)}, bf16[1,128,1408]{2,1,0:T(8,128)(2,1)}, u32[]{:S(2)}) copy-start(bf16[1,128,1408]{2,1,0:T(8,128)(2,1)} %param.6) | copy-start | bytes 1081348
  76.8 2.6 %copy-start.5 = (f32[1408]{0:T(1024)S(1)}, f32[1408]{0:T(1024)}, u32[]{:S(2)}) copy-start(f32[1408]{0:T(1024)} %gain_ref.5) | copy-start | bytes 16900
  77.3 4.3 %collective-permute-start.11 = (bf16[256,1152]{1,0:T(8,128)(2,1)S(1)}, bf16[256,1152]{1,0:T(8,128)(2,1)S(1)}, u32[]{:S(2)}, u32[]{:S(2)}) collective-permute-start(bf16[256,1152]{1,0:T(8,128)(2,1)S(1)} %get-tuple-element.35.dproj_ref.own_ref), channel_id=1, source_target_pairs={{0,16},{16,0},{1,17},{17,1},{2,18},{18,2},{3,19},{19,3},{4,20},{20... | collective-permute-start | bytes 1769480 | tf_op jit(solution)/shard_map/ppermute | solution.py:380

commit v6 on v5

--- a/solution.py
+++ b/solution.py
@@ -26,6 +26,8 @@
 HOP = [
     (z * 2 + c, ((z + (1 if c == 0 else -1)) % NZ) * 2 + c) for z in range(NZ) for c in range(2)
 ]
+
+HOP_BACK = [(there, here) for here, there in HOP]
 
 VMEM = pl.BlockSpec(memory_space=pltpu.VMEM)
 SMEM = pl.BlockSpec(memory_space=pltpu.SMEM)
@@ -57,20 +59,20 @@
     return centred * scale, scale
 
 
-def prepare_kernel(cap_ref, x_ref, gain_ref, text_ref, both_ref):
+def text_kernel(cap_ref, text_ref):
     values = cap_ref[...].astype(F32)
     scale = lax.rsqrt(jnp.sum(values * values, axis=1, keepdims=True) + EPSILON)
-    text = (values * scale).astype(BF16)
-    text_ref[...] = text
-    both_ref[:, :E] = text
+    text_ref[...] = (values * scale).astype(BF16)
+
+
+def norm_kernel(x_ref, gain_ref, normed_ref):
     x_hat, _ = moments(x_ref[...].astype(F32))
-    both_ref[:, E:] = (x_hat * gain_ref[...].reshape(1, W)).astype(BF16)
-
-
-def unpack_swap_kernel(own_ref, got_ref, text_ref, normed_ref):
-    text_ref[...] = got_ref[:, :E]
-    normed_ref[:ROWS, :] = own_ref[:, E:]
-    normed_ref[ROWS:, :] = got_ref[:, E:]
+    normed_ref[...] = (x_hat * gain_ref[...].reshape(1, W)).astype(BF16)
+
+
+def join_kernel(own_ref, got_ref, both_ref):
+    both_ref[:ROWS, :] = own_ref[...]
+    both_ref[ROWS:, :] = got_ref[...]
 
 
 def collect_kernel(*refs):
@@ -281,33 +283,20 @@
     across = functools.partial(lax.ppermute, axis_name=X, perm=SWAP)
     between = functools.partial(lax.ppermute, axis_name=C, perm=SWAP)
     hop = functools.partial(lax.ppermute, axis_name=(Z, C), perm=HOP)
-
-    text, both = call(
-        prepare_kernel,
-        (out((ROWS, E), BF16), out((ROWS, E + W), BF16)),
-        captions[0],
-        x,
-        gain,
-        name="prepare",
-    )
-    swapped, n_here = call(
-        unpack_swap_kernel,
-        (out((ROWS, E), BF16), out((2 * ROWS, W), BF16)),
-        both,
-        between(both),
-        name="unpack_swap",
-    )
+    hop_back = functools.partial(lax.ppermute, axis_name=(Z, C), perm=HOP_BACK)
+
+    text = call(text_kernel, out((ROWS, E), BF16), captions[0], name="text_unit")
     texts = [text]
-    one, two = text, swapped
+    one, two = text, text
     for step in range(4):
         one = hop(one)
-        if step == 0:
-            one, swapped = lax.optimization_barrier((one, swapped))
         texts.append(one)
         if step < 3:
-            two = hop(two)
+            two = hop_back(two)
             texts.append(two)
 
+    n0 = call(norm_kernel, out((ROWS, W), BF16), x, gain, name="normed")
+    n_here = call(join_kernel, out((2 * ROWS, W), BF16), n0, between(n0), name="join")
     img, unit, pnorm, rows = call(
         project_kernel,
         (

time: 141 us -> 145 us (1.028)
  starting transfers between devices: 32 us -> 41.7 us
  waiting for transfers between devices: 32.3 us -> 22.6 us
  blocking collectives: 56 us -> 59.5 us
    ppermute x4, waiting for transfers between devices: 14 us -> 4.13 us  [per_device(): one = hop(one)]
    ppermute x4, starting transfers between devices: 11.2 us -> 20.9 us  [the longest x3 19 us: per_device(): two = hop_back(two)]
    all_to_all x1, blocking collectives: 38.1 us -> 41.3 us  [per_device(): packed = lax.all_to_all(packed, (Z, Y), 0, 0, tiled=True)]
    ppermute x1, waiting for transfers between devices: 0.01 us -> 2.6 us  [per_device(): across(n_here)]
    ppermute x4, waiting for transfers between devices: 2.49 us -> 0.01 us  [the longest x3 0.01 us: per_device(): two = hop_back(two)]
    pallas_call x12 -> x13, Pallas kernels: 15.2 us -> 15.3 us  [call(): pl.pallas_call(kernel, out_shape=out_shape, in_specs=specs or [VMEM] * le...]
  transfers between devices with their start and end apart: 12 -> 12, of which waited for: 8 -> 5; matrix products, arithmetic and copies ran while one was open for 0% -> 0% of each run, Pallas kernels for 5% -> 5%
where the time goes in v6:
time: 145 us; the launch traced here: 144 us
  blocking collectives  59.5 us (41%)
  starting transfers between devices  41.7 us (29%)
  waiting for transfers between devices  22.6 us (16%)
  Pallas kernels  15.3 us (11%)
  local copies, waits for them, and re-layouts  2.64 us (2%)
  between operations  2.18 us (2%)
    all_to_all x1, blocking collectives, per_device(): packed = lax.all_to_all(packed, (Z, Y), 0, 0, tiled=True)  41.3 us
    ppermute x3, starting transfers between devices, per_device(): two = hop_back(two)  19 us
    all_to_all x1, blocking collectives, per_device(): block = lax.all_to_all(piece, (HX, Y), 0, 0, tiled=True)  18.2 us
    pallas_call x13, Pallas kernels, call(): pl.pallas_call(kernel, out_shape=out_shape, in_specs=specs or [VMEM] * le...  15.3 us
    ppermute x1, waiting for transfers between devices, per_device(): across(send)  13.8 us
    ppermute x4, starting transfers between devices, per_device(): one = hop(one)  10 us
    ppermute x4, waiting for transfers between devices, per_device(): one = hop(one)  4.13 us
    ppermute x1, starting transfers between devices, per_device(): across(n_here)  3.4 us
  transfers between devices with their start and end apart: 12, of which 5 were waited for; matrix products, arithmetic and copies ran while one was open for 0% of the time, Pallas kernels for 5%

profile of v6, /device:TPU:8, one launch (start us, length us, event | category | flops | bytes accessed | tf_op | source)
XLA Modules:
  0.0 143.9 jit_solution(7068637090316627946)
XLA Ops:
  0.6 0.0 copy-start.3
  0.6 1.0 copy-done.3
  1.6 0.1 text_unit.1.refs_0_
  1.7 4.3 %collective-permute-start.2 = (bf16[128,1152]{1,0:T(8,128)(2,1)S(1)}, bf16[128,1152]{1,0:T(8,128)(2,1)S(1)}, u32[]{:S(2)}, u32[]{:S(2)}) collective-permute-start(bf16[128,1152]{1,0:T(8,128)(2,1)S(1)} %text_unit.1.refs_0_), channel_id=1, source_target_pairs={{0,32},{16,240},{32,64},{48,16},{64,96},{80,48},{96,128},{112,80},... | collective-permute-start | bytes 884744 | tf_op jit(solution)/shard_map/ppermute | solution.py:292
  6.0 8.6 %collective-permute-start.5 = (bf16[128,1152]{1,0:T(8,128)(2,1)S(1)}, bf16[128,1152]{1,0:T(8,128)(2,1)S(1)}, u32[]{:S(2)}, u32[]{:S(2)}) collective-permute-start(bf16[128,1152]{1,0:T(8,128)(2,1)S(1)} %text_unit.1.refs_0_), channel_id=1, source_target_pairs={{32,0},{240,16},{64,32},{16,48},{96,64},{48,80},{128,96},{80,112},... | collective-permute-start | bytes 884744 | tf_op jit(solution)/shard_map/ppermute | solution.py:295
  14.6 0.0 copy-start.1
  14.6 1.0 copy-done.1
  15.6 0.7 copy-done.4
  16.3 0.3 normed.1.own_ref
  16.6 1.9 %collective-permute-start = (bf16[128,1408]{1,0:T(8,128)(2,1)S(1)}, bf16[128,1408]{1,0:T(8,128)(2,1)S(1)}, u32[]{:S(2)}, u32[]{:S(2)}) collective-permute-start(bf16[128,1408]{1,0:T(8,128)(2,1)S(1)} %normed.1.own_ref), channel_id=1, source_target_pairs={{0,16},{16,0},{1,17},{17,1},{2,18},{18,2},{3,19},{19,3},{4,20},{20... | collective-permute-start | bytes 1081352 | tf_op jit(solution)/shard_map/ppermute | solution.py:299
  18.5 0.0 collective-permute-done.2.refs_1_
  18.5 1.9 %collective-permute-start.3 = (bf16[128,1152]{1,0:T(8,128)(2,1)S(1)}, bf16[128,1152]{1,0:T(8,128)(2,1)S(1)}, u32[]{:S(2)}, u32[]{:S(2)}) collective-permute-start(bf16[128,1152]{1,0:T(8,128)(2,1)S(1)} %collective-permute-done.2.refs_1_), channel_id=1, source_target_pairs={{0,32},{16,240},{32,64},{48,16},{64,96},{80,48},{96,128},{112,80},... | collective-permute-start | bytes 884744 | tf_op jit(solution)/shard_map/ppermute | solution.py:292
  20.5 0.0 collective-permute-done.5.refs_2_
  20.5 5.1 %collective-permute-start.6 = (bf16[128,1152]{1,0:T(8,128)(2,1)S(1)}, bf16[128,1152]{1,0:T(8,128)(2,1)S(1)}, u32[]{:S(2)}, u32[]{:S(2)}) collective-permute-start(bf16[128,1152]{1,0:T(8,128)(2,1)S(1)} %collective-permute-done.5.refs_2_), channel_id=1, source_target_pairs={{32,0},{240,16},{64,32},{16,48},{96,64},{48,80},{128,96},{80,112},... | collective-permute-start | bytes 884744 | tf_op jit(solution)/shard_map/ppermute | solution.py:295
  25.6 0.0 collective-permute-done.got_ref
  25.6 0.1 join.1.n_here
  25.7 3.4 %collective-permute-start.1 = (bf16[256,1408]{1,0:T(8,128)(2,1)S(1)}, bf16[256,1408]{1,0:T(8,128)(2,1)S(1)}, u32[]{:S(2)}, u32[]{:S(2)}) collective-permute-start(bf16[256,1408]{1,0:T(8,128)(2,1)S(1)} %join.1.n_here), channel_id=1, source_target_pairs={{0,256},{256,0},{1,257},{257,1},{2,258},{258,2},{3,259},{259,3},{4... | collective-permute-start | bytes 2162696 | tf_op jit(solution)/shard_map/ppermute | solution.py:309
  29.1 0.0 collective-permute-done.3.refs_3_
  29.1 1.9 %collective-permute-start.4 = (bf16[128,1152]{1,0:T(8,128)(2,1)S(1)}, bf16[128,1152]{1,0:T(8,128)(2,1)S(1)}, u32[]{:S(2)}, u32[]{:S(2)}) collective-permute-start(bf16[128,1152]{1,0:T(8,128)(2,1)S(1)} %collective-permute-done.3.refs_3_), channel_id=1, source_target_pairs={{0,32},{16,240},{32,64},{48,16},{64,96},{80,48},{96,128},{112,80},... | collective-permute-start | bytes 884744 | tf_op jit(solution)/shard_map/ppermute | solution.py:292
  31.0 0.0 collective-permute-done.6.refs_4_
  31.1 5.3 %collective-permute-start.7 = (bf16[128,1152]{1,0:T(8,128)(2,1)S(1)}, bf16[128,1152]{1,0:T(8,128)(2,1)S(1)}, u32[]{:S(2)}, u32[]{:S(2)}) collective-permute-start(bf16[128,1152]{1,0:T(8,128)(2,1)S(1)} %collective-permute-done.6.refs_4_), channel_id=1, source_target_pairs={{32,0},{240,16},{64,32},{16,48},{96,64},{48,80},{128,96},{80,112},... | collective-permute-start | bytes 884744 | tf_op jit(solution)/shard_map/ppermute | solution.py:295
  37.6 2.3 %collective-permute-done.4.after_ref.refs_5_ = bf16[128,1152]{1,0:T(8,128)(2,1)S(1)} collective-permute-done((bf16[128,1152]{1,0:T(8,128)(2,1)S(1)}, bf16[128,1152]{1,0:T(8,128)(2,1)S(1)}, u32[]{:S(2)}, u32[]{:S(2)}) %collective-permute-start.4) | collective-permute-done | bytes 294944 | tf_op jit(solution)/shard_map/ppermute | solution.py:292
  40.0 1.9 %collective-permute-start.8 = (bf16[128,1152]{1,0:T(8,128)(2,1)S(1)}, bf16[128,1152]{1,0:T(8,128)(2,1)S(1)}, u32[]{:S(2)}, u32[]{:S(2)}) collective-permute-start(bf16[128,1152]{1,0:T(8,128)(2,1)S(1)} %collective-permute-done.4.after_ref.refs_5_), channel_id=1, source_target_pairs={{0,32},{16,240},{32,64},{48,16},{64,96},{80,48},{96,128},{112,80},... | collective-permute-start | bytes 884744 | tf_op jit(solution)/shard_map/ppermute | solution.py:292
  41.9 0.0 collective-permute-done.7.refs_6_
  41.9 0.2 collect.1.refs_0_
  42.0 2.6 %collective-permute-done.1.n_there = bf16[256,1408]{1,0:T(8,128)(2,1)S(1)} collective-permute-done((bf16[256,1408]{1,0:T(8,128)(2,1)S(1)}, bf16[256,1408]{1,0:T(8,128)(2,1)S(1)}, u32[]{:S(2)}, u32[]{:S(2)}) %collective-permute-start.1) | collective-permute-done | bytes 720928 | tf_op jit(solution)/shard_map/ppermute | solution.py:309
  44.6 4.3 %project.1 = (bf16[512,1152]{1,0:T(8,128)(2,1)S(1)}, f32[256,1152]{1,0:T(8,128)S(1)}, f32[256,128]{1,0:T(8,128)S(1)}, bf16[512,1408]{1,0:T(8,128)(2,1)S(1)}) custom-call(bf16[256,1408]{1,0:T(8,128)(2,1)S(1)} %join.1.n_here, bf16[256,1408]{1,0:T(8,128)(2,1)S(1)} %collective-permute-done.1.n_there, bf16[1408,1152]{1,0:T(8,128)(2,1)} %w_ref.5, ...), custom_call_target="tpu_custom_call" | custom-call | flops 1660944384 | bytes 8912896 | tf_op jit(solution)/shard_map/project/pallas_call | solution.py:39
  49.0 1.8 %collective-permute-done.8.refs_1_ = bf16[128,1152]{1,0:T(8,128)(2,1)S(1)} collective-permute-done((bf16[128,1152]{1,0:T(8,128)(2,1)S(1)}, bf16[128,1152]{1,0:T(8,128)(2,1)S(1)}, u32[]{:S(2)}, u32[]{:S(2)}) %collective-permute-start.8) | collective-permute-done | bytes 294944 | tf_op jit(solution)/shard_map/ppermute | solution.py:292
  50.8 4.0 %pairs.1 = (f32[256,1152]{1,0:T(8,128)S(1)}, bf16[272,1152]{1,0:T(8,128)(2,1)S(1)}, f32[1,128]{1,0:T(1,128)S(1)}) custom-call(f32[1]{0:T(128)S(6)} %copy.10.scale_ref, f32[1]{0:T(128)S(6)} %copy.11.bias_ref, bf16[512,1152]{1,0:T(8,128)(2,1)S(1)} %get-tuple-element.18.img_ref, bf16[896,1152]{1,0:T(8,128)(2,1)S(1)} %collect.1.refs_0_, ...), custom_call_target="tpu_custom_call" | custom-call | flops 2415919104 | bytes 5345800 | tf_op jit(solution)/shard_map/pairs/pallas_call | solution.py:39
  54.8 1.9 %collective-permute-start.9 = (bf16[272,1152]{1,0:T(8,128)(2,1)S(1)}, bf16[272,1152]{1,0:T(8,128)(2,1)S(1)}, u32[]{:S(2)}, u32[]{:S(2)}) collective-permute-start(bf16[272,1152]{1,0:T(8,128)(2,1)S(1)} %get-tuple-element.21), channel_id=1, source_target_pairs={{0,16},{16,0},{1,17},{17,1},{2,18},{18,2},{3,19},{19,3},{4,20},{20... | collective-permute-start | bytes 1880072 | tf_op jit(solution)/shard_map/ppermute | solution.py:335
  56.7 2.0 %collective-permute-done.9.got_ref.core_ref = bf16[272,1152]{1,0:T(8,128)(2,1)S(1)} collective-permute-done((bf16[272,1152]{1,0:T(8,128)(2,1)S(1)}, bf16[272,1152]{1,0:T(8,128)(2,1)S(1)}, u32[]{:S(2)}, u32[]{:S(2)}) %collective-permute-start.9) | collective-permute-done | bytes 626720 | tf_op jit(solution)/shard_map/ppermute | solution.py:335
  58.7 0.1 add_cores.1.after_ref
  58.9 3.4 %collective-permute-start.10 = (bf16[272,1152]{1,0:T(8,128)(2,1)S(1)}, bf16[272,1152]{1,0:T(8,128)(2,1)S(1)}, u32[]{:S(2)}, u32[]{:S(2)}) collective-permute-start(bf16[272,1152]{1,0:T(8,128)(2,1)S(1)} %add_cores.1.after_ref), channel_id=1, source_target_pairs={{0,256},{256,0},{1,257},{257,1},{2,258},{258,2},{3,259},{259,3},{4... | collective-permute-start | bytes 1880072 | tf_op jit(solution)/shard_map/ppermute | solution.py:361
  62.3 0.8 pick.1.after_ref.pick_ref
  63.1 13.8 %collective-permute-done.10.got_ref = bf16[272,1152]{1,0:T(8,128)(2,1)S(1)} collective-permute-done((bf16[272,1152]{1,0:T(8,128)(2,1)S(1)}, bf16[272,1152]{1,0:T(8,128)(2,1)S(1)}, u32[]{:S(2)}, u32[]{:S(2)}) %collective-permute-start.10) | collective-permute-done | bytes 626720 | tf_op jit(solution)/shard_map/ppermute | solution.py:361
  76.9 0.0 copy-start
  76.9 0.5 d_proj.1
  77.4 2.1 %collective-permute-start.11 = (bf16[256,1152]{1,0:T(8,128)(2,1)S(1)}, bf16[256,1152]{1,0:T(8,128)(2,1)S(1)}, u32[]{:S(2)}, u32[]{:S(2)}) collective-permute-start(bf16[256,1152]{1,0:T(8,128)(2,1)S(1)} %get-tuple-element.25.dproj_ref.own_ref), channel_id=1, source_target_pairs={{0,16},{16,0},{1,17},{17,1},{2,18},{18,2},{3,19},{19,3},{4,20},{20... | collective-permute-start | bytes 1769480 | tf_op jit(solution)/shard_map/ppermute | solution.py:369
  79.5 0.0 copy-done
  79.5 0.0 copy-done.2
  79.5 0.0 copy-done.5
  79.5 2.2 %d_features.1 = (bf16[128,1408]{1,0:T(8,128)(2,1)}, f32[1,1408]{1,0:T(1,128)S(1)}) custom-call(bf16[256,1152]{1,0:T(8,128)(2,1)S(1)} %get-tuple-element.25.dproj_ref.own_ref, bf16[128,1408]{1,0:T(8,128)(2,1)S(1)} %bitcast.11, f32[1408]{0:T(1024)S(1)} %copy-done.5, bf16[512,1408]{1,0:T(8,128)(2,1)S(1)} %get-tuple-element.24.rows_ref, ...), custom_call_target="tpu_custom_call" | custom-call | flops 830472192 | bytes 6007808 | tf_op jit(solution)/shard_map/d_features/pallas_call | solution.py:39
  81.7 0.0 collective-permute-done.11.got_ref
  81.7 1.8 %head.1 = bf16[512,896]{1,0:T(8,128)(2,1)S(1)} custom-call(bf16[256,1152]{1,0:T(8,128)(2,1)S(1)} %get-tuple-element.25.dproj_ref.own_ref, bf16[256,1152]{1,0:T(8,128)(2,1)S(1)} %collective-permute-done.11.got_ref, bf16[384,512]{1,0:T(8,128)(2,1)S(1)} %pick.1.after_ref.pick_ref, bf16[512,1408]{1,0:T(8,128)(2,1)S(1)} %get-tuple-element.24.rows_ref, ...), custom_call_target="tpu_custom_call" | custom-call | flops 1283457024 | bytes 7187968 | tf_op jit(solution)/shard_map/head/pallas_call | solution.py:39
  83.5 41.3 %all_to_all.22 = bf16[64,8,896]{2,1,0:T(8,128)(2,1)S(1)} all-to-all(bf16[64,8,896]{2,1,0:T(8,128)(2,1)S(1)} %bitcast.9), channel_id=1, replica_groups=mesh['x'=2,'z'=8,'c'=2,'hx'=2,'y'=8] {'z','y'}, dimensions={0} | all-to-all | bytes 1835008 | tf_op jit(solution)/shard_map/all_to_all | solution.py:397
  124.8 0.2 reduce.1
  125.0 18.2 %all_to_all.23 = bf16[16,8,896]{2,1,0:T(8,128)(2,1)S(1)} all-to-all(bf16[16,8,896]{2,1,0:T(8,128)(2,1)S(1)} %bitcast.13), channel_id=1, replica_groups=mesh['x'=2,'z'=8,'c'=2,'hx'=2,'y'=8] {'hx','y'}, dimensions={0} | all-to-all | bytes 458752 | tf_op jit(solution)/shard_map/all_to_all | solution.py:404
  143.2 0.7 unpack.1
  (3 shorter events, 0.0 us)
Async XLA Ops:
  0.6 1.0 copy-start.3
  1.7 16.8 %collective-permute-start.2 = (bf16[128,1152]{1,0:T(8,128)(2,1)S(1)}, bf16[128,1152]{1,0:T(8,128)(2,1)S(1)}, u32[]{:S(2)}, u32[]{:S(2)}) collective-permute-start(bf16[128,1152]{1,0:T(8,128)(2,1)S(1)} %text_unit.1.refs_0_), channel_id=1, source_target_pairs={{0,32},{16,240},{32,64},{48,16},{64,96},{80,48},{96,128},{112,80},... | collective-permute-start | bytes 884744 | tf_op jit(solution)/shard_map/ppermute | solution.py:292
  6.0 14.4 %collective-permute-start.5 = (bf16[128,1152]{1,0:T(8,128)(2,1)S(1)}, bf16[128,1152]{1,0:T(8,128)(2,1)S(1)}, u32[]{:S(2)}, u32[]{:S(2)}) collective-permute-start(bf16[128,1152]{1,0:T(8,128)(2,1)S(1)} %text_unit.1.refs_0_), channel_id=1, source_target_pairs={{32,0},{240,16},{64,32},{16,48},{96,64},{48,80},{128,96},{80,112},... | collective-permute-start | bytes 884744 | tf_op jit(solution)/shard_map/ppermute | solution.py:295
  14.6 1.0 copy-start.1
  15.6 0.7 copy-start.4
  16.6 9.0 %collective-permute-start = (bf16[128,1408]{1,0:T(8,128)(2,1)S(1)}, bf16[128,1408]{1,0:T(8,128)(2,1)S(1)}, u32[]{:S(2)}, u32[]{:S(2)}) collective-permute-start(bf16[128,1408]{1,0:T(8,128)(2,1)S(1)} %normed.1.own_ref), channel_id=1, source_target_pairs={{0,16},{16,0},{1,17},{17,1},{2,18},{18,2},{3,19},{19,3},{4,20},{20... | collective-permute-start | bytes 1081352 | tf_op jit(solution)/shard_map/ppermute | solution.py:299
  18.5 10.6 %collective-permute-start.3 = (bf16[128,1152]{1,0:T(8,128)(2,1)S(1)}, bf16[128,1152]{1,0:T(8,128)(2,1)S(1)}, u32[]{:S(2)}, u32[]{:S(2)}) collective-permute-start(bf16[128,1152]{1,0:T(8,128)(2,1)S(1)} %collective-permute-done.2.refs_1_), channel_id=1, source_target_pairs={{0,32},{16,240},{32,64},{48,16},{64,96},{80,48},{96,128},{112,80},... | collective-permute-start | bytes 884744 | tf_op jit(solution)/shard_map/ppermute | solution.py:292
  20.5 10.6 %collective-permute-start.6 = (bf16[128,1152]{1,0:T(8,128)(2,1)S(1)}, bf16[128,1152]{1,0:T(8,128)(2,1)S(1)}, u32[]{:S(2)}, u32[]{:S(2)}) collective-permute-start(bf16[128,1152]{1,0:T(8,128)(2,1)S(1)} %collective-permute-done.5.refs_2_), channel_id=1, source_target_pairs={{32,0},{240,16},{64,32},{16,48},{96,64},{48,80},{128,96},{80,112},... | collective-permute-start | bytes 884744 | tf_op jit(solution)/shard_map/ppermute | solution.py:295
  25.7 18.9 %collective-permute-start.1 = (bf16[256,1408]{1,0:T(8,128)(2,1)S(1)}, bf16[256,1408]{1,0:T(8,128)(2,1)S(1)}, u32[]{:S(2)}, u32[]{:S(2)}) collective-permute-start(bf16[256,1408]{1,0:T(8,128)(2,1)S(1)} %join.1.n_here), channel_id=1, source_target_pairs={{0,256},{256,0},{1,257},{257,1},{2,258},{258,2},{3,259},{259,3},{4... | collective-permute-start | bytes 2162696 | tf_op jit(solution)/shard_map/ppermute | solution.py:309
  29.1 10.8 %collective-permute-start.4 = (bf16[128,1152]{1,0:T(8,128)(2,1)S(1)}, bf16[128,1152]{1,0:T(8,128)(2,1)S(1)}, u32[]{:S(2)}, u32[]{:S(2)}) collective-permute-start(bf16[128,1152]{1,0:T(8,128)(2,1)S(1)} %collective-permute-done.3.refs_3_), channel_id=1, source_target_pairs={{0,32},{16,240},{32,64},{48,16},{64,96},{80,48},{96,128},{112,80},... | collective-permute-start | bytes 884744 | tf_op jit(solution)/shard_map/ppermute | solution.py:292
  31.1 10.8 %collective-permute-start.7 = (bf16[128,1152]{1,0:T(8,128)(2,1)S(1)}, bf16[128,1152]{1,0:T(8,128)(2,1)S(1)}, u32[]{:S(2)}, u32[]{:S(2)}) collective-permute-start(bf16[128,1152]{1,0:T(8,128)(2,1)S(1)} %collective-permute-done.6.refs_4_), channel_id=1, source_target_pairs={{32,0},{240,16},{64,32},{16,48},{96,64},{48,80},{128,96},{80,112},... | collective-permute-start | bytes 884744 | tf_op jit(solution)/shard_map/ppermute | solution.py:295
  40.0 10.8 %collective-permute-start.8 = (bf16[128,1152]{1,0:T(8,128)(2,1)S(1)}, bf16[128,1152]{1,0:T(8,128)(2,1)S(1)}, u32[]{:S(2)}, u32[]{:S(2)}) collective-permute-start(bf16[128,1152]{1,0:T(8,128)(2,1)S(1)} %collective-permute-done.4.after_ref.refs_5_), channel_id=1, source_target_pairs={{0,32},{16,240},{32,64},{48,16},{64,96},{80,48},{96,128},{112,80},... | collective-permute-start | bytes 884744 | tf_op jit(solution)/shard_map/ppermute | solution.py:292
  54.8 4.0 %collective-permute-start.9 = (bf16[272,1152]{1,0:T(8,128)(2,1)S(1)}, bf16[272,1152]{1,0:T(8,128)(2,1)S(1)}, u32[]{:S(2)}, u32[]{:S(2)}) collective-permute-start(bf16[272,1152]{1,0:T(8,128)(2,1)S(1)} %get-tuple-element.21), channel_id=1, source_target_pairs={{0,16},{16,0},{1,17},{17,1},{2,18},{18,2},{3,19},{19,3},{4,20},{20... | collective-permute-start | bytes 1880072 | tf_op jit(solution)/shard_map/ppermute | solution.py:335
  58.9 18.1 %collective-permute-start.10 = (bf16[272,1152]{1,0:T(8,128)(2,1)S(1)}, bf16[272,1152]{1,0:T(8,128)(2,1)S(1)}, u32[]{:S(2)}, u32[]{:S(2)}) collective-permute-start(bf16[272,1152]{1,0:T(8,128)(2,1)S(1)} %add_cores.1.after_ref), channel_id=1, source_target_pairs={{0,256},{256,0},{1,257},{257,1},{2,258},{258,2},{3,259},{259,3},{4... | collective-permute-start | bytes 1880072 | tf_op jit(solution)/shard_map/ppermute | solution.py:361
  76.9 2.6 %copy-start = (bf16[1408,1152]{1,0:T(8,128)(2,1)S(1)}, bf16[1408,1152]{1,0:T(8,128)(2,1)}, u32[]{:S(2)}) copy-start(bf16[1408,1152]{1,0:T(8,128)(2,1)} %w_ref.5) | copy-start | bytes 9732100
  76.9 2.6 %copy-start.2 = (bf16[1,128,1408]{2,1,0:T(8,128)(2,1)S(1)}, bf16[1,128,1408]{2,1,0:T(8,128)(2,1)}, u32[]{:S(2)}) copy-start(bf16[1,128,1408]{2,1,0:T(8,128)(2,1)} %param.6) | copy-start | bytes 1081348
  76.9 2.6 %copy-start.5 = (f32[1408]{0:T(1024)S(1)}, f32[1408]{0:T(1024)}, u32[]{:S(2)}) copy-start(f32[1408]{0:T(1024)} %gain_ref.5) | copy-start | bytes 16900
  77.4 4.3 %collective-permute-start.11 = (bf16[256,1152]{1,0:T(8,128)(2,1)S(1)}, bf16[256,1152]{1,0:T(8,128)(2,1)S(1)}, u32[]{:S(2)}, u32[]{:S(2)}) collective-permute-start(bf16[256,1152]{1,0:T(8,128)(2,1)S(1)} %get-tuple-element.25.dproj_ref.own_ref), channel_id=1, source_target_pairs={{0,16},{16,0},{1,17},{17,1},{2,18},{18,2},{3,19},{19,3},{4,20},{20... | collective-permute-start | bytes 1769480 | tf_op jit(solution)/shard_map/ppermute | solution.py:369

commit v7 on v5

--- a/solution.py
+++ b/solution.py
@@ -164,14 +164,19 @@
 
 
 def pairs_kernel(scale_ref, bias_ref, img_ref, *refs):
-    texts, (keep_ref, send_ref, loss_ref, text, slope) = refs[:2], refs[2:]
+    texts, (send_ref, loss_ref, slope, text) = refs[:2], refs[2:]
     total = pair_terms(scale_ref, bias_ref, img_ref, texts, text, slope)
     loss = jnp.broadcast_to(jnp.sum(total, keepdims=True), (1, 128))
     loss_ref[...] = loss
-    grad = jnp.dot(slope[...], text[...], preferred_element_type=F32)
-    keep_ref[...] = grad[: 2 * ROWS]
-    send_ref[: 2 * ROWS, :] = grad[2 * ROWS :].astype(BF16)
+    grad = jnp.dot(slope[2 * ROWS :, :], text[...], preferred_element_type=F32)
+    send_ref[: 2 * ROWS, :] = grad.astype(BF16)
     send_ref[2 * ROWS :, :] = loss_rows(loss)
+
+
+def keep_kernel(slope_ref, early_ref, last_ref, keep_ref):
+    early = jnp.dot(slope_ref[: 2 * ROWS, : 7 * ROWS], early_ref[...], preferred_element_type=F32)
+    last = jnp.dot(slope_ref[: 2 * ROWS, 7 * ROWS :], last_ref[...], preferred_element_type=F32)
+    keep_ref[...] = early + last
 
 
 def loss_rows(loss):
@@ -330,20 +335,33 @@
         flops=4 * 4 * ROWS * 7 * ROWS * E,
         name="collect",
     )
-    keep, send, loss = call(
+    send, loss, slope = call(
         pairs_kernel,
-        (out((2 * ROWS, E), F32), out((2 * ROWS + EXTRA, E), BF16), out((1, 128), F32)),
+        (
+            out((2 * ROWS + EXTRA, E), BF16),
+            out((1, 128), F32),
+            out((4 * ROWS, 8 * ROWS), BF16),
+        ),
         scale,
         bias,
         img,
         early,
         texts[7],
         specs=[SMEM] * 2 + [VMEM] * 3,
-        scratch=[pltpu.VMEM((8 * ROWS, E), BF16), pltpu.VMEM((4 * ROWS, 8 * ROWS), BF16)],
-        flops=4 * 4 * ROWS * 8 * ROWS * E,
+        scratch=[pltpu.VMEM((8 * ROWS, E), BF16)],
+        flops=3 * 4 * ROWS * 8 * ROWS * E,
         name="pairs",
     )
     core = between(send)
+    keep = call(
+        keep_kernel,
+        out((2 * ROWS, E), F32),
+        slope,
+        early,
+        texts[7],
+        flops=4 * ROWS * 8 * ROWS * E,
+        name="keep",
+    )
     send = call(
         add_kernel,
         out((2 * ROWS + EXTRA, E), BF16),

time: 141 us -> 140 us (level)
    pallas_call x12 -> x13, Pallas kernels: 15.2 us -> 15.6 us  [call(): pl.pallas_call(kernel, out_shape=out_shape, in_specs=specs or [VMEM] * le...]
  transfers between devices with their start and end apart: 12 -> 12, of which waited for: 8 -> 8; matrix products, arithmetic and copies ran while one was open for 0% -> 0% of each run, Pallas kernels for 5% -> 6%
where the time goes in v7:
time: 140 us
  blocking collectives  56 us (40%)
  starting transfers between devices  32 us (23%)
  waiting for transfers between devices  31.4 us (22%)
  Pallas kernels  15.6 us (11%)
  local copies, waits for them, and re-layouts  2.65 us (2%)
  between operations  2.15 us (2%)
    all_to_all x1, blocking collectives, per_device(): packed = lax.all_to_all(packed, (Z, Y), 0, 0, tiled=True)  38.1 us
    all_to_all x1, blocking collectives, per_device(): block = lax.all_to_all(piece, (HX, Y), 0, 0, tiled=True)  17.9 us
    pallas_call x13, Pallas kernels, call(): pl.pallas_call(kernel, out_shape=out_shape, in_specs=specs or [VMEM] * le...  15.6 us
    ppermute x4, waiting for transfers between devices, per_device(): one = hop(one)  14 us
    ppermute x1, waiting for transfers between devices, per_device(): across(send)  13.8 us
    ppermute x4, starting transfers between devices, per_device(): one = hop(one)  10 us
    ppermute x3, starting transfers between devices, per_device(): two = hop(two)  9.26 us
    ppermute x1, starting transfers between devices, per_device(): across(send)  3.4 us
  transfers between devices with their start and end apart: 12, of which 8 were waited for; matrix products, arithmetic and copies ran while one was open for 0% of the time, Pallas kernels for 6%

profile of v7, /device:TPU:8, one launch (start us, length us, event | category | flops | bytes accessed | tf_op | source)
XLA Modules:
  0.0 139.7 jit_solution(4402809721342018207)
XLA Ops:
  0.6 0.0 copy-start.1
  0.6 1.0 copy-done.1
  1.6 0.0 copy-start.3
  1.6 1.0 copy-done.3
  2.6 0.0 copy-start.4
  2.6 0.7 copy-done.4
  3.3 0.3 prepare.1
  3.6 1.9 %collective-permute-start = (bf16[128,2560]{1,0:T(8,128)(2,1)S(1)}, bf16[128,2560]{1,0:T(8,128)(2,1)S(1)}, u32[]{:S(2)}, u32[]{:S(2)}) collective-permute-start(bf16[128,2560]{1,0:T(8,128)(2,1)S(1)} %get-tuple-element.23.own_ref), channel_id=1, source_target_pairs={{0,16},{16,0},{1,17},{17,1},{2,18},{18,2},{3,19},{19,3},{4,20},{20... | collective-permute-start | bytes 1966088 | tf_op jit(solution)/shard_map/ppermute | solution.py:302
  5.5 4.3 %collective-permute-start.2 = (bf16[128,1152]{1,0:T(8,128)(2,1)S(1)}, bf16[128,1152]{1,0:T(8,128)(2,1)S(1)}, u32[]{:S(2)}, u32[]{:S(2)}) collective-permute-start(bf16[128,1152]{1,0:T(8,128)(2,1)S(1)} %get-tuple-element.25.refs_0_), channel_id=1, source_target_pairs={{0,32},{16,240},{32,64},{48,16},{64,96},{80,48},{96,128},{112,80},... | collective-permute-start | bytes 884744 | tf_op jit(solution)/shard_map/ppermute | solution.py:308
  9.8 0.0 collective-permute-done.got_ref
  9.8 0.1 unpack_swap.1
  9.9 4.3 %collective-permute-start.5 = (bf16[128,1152]{1,0:T(8,128)(2,1)S(1)}, bf16[128,1152]{1,0:T(8,128)(2,1)S(1)}, u32[]{:S(2)}, u32[]{:S(2)}) collective-permute-start(bf16[128,1152]{1,0:T(8,128)(2,1)S(1)} %get-tuple-element.26), channel_id=1, source_target_pairs={{0,32},{16,240},{32,64},{48,16},{64,96},{80,48},{96,128},{112,80},... | collective-permute-start | bytes 884744 | tf_op jit(solution)/shard_map/ppermute | solution.py:313
  14.2 3.4 %collective-permute-start.1 = (bf16[256,1408]{1,0:T(8,128)(2,1)S(1)}, bf16[256,1408]{1,0:T(8,128)(2,1)S(1)}, u32[]{:S(2)}, u32[]{:S(2)}) collective-permute-start(bf16[256,1408]{1,0:T(8,128)(2,1)S(1)} %get-tuple-element.24.n_here), channel_id=1, source_target_pairs={{0,256},{256,0},{1,257},{257,1},{2,258},{258,2},{3,259},{259,3},{4... | collective-permute-start | bytes 2162696 | tf_op jit(solution)/shard_map/ppermute | solution.py:325
  17.6 3.6 %collective-permute-done.2.refs_1_ = bf16[128,1152]{1,0:T(8,128)(2,1)S(1)} collective-permute-done((bf16[128,1152]{1,0:T(8,128)(2,1)S(1)}, bf16[128,1152]{1,0:T(8,128)(2,1)S(1)}, u32[]{:S(2)}, u32[]{:S(2)}) %collective-permute-start.2) | collective-permute-done | bytes 294944 | tf_op jit(solution)/shard_map/ppermute | solution.py:308
  21.2 1.9 %collective-permute-start.3 = (bf16[128,1152]{1,0:T(8,128)(2,1)S(1)}, bf16[128,1152]{1,0:T(8,128)(2,1)S(1)}, u32[]{:S(2)}, u32[]{:S(2)}) collective-permute-start(bf16[128,1152]{1,0:T(8,128)(2,1)S(1)} %collective-permute-done.2.refs_1_), channel_id=1, source_target_pairs={{0,32},{16,240},{32,64},{48,16},{64,96},{80,48},{96,128},{112,80},... | collective-permute-start | bytes 884744 | tf_op jit(solution)/shard_map/ppermute | solution.py:308
  23.1 1.2 collective-permute-done.5.refs_2_
  24.3 3.1 %collective-permute-start.6 = (bf16[128,1152]{1,0:T(8,128)(2,1)S(1)}, bf16[128,1152]{1,0:T(8,128)(2,1)S(1)}, u32[]{:S(2)}, u32[]{:S(2)}) collective-permute-start(bf16[128,1152]{1,0:T(8,128)(2,1)S(1)} %collective-permute-done.5.refs_2_), channel_id=1, source_target_pairs={{0,32},{16,240},{32,64},{48,16},{64,96},{80,48},{96,128},{112,80},... | collective-permute-start | bytes 884744 | tf_op jit(solution)/shard_map/ppermute | solution.py:313
  27.4 3.6 %collective-permute-done.3.refs_3_ = bf16[128,1152]{1,0:T(8,128)(2,1)S(1)} collective-permute-done((bf16[128,1152]{1,0:T(8,128)(2,1)S(1)}, bf16[128,1152]{1,0:T(8,128)(2,1)S(1)}, u32[]{:S(2)}, u32[]{:S(2)}) %collective-permute-start.3) | collective-permute-done | bytes 294944 | tf_op jit(solution)/shard_map/ppermute | solution.py:308
  31.0 1.9 %collective-permute-start.4 = (bf16[128,1152]{1,0:T(8,128)(2,1)S(1)}, bf16[128,1152]{1,0:T(8,128)(2,1)S(1)}, u32[]{:S(2)}, u32[]{:S(2)}) collective-permute-start(bf16[128,1152]{1,0:T(8,128)(2,1)S(1)} %collective-permute-done.3.refs_3_), channel_id=1, source_target_pairs={{0,32},{16,240},{32,64},{48,16},{64,96},{80,48},{96,128},{112,80},... | collective-permute-start | bytes 884744 | tf_op jit(solution)/shard_map/ppermute | solution.py:308
  32.9 1.2 collective-permute-done.6.refs_4_
  34.2 1.9 %collective-permute-start.7 = (bf16[128,1152]{1,0:T(8,128)(2,1)S(1)}, bf16[128,1152]{1,0:T(8,128)(2,1)S(1)}, u32[]{:S(2)}, u32[]{:S(2)}) collective-permute-start(bf16[128,1152]{1,0:T(8,128)(2,1)S(1)} %collective-permute-done.6.refs_4_), channel_id=1, source_target_pairs={{0,32},{16,240},{32,64},{48,16},{64,96},{80,48},{96,128},{112,80},... | collective-permute-start | bytes 884744 | tf_op jit(solution)/shard_map/ppermute | solution.py:313
  37.4 3.4 %collective-permute-done.4.after_ref.refs_5_ = bf16[128,1152]{1,0:T(8,128)(2,1)S(1)} collective-permute-done((bf16[128,1152]{1,0:T(8,128)(2,1)S(1)}, bf16[128,1152]{1,0:T(8,128)(2,1)S(1)}, u32[]{:S(2)}, u32[]{:S(2)}) %collective-permute-start.4) | collective-permute-done | bytes 294944 | tf_op jit(solution)/shard_map/ppermute | solution.py:308
  40.8 1.9 %collective-permute-start.8 = (bf16[128,1152]{1,0:T(8,128)(2,1)S(1)}, bf16[128,1152]{1,0:T(8,128)(2,1)S(1)}, u32[]{:S(2)}, u32[]{:S(2)}) collective-permute-start(bf16[128,1152]{1,0:T(8,128)(2,1)S(1)} %collective-permute-done.4.after_ref.refs_5_), channel_id=1, source_target_pairs={{0,32},{16,240},{32,64},{48,16},{64,96},{80,48},{96,128},{112,80},... | collective-permute-start | bytes 884744 | tf_op jit(solution)/shard_map/ppermute | solution.py:308
  42.7 0.0 collective-permute-done.1.n_there
  42.7 4.3 %project.1 = (bf16[512,1152]{1,0:T(8,128)(2,1)S(1)}, f32[256,1152]{1,0:T(8,128)S(1)}, f32[256,128]{1,0:T(8,128)S(1)}, bf16[512,1408]{1,0:T(8,128)(2,1)S(1)}) custom-call(bf16[256,1408]{1,0:T(8,128)(2,1)S(1)} %get-tuple-element.24.n_here, bf16[256,1408]{1,0:T(8,128)(2,1)S(1)} %collective-permute-done.1.n_there, bf16[1408,1152]{1,0:T(8,128)(2,1)} %w_ref.5, ...), custom_call_target="tpu_custom_call" | custom-call | flops 1660944384 | bytes 8912896 | tf_op jit(solution)/shard_map/project/pallas_call | solution.py:37
  47.1 0.0 collective-permute-done.7.refs_6_
  47.1 0.2 collect.1.refs_0_.early_ref
  47.2 3.4 %collective-permute-done.8.refs_1_.last_ref = bf16[128,1152]{1,0:T(8,128)(2,1)S(1)} collective-permute-done((bf16[128,1152]{1,0:T(8,128)(2,1)S(1)}, bf16[128,1152]{1,0:T(8,128)(2,1)S(1)}, u32[]{:S(2)}, u32[]{:S(2)}) %collective-permute-start.8) | collective-permute-done | bytes 294944 | tf_op jit(solution)/shard_map/ppermute | solution.py:308
  50.6 3.4 %pairs.1 = (bf16[272,1152]{1,0:T(8,128)(2,1)S(1)}, f32[1,128]{1,0:T(1,128)S(1)}, bf16[512,1024]{1,0:T(8,128)(2,1)S(1)}) custom-call(f32[1]{0:T(128)S(6)} %copy.10.scale_ref, f32[1]{0:T(128)S(6)} %copy.11.bias_ref, bf16[512,1152]{1,0:T(8,128)(2,1)S(1)} %get-tuple-element.28.img_ref, bf16[896,1152]{1,0:T(8,128)(2,1)S(1)} %collect.1.refs_0_.early_ref, ...), custom_call_target="tpu_custom_call" | custom-call | flops 1811939328 | bytes 5214728 | tf_op jit(solution)/shard_map/pairs/pallas_call | solution.py:37
  54.0 1.9 %collective-permute-start.9 = (bf16[272,1152]{1,0:T(8,128)(2,1)S(1)}, bf16[272,1152]{1,0:T(8,128)(2,1)S(1)}, u32[]{:S(2)}, u32[]{:S(2)}) collective-permute-start(bf16[272,1152]{1,0:T(8,128)(2,1)S(1)} %get-tuple-element.31), channel_id=1, source_target_pairs={{0,16},{16,0},{1,17},{17,1},{2,18},{18,2},{3,19},{19,3},{4,20},{20... | collective-permute-start | bytes 1880072 | tf_op jit(solution)/shard_map/ppermute | solution.py:355
  56.0 1.0 keep.1.keep_ref
  56.9 1.1 collective-permute-done.9.got_ref.core_ref
  58.0 0.1 add_cores.1.after_ref
  58.1 3.4 %collective-permute-start.10 = (bf16[272,1152]{1,0:T(8,128)(2,1)S(1)}, bf16[272,1152]{1,0:T(8,128)(2,1)S(1)}, u32[]{:S(2)}, u32[]{:S(2)}) collective-permute-start(bf16[272,1152]{1,0:T(8,128)(2,1)S(1)} %add_cores.1.after_ref), channel_id=1, source_target_pairs={{0,256},{256,0},{1,257},{257,1},{2,258},{258,2},{3,259},{259,3},{4... | collective-permute-start | bytes 1880072 | tf_op jit(solution)/shard_map/ppermute | solution.py:390
  61.5 0.8 pick.1.after_ref.pick_ref
  62.4 13.8 %collective-permute-done.10.got_ref = bf16[272,1152]{1,0:T(8,128)(2,1)S(1)} collective-permute-done((bf16[272,1152]{1,0:T(8,128)(2,1)S(1)}, bf16[272,1152]{1,0:T(8,128)(2,1)S(1)}, u32[]{:S(2)}, u32[]{:S(2)}) %collective-permute-start.10) | collective-permute-done | bytes 626720 | tf_op jit(solution)/shard_map/ppermute | solution.py:390
  76.2 0.5 d_proj.1
  76.7 2.1 %collective-permute-start.11 = (bf16[256,1152]{1,0:T(8,128)(2,1)S(1)}, bf16[256,1152]{1,0:T(8,128)(2,1)S(1)}, u32[]{:S(2)}, u32[]{:S(2)}) collective-permute-start(bf16[256,1152]{1,0:T(8,128)(2,1)S(1)} %get-tuple-element.35.dproj_ref.own_ref), channel_id=1, source_target_pairs={{0,16},{16,0},{1,17},{17,1},{2,18},{18,2},{3,19},{19,3},{4,20},{20... | collective-permute-start | bytes 1769480 | tf_op jit(solution)/shard_map/ppermute | solution.py:398
  78.8 0.0 copy-done
  78.8 0.0 copy-done.2
  78.8 0.0 copy-done.5
  78.8 2.2 %d_features.1 = (bf16[128,1408]{1,0:T(8,128)(2,1)}, f32[1,1408]{1,0:T(1,128)S(1)}) custom-call(bf16[256,1152]{1,0:T(8,128)(2,1)S(1)} %get-tuple-element.35.dproj_ref.own_ref, bf16[128,1408]{1,0:T(8,128)(2,1)S(1)} %bitcast.11, f32[1408]{0:T(1024)S(1)} %copy-done.5, bf16[512,1408]{1,0:T(8,128)(2,1)S(1)} %get-tuple-element.34.rows_ref, ...), custom_call_target="tpu_custom_call" | custom-call | flops 830472192 | bytes 6007808 | tf_op jit(solution)/shard_map/d_features/pallas_call | solution.py:37
  81.0 0.0 collective-permute-done.11.got_ref
  81.0 1.8 %head.1 = bf16[512,896]{1,0:T(8,128)(2,1)S(1)} custom-call(bf16[256,1152]{1,0:T(8,128)(2,1)S(1)} %get-tuple-element.35.dproj_ref.own_ref, bf16[256,1152]{1,0:T(8,128)(2,1)S(1)} %collective-permute-done.11.got_ref, bf16[384,512]{1,0:T(8,128)(2,1)S(1)} %pick.1.after_ref.pick_ref, bf16[512,1408]{1,0:T(8,128)(2,1)S(1)} %get-tuple-element.34.rows_ref, ...), custom_call_target="tpu_custom_call" | custom-call | flops 1283457024 | bytes 7187968 | tf_op jit(solution)/shard_map/head/pallas_call | solution.py:37
  82.8 38.1 %all_to_all.22 = bf16[64,8,896]{2,1,0:T(8,128)(2,1)S(1)} all-to-all(bf16[64,8,896]{2,1,0:T(8,128)(2,1)S(1)} %bitcast.9), channel_id=1, replica_groups=mesh['x'=2,'z'=8,'c'=2,'hx'=2,'y'=8] {'z','y'}, dimensions={0} | all-to-all | bytes 1835008 | tf_op jit(solution)/shard_map/all_to_all | solution.py:426
  120.9 0.2 reduce.1
  121.1 17.9 %all_to_all.23 = bf16[16,8,896]{2,1,0:T(8,128)(2,1)S(1)} all-to-all(bf16[16,8,896]{2,1,0:T(8,128)(2,1)S(1)} %bitcast.13), channel_id=1, replica_groups=mesh['x'=2,'z'=8,'c'=2,'hx'=2,'y'=8] {'hx','y'}, dimensions={0} | all-to-all | bytes 458752 | tf_op jit(solution)/shard_map/all_to_all | solution.py:433
  139.0 0.7 unpack.1
  (3 shorter events, 0.0 us)
Async XLA Ops:
  0.6 1.0 copy-start.1
  1.6 1.0 copy-start.3
  2.6 0.7 copy-start.4
  3.6 6.2 %collective-permute-start = (bf16[128,2560]{1,0:T(8,128)(2,1)S(1)}, bf16[128,2560]{1,0:T(8,128)(2,1)S(1)}, u32[]{:S(2)}, u32[]{:S(2)}) collective-permute-start(bf16[128,2560]{1,0:T(8,128)(2,1)S(1)} %get-tuple-element.23.own_ref), channel_id=1, source_target_pairs={{0,16},{16,0},{1,17},{17,1},{2,18},{18,2},{3,19},{19,3},{4,20},{20... | collective-permute-start | bytes 1966088 | tf_op jit(solution)/shard_map/ppermute | solution.py:302
  5.5 15.6 %collective-permute-start.2 = (bf16[128,1152]{1,0:T(8,128)(2,1)S(1)}, bf16[128,1152]{1,0:T(8,128)(2,1)S(1)}, u32[]{:S(2)}, u32[]{:S(2)}) collective-permute-start(bf16[128,1152]{1,0:T(8,128)(2,1)S(1)} %get-tuple-element.25.refs_0_), channel_id=1, source_target_pairs={{0,32},{16,240},{32,64},{48,16},{64,96},{80,48},{96,128},{112,80},... | collective-permute-start | bytes 884744 | tf_op jit(solution)/shard_map/ppermute | solution.py:308
  9.9 14.4 %collective-permute-start.5 = (bf16[128,1152]{1,0:T(8,128)(2,1)S(1)}, bf16[128,1152]{1,0:T(8,128)(2,1)S(1)}, u32[]{:S(2)}, u32[]{:S(2)}) collective-permute-start(bf16[128,1152]{1,0:T(8,128)(2,1)S(1)} %get-tuple-element.26), channel_id=1, source_target_pairs={{0,32},{16,240},{32,64},{48,16},{64,96},{80,48},{96,128},{112,80},... | collective-permute-start | bytes 884744 | tf_op jit(solution)/shard_map/ppermute | solution.py:313
  14.2 28.5 %collective-permute-start.1 = (bf16[256,1408]{1,0:T(8,128)(2,1)S(1)}, bf16[256,1408]{1,0:T(8,128)(2,1)S(1)}, u32[]{:S(2)}, u32[]{:S(2)}) collective-permute-start(bf16[256,1408]{1,0:T(8,128)(2,1)S(1)} %get-tuple-element.24.n_here), channel_id=1, source_target_pairs={{0,256},{256,0},{1,257},{257,1},{2,258},{258,2},{3,259},{259,3},{4... | collective-permute-start | bytes 2162696 | tf_op jit(solution)/shard_map/ppermute | solution.py:325
  21.2 9.8 %collective-permute-start.3 = (bf16[128,1152]{1,0:T(8,128)(2,1)S(1)}, bf16[128,1152]{1,0:T(8,128)(2,1)S(1)}, u32[]{:S(2)}, u32[]{:S(2)}) collective-permute-start(bf16[128,1152]{1,0:T(8,128)(2,1)S(1)} %collective-permute-done.2.refs_1_), channel_id=1, source_target_pairs={{0,32},{16,240},{32,64},{48,16},{64,96},{80,48},{96,128},{112,80},... | collective-permute-start | bytes 884744 | tf_op jit(solution)/shard_map/ppermute | solution.py:308
  24.3 9.8 %collective-permute-start.6 = (bf16[128,1152]{1,0:T(8,128)(2,1)S(1)}, bf16[128,1152]{1,0:T(8,128)(2,1)S(1)}, u32[]{:S(2)}, u32[]{:S(2)}) collective-permute-start(bf16[128,1152]{1,0:T(8,128)(2,1)S(1)} %collective-permute-done.5.refs_2_), channel_id=1, source_target_pairs={{0,32},{16,240},{32,64},{48,16},{64,96},{80,48},{96,128},{112,80},... | collective-permute-start | bytes 884744 | tf_op jit(solution)/shard_map/ppermute | solution.py:313
  31.0 9.8 %collective-permute-start.4 = (bf16[128,1152]{1,0:T(8,128)(2,1)S(1)}, bf16[128,1152]{1,0:T(8,128)(2,1)S(1)}, u32[]{:S(2)}, u32[]{:S(2)}) collective-permute-start(bf16[128,1152]{1,0:T(8,128)(2,1)S(1)} %collective-permute-done.3.refs_3_), channel_id=1, source_target_pairs={{0,32},{16,240},{32,64},{48,16},{64,96},{80,48},{96,128},{112,80},... | collective-permute-start | bytes 884744 | tf_op jit(solution)/shard_map/ppermute | solution.py:308
  34.2 12.9 %collective-permute-start.7 = (bf16[128,1152]{1,0:T(8,128)(2,1)S(1)}, bf16[128,1152]{1,0:T(8,128)(2,1)S(1)}, u32[]{:S(2)}, u32[]{:S(2)}) collective-permute-start(bf16[128,1152]{1,0:T(8,128)(2,1)S(1)} %collective-permute-done.6.refs_4_), channel_id=1, source_target_pairs={{0,32},{16,240},{32,64},{48,16},{64,96},{80,48},{96,128},{112,80},... | collective-permute-start | bytes 884744 | tf_op jit(solution)/shard_map/ppermute | solution.py:313
  40.8 9.8 %collective-permute-start.8 = (bf16[128,1152]{1,0:T(8,128)(2,1)S(1)}, bf16[128,1152]{1,0:T(8,128)(2,1)S(1)}, u32[]{:S(2)}, u32[]{:S(2)}) collective-permute-start(bf16[128,1152]{1,0:T(8,128)(2,1)S(1)} %collective-permute-done.4.after_ref.refs_5_), channel_id=1, source_target_pairs={{0,32},{16,240},{32,64},{48,16},{64,96},{80,48},{96,128},{112,80},... | collective-permute-start | bytes 884744 | tf_op jit(solution)/shard_map/ppermute | solution.py:308
  54.0 4.0 %collective-permute-start.9 = (bf16[272,1152]{1,0:T(8,128)(2,1)S(1)}, bf16[272,1152]{1,0:T(8,128)(2,1)S(1)}, u32[]{:S(2)}, u32[]{:S(2)}) collective-permute-start(bf16[272,1152]{1,0:T(8,128)(2,1)S(1)} %get-tuple-element.31), channel_id=1, source_target_pairs={{0,16},{16,0},{1,17},{17,1},{2,18},{18,2},{3,19},{19,3},{4,20},{20... | collective-permute-start | bytes 1880072 | tf_op jit(solution)/shard_map/ppermute | solution.py:355
  58.1 18.1 %collective-permute-start.10 = (bf16[272,1152]{1,0:T(8,128)(2,1)S(1)}, bf16[272,1152]{1,0:T(8,128)(2,1)S(1)}, u32[]{:S(2)}, u32[]{:S(2)}) collective-permute-start(bf16[272,1152]{1,0:T(8,128)(2,1)S(1)} %add_cores.1.after_ref), channel_id=1, source_target_pairs={{0,256},{256,0},{1,257},{257,1},{2,258},{258,2},{3,259},{259,3},{4... | collective-permute-start | bytes 1880072 | tf_op jit(solution)/shard_map/ppermute | solution.py:390
  76.2 2.6 %copy-start = (bf16[1408,1152]{1,0:T(8,128)(2,1)S(1)}, bf16[1408,1152]{1,0:T(8,128)(2,1)}, u32[]{:S(2)}) copy-start(bf16[1408,1152]{1,0:T(8,128)(2,1)} %w_ref.5) | copy-start | bytes 9732100
  76.2 2.6 %copy-start.2 = (bf16[1,128,1408]{2,1,0:T(8,128)(2,1)S(1)}, bf16[1,128,1408]{2,1,0:T(8,128)(2,1)}, u32[]{:S(2)}) copy-start(bf16[1,128,1408]{2,1,0:T(8,128)(2,1)} %param.6) | copy-start | bytes 1081348
  76.2 2.6 %copy-start.5 = (f32[1408]{0:T(1024)S(1)}, f32[1408]{0:T(1024)}, u32[]{:S(2)}) copy-start(f32[1408]{0:T(1024)} %gain_ref.5) | copy-start | bytes 16900
  76.7 4.3 %collective-permute-start.11 = (bf16[256,1152]{1,0:T(8,128)(2,1)S(1)}, bf16[256,1152]{1,0:T(8,128)(2,1)S(1)}, u32[]{:S(2)}, u32[]{:S(2)}) collective-permute-start(bf16[256,1152]{1,0:T(8,128)(2,1)S(1)} %get-tuple-element.35.dproj_ref.own_ref), channel_id=1, source_target_pairs={{0,16},{16,0},{1,17},{17,1},{2,18},{18,2},{3,19},{19,3},{4,20},{20... | collective-permute-start | bytes 1769480 | tf_op jit(solution)/shard_map/ppermute | solution.py:398

commit v8 on v6

--- a/solution.py
+++ b/solution.py
@@ -80,11 +80,10 @@
         refs[-1][pl.ds(i * ROWS, ROWS), :] = piece[...]
 
 
-def project_kernel(n_here, n_there, w_ref, after_ref, img_ref, unit_ref, pnorm_ref, rows_ref):
+def project_kernel(n_own, n_core, w_ref, after_ref, img_ref, unit_ref, pnorm_ref, rows_ref):
     del after_ref
-    for i, part in enumerate((n_here, n_there)):
-        rows_ref[i * ROWS : (i + 1) * ROWS, :] = part[:ROWS, :]
-        rows_ref[(i + 2) * ROWS : (i + 3) * ROWS, :] = part[ROWS:, :]
+    rows_ref[: 2 * ROWS, :] = n_own[...]
+    rows_ref[2 * ROWS :, :] = n_core[...]
     proj = jnp.dot(rows_ref[...], w_ref[...], preferred_element_type=F32)
     pnorm = lax.rsqrt(jnp.sum(proj * proj, axis=1, keepdims=True) + EPSILON)
     unit = proj * pnorm
@@ -166,14 +165,19 @@
 
 
 def pairs_kernel(scale_ref, bias_ref, img_ref, *refs):
-    texts, (keep_ref, send_ref, loss_ref, text, slope) = refs[:2], refs[2:]
+    texts, (send_ref, loss_ref, slope, text) = refs[:2], refs[2:]
     total = pair_terms(scale_ref, bias_ref, img_ref, texts, text, slope)
     loss = jnp.broadcast_to(jnp.sum(total, keepdims=True), (1, 128))
     loss_ref[...] = loss
-    grad = jnp.dot(slope[...], text[...], preferred_element_type=F32)
-    keep_ref[...] = grad[: 2 * ROWS]
-    send_ref[: 2 * ROWS, :] = grad[2 * ROWS :].astype(BF16)
+    grad = jnp.dot(slope[2 * ROWS :, :], text[...], preferred_element_type=F32)
+    send_ref[: 2 * ROWS, :] = grad.astype(BF16)
     send_ref[2 * ROWS :, :] = loss_rows(loss)
+
+
+def keep_kernel(slope_ref, early_ref, last_ref, keep_ref):
+    early = jnp.dot(slope_ref[: 2 * ROWS, : 7 * ROWS], early_ref[...], preferred_element_type=F32)
+    last = jnp.dot(slope_ref[: 2 * ROWS, 7 * ROWS :], last_ref[...], preferred_element_type=F32)
+    keep_ref[...] = early + last
 
 
 def loss_rows(loss):
@@ -286,6 +290,8 @@
     hop_back = functools.partial(lax.ppermute, axis_name=(Z, C), perm=HOP_BACK)
 
     text = call(text_kernel, out((ROWS, E), BF16), captions[0], name="text_unit")
+    n0 = call(norm_kernel, out((ROWS, W), BF16), x, gain, name="normed")
+    far = across(n0)
     texts = [text]
     one, two = text, text
     for step in range(4):
@@ -295,8 +301,7 @@
             two = hop_back(two)
             texts.append(two)
 
-    n0 = call(norm_kernel, out((ROWS, W), BF16), x, gain, name="normed")
-    n_here = call(join_kernel, out((2 * ROWS, W), BF16), n0, between(n0), name="join")
+    n_own = call(join_kernel, out((2 * ROWS, W), BF16), n0, far, name="join")
     img, unit, pnorm, rows = call(
         project_kernel,
         (
@@ -305,8 +310,8 @@
             out((2 * ROWS, 128), F32),
             out((4 * ROWS, W), BF16),
         ),
-        n_here,
-        across(n_here),
+        n_own,
+        between(n_own),
         w,
         texts[5],
         flops=2 * 4 * ROWS * W * E,
@@ -319,20 +324,33 @@
         flops=4 * 4 * ROWS * 7 * ROWS * E,
         name="collect",
     )
-    keep, send, loss = call(
+    send, loss, slope = call(
         pairs_kernel,
-        (out((2 * ROWS, E), F32), out((2 * ROWS + EXTRA, E), BF16), out((1, 128), F32)),
+        (
+            out((2 * ROWS + EXTRA, E), BF16),
+            out((1, 128), F32),
+            out((4 * ROWS, 8 * ROWS), BF16),
+        ),
         scale,
         bias,
         img,
         early,
         texts[7],
         specs=[SMEM] * 2 + [VMEM] * 3,
-        scratch=[pltpu.VMEM((8 * ROWS, E), BF16), pltpu.VMEM((4 * ROWS, 8 * ROWS), BF16)],
-        flops=4 * 4 * ROWS * 8 * ROWS * E,
+        scratch=[pltpu.VMEM((8 * ROWS, E), BF16)],
+        flops=3 * 4 * ROWS * 8 * ROWS * E,
         name="pairs",
     )
     core = between(send)
+    keep = call(
+        keep_kernel,
+        out((2 * ROWS, E), F32),
+        slope,
+        early,
+        texts[7],
+        flops=4 * ROWS * 8 * ROWS * E,
+        name="keep",
+    )
     send = call(
         add_kernel,
         out((2 * ROWS + EXTRA, E), BF16),

time: 145 us -> 144 us (level)
    pallas_call x13 -> x14, Pallas kernels: 15.3 us -> 15.7 us  [call(): pl.pallas_call(kernel, out_shape=out_shape, in_specs=specs or [VMEM] * le...]
  transfers between devices with their start and end apart: 12 -> 12, of which waited for: 5 -> 5; matrix products, arithmetic and copies ran while one was open for 0% -> 0% of each run, Pallas kernels for 5% -> 6%
where the time goes in v8:
time: 144 us; the launch traced here: 143 us
  blocking collectives  60.2 us (42%)
  starting transfers between devices  41.6 us (29%)
  waiting for transfers between devices  21.2 us (15%)
  Pallas kernels  15.7 us (11%)
  local copies, waits for them, and re-layouts  2.64 us (2%)
  between operations  2.17 us (2%)
    all_to_all x1, blocking collectives, per_device(): packed = lax.all_to_all(packed, (Z, Y), 0, 0, tiled=True)  42.4 us
    ppermute x3, starting transfers between devices, per_device(): two = hop_back(two)  18.9 us
    all_to_all x1, blocking collectives, per_device(): block = lax.all_to_all(piece, (HX, Y), 0, 0, tiled=True)  17.8 us
    pallas_call x14, Pallas kernels, call(): pl.pallas_call(kernel, out_shape=out_shape, in_specs=specs or [VMEM] * le...  15.7 us
    ppermute x1, waiting for transfers between devices, per_device(): across(send)  13.8 us
    ppermute x4, starting transfers between devices, per_device(): one = hop(one)  10 us
    ppermute x4, waiting for transfers between devices, per_device(): one = hop(one)  4.99 us
    ppermute x1, starting transfers between devices, per_device(): across(send)  3.4 us
  transfers between devices with their start and end apart: 12, of which 5 were waited for; matrix products, arithmetic and copies ran while one was open for 0% of the time, Pallas kernels for 6%

profile of v8, /device:TPU:8, one launch (start us, length us, event | category | flops | bytes accessed | tf_op | source)
XLA Modules:
  0.0 143.4 jit_solution(18393437192376809357)
XLA Ops:
  0.6 0.0 copy-start.3
  0.6 1.0 copy-done.3
  1.6 0.1 text_unit.1.refs_0_
  1.7 4.3 %collective-permute-start.2 = (bf16[128,1152]{1,0:T(8,128)(2,1)S(1)}, bf16[128,1152]{1,0:T(8,128)(2,1)S(1)}, u32[]{:S(2)}, u32[]{:S(2)}) collective-permute-start(bf16[128,1152]{1,0:T(8,128)(2,1)S(1)} %text_unit.1.refs_0_), channel_id=1, source_target_pairs={{0,32},{16,240},{32,64},{48,16},{64,96},{80,48},{96,128},{112,80},... | collective-permute-start | bytes 884744 | tf_op jit(solution)/shard_map/ppermute | solution.py:298
  6.0 8.6 %collective-permute-start.5 = (bf16[128,1152]{1,0:T(8,128)(2,1)S(1)}, bf16[128,1152]{1,0:T(8,128)(2,1)S(1)}, u32[]{:S(2)}, u32[]{:S(2)}) collective-permute-start(bf16[128,1152]{1,0:T(8,128)(2,1)S(1)} %text_unit.1.refs_0_), channel_id=1, source_target_pairs={{32,0},{240,16},{64,32},{16,48},{96,64},{48,80},{128,96},{80,112},... | collective-permute-start | bytes 884744 | tf_op jit(solution)/shard_map/ppermute | solution.py:301
  14.6 0.0 copy-start.1
  14.6 1.0 copy-done.1
  15.6 0.7 copy-done.4
  16.3 0.3 normed.1.own_ref
  16.6 3.4 %collective-permute-start = (bf16[128,1408]{1,0:T(8,128)(2,1)S(1)}, bf16[128,1408]{1,0:T(8,128)(2,1)S(1)}, u32[]{:S(2)}, u32[]{:S(2)}) collective-permute-start(bf16[128,1408]{1,0:T(8,128)(2,1)S(1)} %normed.1.own_ref), channel_id=1, source_target_pairs={{0,256},{256,0},{1,257},{257,1},{2,258},{258,2},{3,259},{259,3},{4... | collective-permute-start | bytes 1081352 | tf_op jit(solution)/shard_map/ppermute | solution.py:294
  20.0 0.0 collective-permute-done.2.refs_1_
  20.0 1.9 %collective-permute-start.3 = (bf16[128,1152]{1,0:T(8,128)(2,1)S(1)}, bf16[128,1152]{1,0:T(8,128)(2,1)S(1)}, u32[]{:S(2)}, u32[]{:S(2)}) collective-permute-start(bf16[128,1152]{1,0:T(8,128)(2,1)S(1)} %collective-permute-done.2.refs_1_), channel_id=1, source_target_pairs={{0,32},{16,240},{32,64},{48,16},{64,96},{80,48},{96,128},{112,80},... | collective-permute-start | bytes 884744 | tf_op jit(solution)/shard_map/ppermute | solution.py:298
  22.0 0.0 collective-permute-done.5.refs_2_
  22.0 5.1 %collective-permute-start.6 = (bf16[128,1152]{1,0:T(8,128)(2,1)S(1)}, bf16[128,1152]{1,0:T(8,128)(2,1)S(1)}, u32[]{:S(2)}, u32[]{:S(2)}) collective-permute-start(bf16[128,1152]{1,0:T(8,128)(2,1)S(1)} %collective-permute-done.5.refs_2_), channel_id=1, source_target_pairs={{32,0},{240,16},{64,32},{16,48},{96,64},{48,80},{128,96},{80,112},... | collective-permute-start | bytes 884744 | tf_op jit(solution)/shard_map/ppermute | solution.py:301
  27.1 1.3 collective-permute-done.got_ref
  28.4 0.1 join.1.n_own
  28.4 1.9 %collective-permute-start.1 = (bf16[256,1408]{1,0:T(8,128)(2,1)S(1)}, bf16[256,1408]{1,0:T(8,128)(2,1)S(1)}, u32[]{:S(2)}, u32[]{:S(2)}) collective-permute-start(bf16[256,1408]{1,0:T(8,128)(2,1)S(1)} %join.1.n_own), channel_id=1, source_target_pairs={{0,16},{16,0},{1,17},{17,1},{2,18},{18,2},{3,19},{19,3},{4,20},{20... | collective-permute-start | bytes 2162696 | tf_op jit(solution)/shard_map/ppermute | solution.py:314
  30.4 0.0 collective-permute-done.3.refs_3_
  30.4 1.9 %collective-permute-start.4 = (bf16[128,1152]{1,0:T(8,128)(2,1)S(1)}, bf16[128,1152]{1,0:T(8,128)(2,1)S(1)}, u32[]{:S(2)}, u32[]{:S(2)}) collective-permute-start(bf16[128,1152]{1,0:T(8,128)(2,1)S(1)} %collective-permute-done.3.refs_3_), channel_id=1, source_target_pairs={{0,32},{16,240},{32,64},{48,16},{64,96},{80,48},{96,128},{112,80},... | collective-permute-start | bytes 884744 | tf_op jit(solution)/shard_map/ppermute | solution.py:298
  32.3 0.0 collective-permute-done.6.refs_4_
  32.3 5.1 %collective-permute-start.7 = (bf16[128,1152]{1,0:T(8,128)(2,1)S(1)}, bf16[128,1152]{1,0:T(8,128)(2,1)S(1)}, u32[]{:S(2)}, u32[]{:S(2)}) collective-permute-start(bf16[128,1152]{1,0:T(8,128)(2,1)S(1)} %collective-permute-done.6.refs_4_), channel_id=1, source_target_pairs={{32,0},{240,16},{64,32},{16,48},{96,64},{48,80},{128,96},{80,112},... | collective-permute-start | bytes 884744 | tf_op jit(solution)/shard_map/ppermute | solution.py:301
  38.7 1.5 %collective-permute-done.4.after_ref.refs_5_ = bf16[128,1152]{1,0:T(8,128)(2,1)S(1)} collective-permute-done((bf16[128,1152]{1,0:T(8,128)(2,1)S(1)}, bf16[128,1152]{1,0:T(8,128)(2,1)S(1)}, u32[]{:S(2)}, u32[]{:S(2)}) %collective-permute-start.4) | collective-permute-done | bytes 294944 | tf_op jit(solution)/shard_map/ppermute | solution.py:298
  40.2 1.9 %collective-permute-start.8 = (bf16[128,1152]{1,0:T(8,128)(2,1)S(1)}, bf16[128,1152]{1,0:T(8,128)(2,1)S(1)}, u32[]{:S(2)}, u32[]{:S(2)}) collective-permute-start(bf16[128,1152]{1,0:T(8,128)(2,1)S(1)} %collective-permute-done.4.after_ref.refs_5_), channel_id=1, source_target_pairs={{0,32},{16,240},{32,64},{48,16},{64,96},{80,48},{96,128},{112,80},... | collective-permute-start | bytes 884744 | tf_op jit(solution)/shard_map/ppermute | solution.py:298
  42.1 0.0 collective-permute-done.7.refs_6_
  42.1 0.1 collect.1.refs_0_.early_ref
  42.3 0.0 collective-permute-done.1.n_core
  42.3 4.3 %project.1 = (bf16[512,1152]{1,0:T(8,128)(2,1)S(1)}, f32[256,1152]{1,0:T(8,128)S(1)}, f32[256,128]{1,0:T(8,128)S(1)}, bf16[512,1408]{1,0:T(8,128)(2,1)S(1)}) custom-call(bf16[256,1408]{1,0:T(8,128)(2,1)S(1)} %join.1.n_own, bf16[256,1408]{1,0:T(8,128)(2,1)S(1)} %collective-permute-done.1.n_core, bf16[1408,1152]{1,0:T(8,128)(2,1)} %w_ref.5, ...), custom_call_target="tpu_custom_call" | custom-call | flops 1660944384 | bytes 8912896 | tf_op jit(solution)/shard_map/project/pallas_call | solution.py:39
  46.6 3.5 %collective-permute-done.8.refs_1_.last_ref = bf16[128,1152]{1,0:T(8,128)(2,1)S(1)} collective-permute-done((bf16[128,1152]{1,0:T(8,128)(2,1)S(1)}, bf16[128,1152]{1,0:T(8,128)(2,1)S(1)}, u32[]{:S(2)}, u32[]{:S(2)}) %collective-permute-start.8) | collective-permute-done | bytes 294944 | tf_op jit(solution)/shard_map/ppermute | solution.py:298
  50.1 3.4 %pairs.1 = (bf16[272,1152]{1,0:T(8,128)(2,1)S(1)}, f32[1,128]{1,0:T(1,128)S(1)}, bf16[512,1024]{1,0:T(8,128)(2,1)S(1)}) custom-call(f32[1]{0:T(128)S(6)} %copy.10.scale_ref, f32[1]{0:T(128)S(6)} %copy.11.bias_ref, bf16[512,1152]{1,0:T(8,128)(2,1)S(1)} %get-tuple-element.18.img_ref, bf16[896,1152]{1,0:T(8,128)(2,1)S(1)} %collect.1.refs_0_.early_ref, ...), custom_call_target="tpu_custom_call" | custom-call | flops 1811939328 | bytes 5214728 | tf_op jit(solution)/shard_map/pairs/pallas_call | solution.py:39
  53.5 1.9 %collective-permute-start.9 = (bf16[272,1152]{1,0:T(8,128)(2,1)S(1)}, bf16[272,1152]{1,0:T(8,128)(2,1)S(1)}, u32[]{:S(2)}, u32[]{:S(2)}) collective-permute-start(bf16[272,1152]{1,0:T(8,128)(2,1)S(1)} %get-tuple-element.21), channel_id=1, source_target_pairs={{0,16},{16,0},{1,17},{17,1},{2,18},{18,2},{3,19},{19,3},{4,20},{20... | collective-permute-start | bytes 1880072 | tf_op jit(solution)/shard_map/ppermute | solution.py:344
  55.5 1.0 keep.1.keep_ref
  56.5 1.0 collective-permute-done.9.got_ref.core_ref
  57.5 0.1 add_cores.1.after_ref
  57.6 3.4 %collective-permute-start.10 = (bf16[272,1152]{1,0:T(8,128)(2,1)S(1)}, bf16[272,1152]{1,0:T(8,128)(2,1)S(1)}, u32[]{:S(2)}, u32[]{:S(2)}) collective-permute-start(bf16[272,1152]{1,0:T(8,128)(2,1)S(1)} %add_cores.1.after_ref), channel_id=1, source_target_pairs={{0,256},{256,0},{1,257},{257,1},{2,258},{258,2},{3,259},{259,3},{4... | collective-permute-start | bytes 1880072 | tf_op jit(solution)/shard_map/ppermute | solution.py:379
  61.1 0.8 pick.1.after_ref.pick_ref
  61.9 13.8 %collective-permute-done.10.got_ref = bf16[272,1152]{1,0:T(8,128)(2,1)S(1)} collective-permute-done((bf16[272,1152]{1,0:T(8,128)(2,1)S(1)}, bf16[272,1152]{1,0:T(8,128)(2,1)S(1)}, u32[]{:S(2)}, u32[]{:S(2)}) %collective-permute-start.10) | collective-permute-done | bytes 626720 | tf_op jit(solution)/shard_map/ppermute | solution.py:379
  75.7 0.5 d_proj.1
  76.2 2.1 %collective-permute-start.11 = (bf16[256,1152]{1,0:T(8,128)(2,1)S(1)}, bf16[256,1152]{1,0:T(8,128)(2,1)S(1)}, u32[]{:S(2)}, u32[]{:S(2)}) collective-permute-start(bf16[256,1152]{1,0:T(8,128)(2,1)S(1)} %get-tuple-element.25.dproj_ref.own_ref), channel_id=1, source_target_pairs={{0,16},{16,0},{1,17},{17,1},{2,18},{18,2},{3,19},{19,3},{4,20},{20... | collective-permute-start | bytes 1769480 | tf_op jit(solution)/shard_map/ppermute | solution.py:387
  78.3 0.0 copy-done
  78.3 0.0 copy-done.2
  78.3 0.0 copy-done.5
  78.3 2.2 %d_features.1 = (bf16[128,1408]{1,0:T(8,128)(2,1)}, f32[1,1408]{1,0:T(1,128)S(1)}) custom-call(bf16[256,1152]{1,0:T(8,128)(2,1)S(1)} %get-tuple-element.25.dproj_ref.own_ref, bf16[128,1408]{1,0:T(8,128)(2,1)S(1)} %bitcast.11, f32[1408]{0:T(1024)S(1)} %copy-done.5, bf16[512,1408]{1,0:T(8,128)(2,1)S(1)} %get-tuple-element.24.rows_ref, ...), custom_call_target="tpu_custom_call" | custom-call | flops 830472192 | bytes 6007808 | tf_op jit(solution)/shard_map/d_features/pallas_call | solution.py:39
  80.5 0.0 collective-permute-done.11.got_ref
  80.5 1.8 %head.1 = bf16[512,896]{1,0:T(8,128)(2,1)S(1)} custom-call(bf16[256,1152]{1,0:T(8,128)(2,1)S(1)} %get-tuple-element.25.dproj_ref.own_ref, bf16[256,1152]{1,0:T(8,128)(2,1)S(1)} %collective-permute-done.11.got_ref, bf16[384,512]{1,0:T(8,128)(2,1)S(1)} %pick.1.after_ref.pick_ref, bf16[512,1408]{1,0:T(8,128)(2,1)S(1)} %get-tuple-element.24.rows_ref, ...), custom_call_target="tpu_custom_call" | custom-call | flops 1283457024 | bytes 7187968 | tf_op jit(solution)/shard_map/head/pallas_call | solution.py:39
  82.3 42.4 %all_to_all.22 = bf16[64,8,896]{2,1,0:T(8,128)(2,1)S(1)} all-to-all(bf16[64,8,896]{2,1,0:T(8,128)(2,1)S(1)} %bitcast.9), channel_id=1, replica_groups=mesh['x'=2,'z'=8,'c'=2,'hx'=2,'y'=8] {'z','y'}, dimensions={0} | all-to-all | bytes 1835008 | tf_op jit(solution)/shard_map/all_to_all | solution.py:415
  124.7 0.2 reduce.1
  124.9 17.8 %all_to_all.23 = bf16[16,8,896]{2,1,0:T(8,128)(2,1)S(1)} all-to-all(bf16[16,8,896]{2,1,0:T(8,128)(2,1)S(1)} %bitcast.13), channel_id=1, replica_groups=mesh['x'=2,'z'=8,'c'=2,'hx'=2,'y'=8] {'hx','y'}, dimensions={0} | all-to-all | bytes 458752 | tf_op jit(solution)/shard_map/all_to_all | solution.py:422
  142.7 0.7 unpack.1
  (4 shorter events, 0.0 us)
Async XLA Ops:
  0.6 1.0 copy-start.3
  1.7 18.3 %collective-permute-start.2 = (bf16[128,1152]{1,0:T(8,128)(2,1)S(1)}, bf16[128,1152]{1,0:T(8,128)(2,1)S(1)}, u32[]{:S(2)}, u32[]{:S(2)}) collective-permute-start(bf16[128,1152]{1,0:T(8,128)(2,1)S(1)} %text_unit.1.refs_0_), channel_id=1, source_target_pairs={{0,32},{16,240},{32,64},{48,16},{64,96},{80,48},{96,128},{112,80},... | collective-permute-start | bytes 884744 | tf_op jit(solution)/shard_map/ppermute | solution.py:298
  6.0 15.9 %collective-permute-start.5 = (bf16[128,1152]{1,0:T(8,128)(2,1)S(1)}, bf16[128,1152]{1,0:T(8,128)(2,1)S(1)}, u32[]{:S(2)}, u32[]{:S(2)}) collective-permute-start(bf16[128,1152]{1,0:T(8,128)(2,1)S(1)} %text_unit.1.refs_0_), channel_id=1, source_target_pairs={{32,0},{240,16},{64,32},{16,48},{96,64},{48,80},{128,96},{80,112},... | collective-permute-start | bytes 884744 | tf_op jit(solution)/shard_map/ppermute | solution.py:301
  14.6 1.0 copy-start.1
  15.6 0.7 copy-start.4
  16.6 11.8 %collective-permute-start = (bf16[128,1408]{1,0:T(8,128)(2,1)S(1)}, bf16[128,1408]{1,0:T(8,128)(2,1)S(1)}, u32[]{:S(2)}, u32[]{:S(2)}) collective-permute-start(bf16[128,1408]{1,0:T(8,128)(2,1)S(1)} %normed.1.own_ref), channel_id=1, source_target_pairs={{0,256},{256,0},{1,257},{257,1},{2,258},{258,2},{3,259},{259,3},{4... | collective-permute-start | bytes 1081352 | tf_op jit(solution)/shard_map/ppermute | solution.py:294
  20.0 10.3 %collective-permute-start.3 = (bf16[128,1152]{1,0:T(8,128)(2,1)S(1)}, bf16[128,1152]{1,0:T(8,128)(2,1)S(1)}, u32[]{:S(2)}, u32[]{:S(2)}) collective-permute-start(bf16[128,1152]{1,0:T(8,128)(2,1)S(1)} %collective-permute-done.2.refs_1_), channel_id=1, source_target_pairs={{0,32},{16,240},{32,64},{48,16},{64,96},{80,48},{96,128},{112,80},... | collective-permute-start | bytes 884744 | tf_op jit(solution)/shard_map/ppermute | solution.py:298
  22.0 10.3 %collective-permute-start.6 = (bf16[128,1152]{1,0:T(8,128)(2,1)S(1)}, bf16[128,1152]{1,0:T(8,128)(2,1)S(1)}, u32[]{:S(2)}, u32[]{:S(2)}) collective-permute-start(bf16[128,1152]{1,0:T(8,128)(2,1)S(1)} %collective-permute-done.5.refs_2_), channel_id=1, source_target_pairs={{32,0},{240,16},{64,32},{16,48},{96,64},{48,80},{128,96},{80,112},... | collective-permute-start | bytes 884744 | tf_op jit(solution)/shard_map/ppermute | solution.py:301
  28.4 13.9 %collective-permute-start.1 = (bf16[256,1408]{1,0:T(8,128)(2,1)S(1)}, bf16[256,1408]{1,0:T(8,128)(2,1)S(1)}, u32[]{:S(2)}, u32[]{:S(2)}) collective-permute-start(bf16[256,1408]{1,0:T(8,128)(2,1)S(1)} %join.1.n_own), channel_id=1, source_target_pairs={{0,16},{16,0},{1,17},{17,1},{2,18},{18,2},{3,19},{19,3},{4,20},{20... | collective-permute-start | bytes 2162696 | tf_op jit(solution)/shard_map/ppermute | solution.py:314
  30.4 9.8 %collective-permute-start.4 = (bf16[128,1152]{1,0:T(8,128)(2,1)S(1)}, bf16[128,1152]{1,0:T(8,128)(2,1)S(1)}, u32[]{:S(2)}, u32[]{:S(2)}) collective-permute-start(bf16[128,1152]{1,0:T(8,128)(2,1)S(1)} %collective-permute-done.3.refs_3_), channel_id=1, source_target_pairs={{0,32},{16,240},{32,64},{48,16},{64,96},{80,48},{96,128},{112,80},... | collective-permute-start | bytes 884744 | tf_op jit(solution)/shard_map/ppermute | solution.py:298
  32.3 9.8 %collective-permute-start.7 = (bf16[128,1152]{1,0:T(8,128)(2,1)S(1)}, bf16[128,1152]{1,0:T(8,128)(2,1)S(1)}, u32[]{:S(2)}, u32[]{:S(2)}) collective-permute-start(bf16[128,1152]{1,0:T(8,128)(2,1)S(1)} %collective-permute-done.6.refs_4_), channel_id=1, source_target_pairs={{32,0},{240,16},{64,32},{16,48},{96,64},{48,80},{128,96},{80,112},... | collective-permute-start | bytes 884744 | tf_op jit(solution)/shard_map/ppermute | solution.py:301
  40.2 9.9 %collective-permute-start.8 = (bf16[128,1152]{1,0:T(8,128)(2,1)S(1)}, bf16[128,1152]{1,0:T(8,128)(2,1)S(1)}, u32[]{:S(2)}, u32[]{:S(2)}) collective-permute-start(bf16[128,1152]{1,0:T(8,128)(2,1)S(1)} %collective-permute-done.4.after_ref.refs_5_), channel_id=1, source_target_pairs={{0,32},{16,240},{32,64},{48,16},{64,96},{80,48},{96,128},{112,80},... | collective-permute-start | bytes 884744 | tf_op jit(solution)/shard_map/ppermute | solution.py:298
  53.5 4.0 %collective-permute-start.9 = (bf16[272,1152]{1,0:T(8,128)(2,1)S(1)}, bf16[272,1152]{1,0:T(8,128)(2,1)S(1)}, u32[]{:S(2)}, u32[]{:S(2)}) collective-permute-start(bf16[272,1152]{1,0:T(8,128)(2,1)S(1)} %get-tuple-element.21), channel_id=1, source_target_pairs={{0,16},{16,0},{1,17},{17,1},{2,18},{18,2},{3,19},{19,3},{4,20},{20... | collective-permute-start | bytes 1880072 | tf_op jit(solution)/shard_map/ppermute | solution.py:344
  57.6 18.1 %collective-permute-start.10 = (bf16[272,1152]{1,0:T(8,128)(2,1)S(1)}, bf16[272,1152]{1,0:T(8,128)(2,1)S(1)}, u32[]{:S(2)}, u32[]{:S(2)}) collective-permute-start(bf16[272,1152]{1,0:T(8,128)(2,1)S(1)} %add_cores.1.after_ref), channel_id=1, source_target_pairs={{0,256},{256,0},{1,257},{257,1},{2,258},{258,2},{3,259},{259,3},{4... | collective-permute-start | bytes 1880072 | tf_op jit(solution)/shard_map/ppermute | solution.py:379
  75.7 2.6 %copy-start = (bf16[1408,1152]{1,0:T(8,128)(2,1)S(1)}, bf16[1408,1152]{1,0:T(8,128)(2,1)}, u32[]{:S(2)}) copy-start(bf16[1408,1152]{1,0:T(8,128)(2,1)} %w_ref.5) | copy-start | bytes 9732100
  75.7 2.6 %copy-start.2 = (bf16[1,128,1408]{2,1,0:T(8,128)(2,1)S(1)}, bf16[1,128,1408]{2,1,0:T(8,128)(2,1)}, u32[]{:S(2)}) copy-start(bf16[1,128,1408]{2,1,0:T(8,128)(2,1)} %param.6) | copy-start | bytes 1081348
  75.7 2.6 %copy-start.5 = (f32[1408]{0:T(1024)S(1)}, f32[1408]{0:T(1024)}, u32[]{:S(2)}) copy-start(f32[1408]{0:T(1024)} %gain_ref.5) | copy-start | bytes 16900
  76.2 4.3 %collective-permute-start.11 = (bf16[256,1152]{1,0:T(8,128)(2,1)S(1)}, bf16[256,1152]{1,0:T(8,128)(2,1)S(1)}, u32[]{:S(2)}, u32[]{:S(2)}) collective-permute-start(bf16[256,1152]{1,0:T(8,128)(2,1)S(1)} %get-tuple-element.25.dproj_ref.own_ref), channel_id=1, source_target_pairs={{0,16},{16,0},{1,17},{17,1},{2,18},{18,2},{3,19},{19,3},{4,20},{20... | collective-permute-start | bytes 1769480 | tf_op jit(solution)/shard_map/ppermute | solution.py:387

commit v9 on v8

--- a/solution.py
+++ b/solution.py
@@ -70,7 +70,8 @@
     normed_ref[...] = (x_hat * gain_ref[...].reshape(1, W)).astype(BF16)
 
 
-def join_kernel(own_ref, got_ref, both_ref):
+def join_kernel(own_ref, got_ref, after_ref, both_ref):
+    del after_ref
     both_ref[:ROWS, :] = own_ref[...]
     both_ref[ROWS:, :] = got_ref[...]
 
@@ -301,7 +302,7 @@
             two = hop_back(two)
             texts.append(two)
 
-    n_own = call(join_kernel, out((2 * ROWS, W), BF16), n0, far, name="join")
+    n_own = call(join_kernel, out((2 * ROWS, W), BF16), n0, far, texts[4], name="join")
     img, unit, pnorm, rows = call(
         project_kernel,
         (
@@ -321,8 +322,14 @@
         collect_kernel,
         out((7 * ROWS, E), BF16),
         *texts[:7],
-        flops=4 * 4 * ROWS * 7 * ROWS * E,
         name="collect",
+    )
+    last = call(
+        collect_kernel,
+        out((ROWS, E), BF16),
+        texts[7],
+        flops=12 * 4 * ROWS * 8 * ROWS * E,
+        name="last",
     )
     send, loss, slope = call(
         pairs_kernel,
@@ -335,7 +342,7 @@
         bias,
         img,
         early,
-        texts[7],
+        last,
         specs=[SMEM] * 2 + [VMEM] * 3,
         scratch=[pltpu.VMEM((8 * ROWS, E), BF16)],
         flops=3 * 4 * ROWS * 8 * ROWS * E,
@@ -347,7 +354,7 @@
         out((2 * ROWS, E), F32),
         slope,
         early,
-        texts[7],
+        last,
         flops=4 * ROWS * 8 * ROWS * E,
         name="keep",
     )

time: 144 us -> 148 us (1.028)
  waiting for transfers between devices: 21.2 us -> 26.9 us
  blocking collectives: 60.2 us -> 58.1 us
    ppermute x4, waiting for transfers between devices: 4.99 us -> 10.3 us  [per_device(): one = hop(one)]
    all_to_all x1, blocking collectives: 42.4 us -> 40.2 us  [per_device(): packed = lax.all_to_all(packed, (Z, Y), 0, 0, tiled=True)]
    ppermute x3, starting transfers between devices: 18.9 us -> 20.4 us  [per_device(): two = hop_back(two)]
    pallas_call x14 -> x15, Pallas kernels: 15.7 us -> 15.6 us  [call(): pl.pallas_call(kernel, out_shape=out_shape, in_specs=specs or [VMEM] * le...]
  transfers between devices with their start and end apart: 12 -> 12, of which waited for: 5 -> 6; matrix products, arithmetic and copies ran while one was open for 0% -> 0% of each run, Pallas kernels for 6% -> 3%
where the time goes in v9:
time: 148 us
  blocking collectives  58.1 us (39%)
  starting transfers between devices  42.2 us (29%)
  waiting for transfers between devices  26.9 us (18%)
  Pallas kernels  15.6 us (11%)
  local copies, waits for them, and re-layouts  2.64 us (2%)
  between operations  2.18 us (1%)
    all_to_all x1, blocking collectives, per_device(): packed = lax.all_to_all(packed, (Z, Y), 0, 0, tiled=True)  40.2 us
    ppermute x3, starting transfers between devices, per_device(): two = hop_back(two)  20.4 us
    all_to_all x1, blocking collectives, per_device(): block = lax.all_to_all(piece, (HX, Y), 0, 0, tiled=True)  17.9 us
    pallas_call x15, Pallas kernels, call(): pl.pallas_call(kernel, out_shape=out_shape, in_specs=specs or [VMEM] * le...  15.6 us
    ppermute x1, waiting for transfers between devices, per_device(): across(send)  14.8 us
    ppermute x4, waiting for transfers between devices, per_device(): one = hop(one)  10.3 us
    ppermute x4, starting transfers between devices, per_device(): one = hop(one)  10 us
    ppermute x1, starting transfers between devices, per_device(): far = across(n0)  3.4 us
  transfers between devices with their start and end apart: 12, of which 6 were waited for; matrix products, arithmetic and copies ran while one was open for 0% of the time, Pallas kernels for 3%

profile of v9, /device:TPU:8, one launch (start us, length us, event | category | flops | bytes accessed | tf_op | source)
XLA Modules:
  0.0 147.5 jit_solution(7781781709656469780)
XLA Ops:
  0.6 0.0 copy-start.3
  0.6 1.0 copy-done.3
  1.6 0.1 text_unit.1.refs_0_
  1.7 4.3 %collective-permute-start.4 = (bf16[128,1152]{1,0:T(8,128)(2,1)S(1)}, bf16[128,1152]{1,0:T(8,128)(2,1)S(1)}, u32[]{:S(2)}, u32[]{:S(2)}) collective-permute-start(bf16[128,1152]{1,0:T(8,128)(2,1)S(1)} %text_unit.1.refs_0_), channel_id=1, source_target_pairs={{0,32},{16,240},{32,64},{48,16},{64,96},{80,48},{96,128},{112,80},... | collective-permute-start | bytes 884744 | tf_op jit(solution)/shard_map/ppermute | solution.py:299
  6.0 8.6 %collective-permute-start.1 = (bf16[128,1152]{1,0:T(8,128)(2,1)S(1)}, bf16[128,1152]{1,0:T(8,128)(2,1)S(1)}, u32[]{:S(2)}, u32[]{:S(2)}) collective-permute-start(bf16[128,1152]{1,0:T(8,128)(2,1)S(1)} %text_unit.1.refs_0_), channel_id=1, source_target_pairs={{32,0},{240,16},{64,32},{16,48},{96,64},{48,80},{128,96},{80,112},... | collective-permute-start | bytes 884744 | tf_op jit(solution)/shard_map/ppermute | solution.py:302
  14.6 2.8 %collective-permute-done.4.refs_1_ = bf16[128,1152]{1,0:T(8,128)(2,1)S(1)} collective-permute-done((bf16[128,1152]{1,0:T(8,128)(2,1)S(1)}, bf16[128,1152]{1,0:T(8,128)(2,1)S(1)}, u32[]{:S(2)}, u32[]{:S(2)}) %collective-permute-start.4) | collective-permute-done | bytes 294944 | tf_op jit(solution)/shard_map/ppermute | solution.py:299
  17.4 1.9 %collective-permute-start.5 = (bf16[128,1152]{1,0:T(8,128)(2,1)S(1)}, bf16[128,1152]{1,0:T(8,128)(2,1)S(1)}, u32[]{:S(2)}, u32[]{:S(2)}) collective-permute-start(bf16[128,1152]{1,0:T(8,128)(2,1)S(1)} %collective-permute-done.4.refs_1_), channel_id=1, source_target_pairs={{0,32},{16,240},{32,64},{48,16},{64,96},{80,48},{96,128},{112,80},... | collective-permute-start | bytes 884744 | tf_op jit(solution)/shard_map/ppermute | solution.py:299
  19.3 0.0 collective-permute-done.1.refs_2_
  19.3 6.0 %collective-permute-start.2 = (bf16[128,1152]{1,0:T(8,128)(2,1)S(1)}, bf16[128,1152]{1,0:T(8,128)(2,1)S(1)}, u32[]{:S(2)}, u32[]{:S(2)}) collective-permute-start(bf16[128,1152]{1,0:T(8,128)(2,1)S(1)} %collective-permute-done.1.refs_2_), channel_id=1, source_target_pairs={{32,0},{240,16},{64,32},{16,48},{96,64},{48,80},{128,96},{80,112},... | collective-permute-start | bytes 884744 | tf_op jit(solution)/shard_map/ppermute | solution.py:302
  25.3 3.8 %collective-permute-done.5.refs_3_ = bf16[128,1152]{1,0:T(8,128)(2,1)S(1)} collective-permute-done((bf16[128,1152]{1,0:T(8,128)(2,1)S(1)}, bf16[128,1152]{1,0:T(8,128)(2,1)S(1)}, u32[]{:S(2)}, u32[]{:S(2)}) %collective-permute-start.5) | collective-permute-done | bytes 294944 | tf_op jit(solution)/shard_map/ppermute | solution.py:299
  29.2 1.9 %collective-permute-start.6 = (bf16[128,1152]{1,0:T(8,128)(2,1)S(1)}, bf16[128,1152]{1,0:T(8,128)(2,1)S(1)}, u32[]{:S(2)}, u32[]{:S(2)}) collective-permute-start(bf16[128,1152]{1,0:T(8,128)(2,1)S(1)} %collective-permute-done.5.refs_3_), channel_id=1, source_target_pairs={{0,32},{16,240},{32,64},{48,16},{64,96},{80,48},{96,128},{112,80},... | collective-permute-start | bytes 884744 | tf_op jit(solution)/shard_map/ppermute | solution.py:299
  31.1 0.0 copy-start.1
  31.1 1.0 copy-done.1
  32.1 0.7 copy-done.4
  32.8 0.3 normed.1.own_ref
  33.1 3.4 %collective-permute-start = (bf16[128,1408]{1,0:T(8,128)(2,1)S(1)}, bf16[128,1408]{1,0:T(8,128)(2,1)S(1)}, u32[]{:S(2)}, u32[]{:S(2)}) collective-permute-start(bf16[128,1408]{1,0:T(8,128)(2,1)S(1)} %normed.1.own_ref), channel_id=1, source_target_pairs={{0,256},{256,0},{1,257},{257,1},{2,258},{258,2},{3,259},{259,3},{4... | collective-permute-start | bytes 1081352 | tf_op jit(solution)/shard_map/ppermute | solution.py:295
  36.5 0.0 collective-permute-done.2.after_ref.refs_4_
  36.5 5.8 %collective-permute-start.7 = (bf16[128,1152]{1,0:T(8,128)(2,1)S(1)}, bf16[128,1152]{1,0:T(8,128)(2,1)S(1)}, u32[]{:S(2)}, u32[]{:S(2)}) collective-permute-start(bf16[128,1152]{1,0:T(8,128)(2,1)S(1)} %collective-permute-done.2.after_ref.refs_4_), channel_id=1, source_target_pairs={{32,0},{240,16},{64,32},{16,48},{96,64},{48,80},{128,96},{80,112},... | collective-permute-start | bytes 884744 | tf_op jit(solution)/shard_map/ppermute | solution.py:302
  42.3 0.0 collective-permute-done.6.after_ref.refs_5_
  42.3 1.9 %collective-permute-start.8 = (bf16[128,1152]{1,0:T(8,128)(2,1)S(1)}, bf16[128,1152]{1,0:T(8,128)(2,1)S(1)}, u32[]{:S(2)}, u32[]{:S(2)}) collective-permute-start(bf16[128,1152]{1,0:T(8,128)(2,1)S(1)} %collective-permute-done.6.after_ref.refs_5_), channel_id=1, source_target_pairs={{0,32},{16,240},{32,64},{48,16},{64,96},{80,48},{96,128},{112,80},... | collective-permute-start | bytes 884744 | tf_op jit(solution)/shard_map/ppermute | solution.py:299
  44.2 0.0 collective-permute-done.got_ref
  44.2 0.1 join.1.n_own
  44.3 1.9 %collective-permute-start.3 = (bf16[256,1408]{1,0:T(8,128)(2,1)S(1)}, bf16[256,1408]{1,0:T(8,128)(2,1)S(1)}, u32[]{:S(2)}, u32[]{:S(2)}) collective-permute-start(bf16[256,1408]{1,0:T(8,128)(2,1)S(1)} %join.1.n_own), channel_id=1, source_target_pairs={{0,16},{16,0},{1,17},{17,1},{2,18},{18,2},{3,19},{19,3},{4,20},{20... | collective-permute-start | bytes 2162696 | tf_op jit(solution)/shard_map/ppermute | solution.py:315
  47.5 0.7 collective-permute-done.7.refs_6_
  48.2 0.1 collect.1.refs_0_.early_ref
  48.4 3.7 %collective-permute-done.8.refs_0_ = bf16[128,1152]{1,0:T(8,128)(2,1)S(1)} collective-permute-done((bf16[128,1152]{1,0:T(8,128)(2,1)S(1)}, bf16[128,1152]{1,0:T(8,128)(2,1)S(1)}, u32[]{:S(2)}, u32[]{:S(2)}) %collective-permute-start.8) | collective-permute-done | bytes 294944 | tf_op jit(solution)/shard_map/ppermute | solution.py:299
  52.1 0.0 collective-permute-done.3.n_core
  52.2 4.3 %project.1 = (bf16[512,1152]{1,0:T(8,128)(2,1)S(1)}, f32[256,1152]{1,0:T(8,128)S(1)}, f32[256,128]{1,0:T(8,128)S(1)}, bf16[512,1408]{1,0:T(8,128)(2,1)S(1)}) custom-call(bf16[256,1408]{1,0:T(8,128)(2,1)S(1)} %join.1.n_own, bf16[256,1408]{1,0:T(8,128)(2,1)S(1)} %collective-permute-done.3.n_core, bf16[1408,1152]{1,0:T(8,128)(2,1)} %w_ref.5, ...), custom_call_target="tpu_custom_call" | custom-call | flops 1660944384 | bytes 8912896 | tf_op jit(solution)/shard_map/project/pallas_call | solution.py:39
  56.5 3.4 %pairs.1 = (bf16[272,1152]{1,0:T(8,128)(2,1)S(1)}, f32[1,128]{1,0:T(1,128)S(1)}, bf16[512,1024]{1,0:T(8,128)(2,1)S(1)}) custom-call(f32[1]{0:T(128)S(6)} %copy.10.scale_ref, f32[1]{0:T(128)S(6)} %copy.11.bias_ref, bf16[512,1152]{1,0:T(8,128)(2,1)S(1)} %get-tuple-element.18.img_ref, bf16[896,1152]{1,0:T(8,128)(2,1)S(1)} %collect.1.refs_0_.early_ref, ...), custom_call_target="tpu_custom_call" | custom-call | flops 1811939328 | bytes 5214728 | tf_op jit(solution)/shard_map/pairs/pallas_call | solution.py:39
  59.9 1.9 %collective-permute-start.9 = (bf16[272,1152]{1,0:T(8,128)(2,1)S(1)}, bf16[272,1152]{1,0:T(8,128)(2,1)S(1)}, u32[]{:S(2)}, u32[]{:S(2)}) collective-permute-start(bf16[272,1152]{1,0:T(8,128)(2,1)S(1)} %get-tuple-element.21), channel_id=1, source_target_pairs={{0,16},{16,0},{1,17},{17,1},{2,18},{18,2},{3,19},{19,3},{4,20},{20... | collective-permute-start | bytes 1880072 | tf_op jit(solution)/shard_map/ppermute | solution.py:351
  61.8 1.0 keep.1.keep_ref
  62.8 1.0 collective-permute-done.9.got_ref.core_ref
  63.8 0.1 add_cores.1.after_ref
  63.9 2.4 %collective-permute-start.10 = (bf16[272,1152]{1,0:T(8,128)(2,1)S(1)}, bf16[272,1152]{1,0:T(8,128)(2,1)S(1)}, u32[]{:S(2)}, u32[]{:S(2)}) collective-permute-start(bf16[272,1152]{1,0:T(8,128)(2,1)S(1)} %add_cores.1.after_ref), channel_id=1, source_target_pairs={{0,256},{256,0},{1,257},{257,1},{2,258},{258,2},{3,259},{259,3},{4... | collective-permute-start | bytes 1880072 | tf_op jit(solution)/shard_map/ppermute | solution.py:386
  66.4 0.8 pick.1.after_ref.pick_ref
  67.2 14.8 %collective-permute-done.10.got_ref = bf16[272,1152]{1,0:T(8,128)(2,1)S(1)} collective-permute-done((bf16[272,1152]{1,0:T(8,128)(2,1)S(1)}, bf16[272,1152]{1,0:T(8,128)(2,1)S(1)}, u32[]{:S(2)}, u32[]{:S(2)}) %collective-permute-start.10) | collective-permute-done | bytes 626720 | tf_op jit(solution)/shard_map/ppermute | solution.py:386
  82.0 0.5 d_proj.1
  82.5 2.1 %collective-permute-start.11 = (bf16[256,1152]{1,0:T(8,128)(2,1)S(1)}, bf16[256,1152]{1,0:T(8,128)(2,1)S(1)}, u32[]{:S(2)}, u32[]{:S(2)}) collective-permute-start(bf16[256,1152]{1,0:T(8,128)(2,1)S(1)} %get-tuple-element.25.dproj_ref.own_ref), channel_id=1, source_target_pairs={{0,16},{16,0},{1,17},{17,1},{2,18},{18,2},{3,19},{19,3},{4,20},{20... | collective-permute-start | bytes 1769480 | tf_op jit(solution)/shard_map/ppermute | solution.py:394
  84.6 0.0 copy-done
  84.6 0.0 copy-done.2
  84.6 0.0 copy-done.5
  84.6 2.2 %d_features.1 = (bf16[128,1408]{1,0:T(8,128)(2,1)}, f32[1,1408]{1,0:T(1,128)S(1)}) custom-call(bf16[256,1152]{1,0:T(8,128)(2,1)S(1)} %get-tuple-element.25.dproj_ref.own_ref, bf16[128,1408]{1,0:T(8,128)(2,1)S(1)} %bitcast.11, f32[1408]{0:T(1024)S(1)} %copy-done.5, bf16[512,1408]{1,0:T(8,128)(2,1)S(1)} %get-tuple-element.24.rows_ref, ...), custom_call_target="tpu_custom_call" | custom-call | flops 830472192 | bytes 6007808 | tf_op jit(solution)/shard_map/d_features/pallas_call | solution.py:39
  86.8 0.0 collective-permute-done.11.got_ref
  86.8 1.8 %head.1 = bf16[512,896]{1,0:T(8,128)(2,1)S(1)} custom-call(bf16[256,1152]{1,0:T(8,128)(2,1)S(1)} %get-tuple-element.25.dproj_ref.own_ref, bf16[256,1152]{1,0:T(8,128)(2,1)S(1)} %collective-permute-done.11.got_ref, bf16[384,512]{1,0:T(8,128)(2,1)S(1)} %pick.1.after_ref.pick_ref, bf16[512,1408]{1,0:T(8,128)(2,1)S(1)} %get-tuple-element.24.rows_ref, ...), custom_call_target="tpu_custom_call" | custom-call | flops 1283457024 | bytes 7187968 | tf_op jit(solution)/shard_map/head/pallas_call | solution.py:39
  88.6 40.2 %all_to_all.22 = bf16[64,8,896]{2,1,0:T(8,128)(2,1)S(1)} all-to-all(bf16[64,8,896]{2,1,0:T(8,128)(2,1)S(1)} %bitcast.9), channel_id=1, replica_groups=mesh['x'=2,'z'=8,'c'=2,'hx'=2,'y'=8] {'z','y'}, dimensions={0} | all-to-all | bytes 1835008 | tf_op jit(solution)/shard_map/all_to_all | solution.py:422
  128.7 0.2 reduce.1
  128.9 17.9 %all_to_all.23 = bf16[16,8,896]{2,1,0:T(8,128)(2,1)S(1)} all-to-all(bf16[16,8,896]{2,1,0:T(8,128)(2,1)S(1)} %bitcast.13), channel_id=1, replica_groups=mesh['x'=2,'z'=8,'c'=2,'hx'=2,'y'=8] {'hx','y'}, dimensions={0} | all-to-all | bytes 458752 | tf_op jit(solution)/shard_map/all_to_all | solution.py:429
  146.8 0.7 unpack.1
  (5 shorter events, 0.0 us)
Async XLA Ops:
  0.6 1.0 copy-start.3
  1.7 15.6 %collective-permute-start.4 = (bf16[128,1152]{1,0:T(8,128)(2,1)S(1)}, bf16[128,1152]{1,0:T(8,128)(2,1)S(1)}, u32[]{:S(2)}, u32[]{:S(2)}) collective-permute-start(bf16[128,1152]{1,0:T(8,128)(2,1)S(1)} %text_unit.1.refs_0_), channel_id=1, source_target_pairs={{0,32},{16,240},{32,64},{48,16},{64,96},{80,48},{96,128},{112,80},... | collective-permute-start | bytes 884744 | tf_op jit(solution)/shard_map/ppermute | solution.py:299
  6.0 13.3 %collective-permute-start.1 = (bf16[128,1152]{1,0:T(8,128)(2,1)S(1)}, bf16[128,1152]{1,0:T(8,128)(2,1)S(1)}, u32[]{:S(2)}, u32[]{:S(2)}) collective-permute-start(bf16[128,1152]{1,0:T(8,128)(2,1)S(1)} %text_unit.1.refs_0_), channel_id=1, source_target_pairs={{32,0},{240,16},{64,32},{16,48},{96,64},{48,80},{128,96},{80,112},... | collective-permute-start | bytes 884744 | tf_op jit(solution)/shard_map/ppermute | solution.py:302
  17.4 11.8 %collective-permute-start.5 = (bf16[128,1152]{1,0:T(8,128)(2,1)S(1)}, bf16[128,1152]{1,0:T(8,128)(2,1)S(1)}, u32[]{:S(2)}, u32[]{:S(2)}) collective-permute-start(bf16[128,1152]{1,0:T(8,128)(2,1)S(1)} %collective-permute-done.4.refs_1_), channel_id=1, source_target_pairs={{0,32},{16,240},{32,64},{48,16},{64,96},{80,48},{96,128},{112,80},... | collective-permute-start | bytes 884744 | tf_op jit(solution)/shard_map/ppermute | solution.py:299
  19.3 17.1 %collective-permute-start.2 = (bf16[128,1152]{1,0:T(8,128)(2,1)S(1)}, bf16[128,1152]{1,0:T(8,128)(2,1)S(1)}, u32[]{:S(2)}, u32[]{:S(2)}) collective-permute-start(bf16[128,1152]{1,0:T(8,128)(2,1)S(1)} %collective-permute-done.1.refs_2_), channel_id=1, source_target_pairs={{32,0},{240,16},{64,32},{16,48},{96,64},{48,80},{128,96},{80,112},... | collective-permute-start | bytes 884744 | tf_op jit(solution)/shard_map/ppermute | solution.py:302
  29.2 13.1 %collective-permute-start.6 = (bf16[128,1152]{1,0:T(8,128)(2,1)S(1)}, bf16[128,1152]{1,0:T(8,128)(2,1)S(1)}, u32[]{:S(2)}, u32[]{:S(2)}) collective-permute-start(bf16[128,1152]{1,0:T(8,128)(2,1)S(1)} %collective-permute-done.5.refs_3_), channel_id=1, source_target_pairs={{0,32},{16,240},{32,64},{48,16},{64,96},{80,48},{96,128},{112,80},... | collective-permute-start | bytes 884744 | tf_op jit(solution)/shard_map/ppermute | solution.py:299
  31.1 1.0 copy-start.1
  32.1 0.7 copy-start.4
  33.1 11.2 %collective-permute-start = (bf16[128,1408]{1,0:T(8,128)(2,1)S(1)}, bf16[128,1408]{1,0:T(8,128)(2,1)S(1)}, u32[]{:S(2)}, u32[]{:S(2)}) collective-permute-start(bf16[128,1408]{1,0:T(8,128)(2,1)S(1)} %normed.1.own_ref), channel_id=1, source_target_pairs={{0,256},{256,0},{1,257},{257,1},{2,258},{258,2},{3,259},{259,3},{4... | collective-permute-start | bytes 1081352 | tf_op jit(solution)/shard_map/ppermute | solution.py:295
  36.5 11.8 %collective-permute-start.7 = (bf16[128,1152]{1,0:T(8,128)(2,1)S(1)}, bf16[128,1152]{1,0:T(8,128)(2,1)S(1)}, u32[]{:S(2)}, u32[]{:S(2)}) collective-permute-start(bf16[128,1152]{1,0:T(8,128)(2,1)S(1)} %collective-permute-done.2.after_ref.refs_4_), channel_id=1, source_target_pairs={{32,0},{240,16},{64,32},{16,48},{96,64},{48,80},{128,96},{80,112},... | collective-permute-start | bytes 884744 | tf_op jit(solution)/shard_map/ppermute | solution.py:302
  42.3 9.8 %collective-permute-start.8 = (bf16[128,1152]{1,0:T(8,128)(2,1)S(1)}, bf16[128,1152]{1,0:T(8,128)(2,1)S(1)}, u32[]{:S(2)}, u32[]{:S(2)}) collective-permute-start(bf16[128,1152]{1,0:T(8,128)(2,1)S(1)} %collective-permute-done.6.after_ref.refs_5_), channel_id=1, source_target_pairs={{0,32},{16,240},{32,64},{48,16},{64,96},{80,48},{96,128},{112,80},... | collective-permute-start | bytes 884744 | tf_op jit(solution)/shard_map/ppermute | solution.py:299
  44.3 7.9 %collective-permute-start.3 = (bf16[256,1408]{1,0:T(8,128)(2,1)S(1)}, bf16[256,1408]{1,0:T(8,128)(2,1)S(1)}, u32[]{:S(2)}, u32[]{:S(2)}) collective-permute-start(bf16[256,1408]{1,0:T(8,128)(2,1)S(1)} %join.1.n_own), channel_id=1, source_target_pairs={{0,16},{16,0},{1,17},{17,1},{2,18},{18,2},{3,19},{19,3},{4,20},{20... | collective-permute-start | bytes 2162696 | tf_op jit(solution)/shard_map/ppermute | solution.py:315
  59.9 4.0 %collective-permute-start.9 = (bf16[272,1152]{1,0:T(8,128)(2,1)S(1)}, bf16[272,1152]{1,0:T(8,128)(2,1)S(1)}, u32[]{:S(2)}, u32[]{:S(2)}) collective-permute-start(bf16[272,1152]{1,0:T(8,128)(2,1)S(1)} %get-tuple-element.21), channel_id=1, source_target_pairs={{0,16},{16,0},{1,17},{17,1},{2,18},{18,2},{3,19},{19,3},{4,20},{20... | collective-permute-start | bytes 1880072 | tf_op jit(solution)/shard_map/ppermute | solution.py:351
  63.9 18.1 %collective-permute-start.10 = (bf16[272,1152]{1,0:T(8,128)(2,1)S(1)}, bf16[272,1152]{1,0:T(8,128)(2,1)S(1)}, u32[]{:S(2)}, u32[]{:S(2)}) collective-permute-start(bf16[272,1152]{1,0:T(8,128)(2,1)S(1)} %add_cores.1.after_ref), channel_id=1, source_target_pairs={{0,256},{256,0},{1,257},{257,1},{2,258},{258,2},{3,259},{259,3},{4... | collective-permute-start | bytes 1880072 | tf_op jit(solution)/shard_map/ppermute | solution.py:386
  82.0 2.6 %copy-start = (bf16[1408,1152]{1,0:T(8,128)(2,1)S(1)}, bf16[1408,1152]{1,0:T(8,128)(2,1)}, u32[]{:S(2)}) copy-start(bf16[1408,1152]{1,0:T(8,128)(2,1)} %w_ref.5) | copy-start | bytes 9732100
  82.0 2.6 %copy-start.2 = (bf16[1,128,1408]{2,1,0:T(8,128)(2,1)S(1)}, bf16[1,128,1408]{2,1,0:T(8,128)(2,1)}, u32[]{:S(2)}) copy-start(bf16[1,128,1408]{2,1,0:T(8,128)(2,1)} %param.6) | copy-start | bytes 1081348
  82.0 2.6 %copy-start.5 = (f32[1408]{0:T(1024)S(1)}, f32[1408]{0:T(1024)}, u32[]{:S(2)}) copy-start(f32[1408]{0:T(1024)} %gain_ref.5) | copy-start | bytes 16900
  82.5 4.3 %collective-permute-start.11 = (bf16[256,1152]{1,0:T(8,128)(2,1)S(1)}, bf16[256,1152]{1,0:T(8,128)(2,1)S(1)}, u32[]{:S(2)}, u32[]{:S(2)}) collective-permute-start(bf16[256,1152]{1,0:T(8,128)(2,1)S(1)} %get-tuple-element.25.dproj_ref.own_ref), channel_id=1, source_target_pairs={{0,16},{16,0},{1,17},{17,1},{2,18},{18,2},{3,19},{19,3},{4,20},{20... | collective-permute-start | bytes 1769480 | tf_op jit(solution)/shard_map/ppermute | solution.py:394
